TPU v7x, 256 devices: a whole 4x4x8 slice. The times are simulated.
256 devices in a mesh: row: 8 (over x, core), col: 32 (over z, y).
Axes of the slice: x: 4, y: 4, z: 8, core: 2. Of those that a mesh axis runs over, the one named last changes fastest.
Arguments:
- tokens: bfloat16 [1024, 8192], P('col', 'row'), may hold values from -6 to 6
- gate_weight: bfloat16 [8192, 24576], P('row', 'col'), may hold values from -0.0625 to 0.0625
- up_weight: bfloat16 [8192, 24576], P('row', 'col'), may hold values from -0.0625 to 0.0625
- down_weight: bfloat16 [24576, 8192], P('col', 'row'), may hold values from -0.0390625 to 0.0390625
- out_grad: bfloat16 [1024, 8192], P('col', 'row'), may hold values from -6 to 6
Outputs:
- mixed: bfloat16 [1024, 8192], P('col', 'row')
- input_grad: bfloat16 [1024, 8192], P('col', 'row')
- gate_grad: bfloat16 [8192, 24576], P('row', 'col')
- up_grad: bfloat16 [8192, 24576], P('row', 'col')
- down_grad: bfloat16 [24576, 8192], P('col', 'row')
All inputs are finite; a program needn't handle non-finite values.
Results may differ from a plain program's by a relative error of at most 0.034.
Values may be sent and summed in bfloat16 or wider, within the bound.
No kernel may reach another device: no remote copies, remote signals or barrier semaphores. Data moves between devices by JAX's collectives and lax.ppermute only.
A program may use at most 128 MiB of HBM per device.

v0:
```python
import jax
import jax.numpy as jnp
from jax import lax
from jax.experimental import pallas as pl
from jax.experimental.pallas import tpu as pltpu
from jax.sharding import PartitionSpec as P

BF16 = jnp.bfloat16
F32 = jnp.float32
NX, NC, NZ, NY = 4, 2, 8, 4
MIB = 1024 * 1024
LIMIT = 24
TILE = 256

X_GROUPS = [[x * NC + c for x in range(NX)] for c in range(NC)]
Y_GROUPS = [[z * NY + y for y in range(NY)] for z in range(NZ)]
Z_GROUPS = [[z * NY + y for z in range(NZ)] for y in range(NY)]
Y_STEP = [
    [(z * NY + y, z * NY + (y + k) % NY) for z in range(NZ) for y in range(NY)] for k in range(NY)
]
Z_STEP = [
    [(z * NY + y, (z + k) % NZ * NY + y) for z in range(NZ) for y in range(NY)] for k in range(NZ)
]
Z_UP = [(z * NY + y, (z + 1) % NZ * NY + y) for z in range(NZ) for y in range(NY)]
Z_DOWN = [(dst, src) for src, dst in Z_UP]
X_STEP = [
    [(x * NC + c, (x + k) % NX * NC + c) for x in range(NX) for c in range(NC)] for k in range(NX)
]
CORE_PAIRS = [(r, r ^ 1) for r in range(NX * NC)]

NN = (((1,), (0,)), ((), ()))
NT = (((1,), (1,)), ((), ()))
TN = (((0,), (0,)), ((), ()))


def dot(left, right, dims):
    return lax.dot_general(left, right, dims, preferred_element_type=F32)


def swap_core(value):
    return lax.ppermute(value, "row", CORE_PAIRS)


def exchange(value, axis, groups):
    count = len(groups[0])
    got = lax.all_to_all(value, axis, 0, 0, axis_index_groups=groups, tiled=True)
    return got.reshape(count, value.shape[0] // count, value.shape[1])


def share(value, axis, groups):
    got = exchange(jnp.tile(value, (len(groups[0]), 1)), axis, groups)
    return got.reshape(-1, value.shape[1])


def after(value, *others):
    return lax.optimization_barrier((value,) + others)[0]


def gather_blocks(own, axis, steps):
    count = len(steps)
    return [own] + [lax.ppermute(own, axis, steps[count - k]) for k in range(1, count)]


def ring_eight(own, axis, up, down):
    half = own.shape[0] // 2
    before, behind = [own], [own]
    for _ in range(3):
        before.append(lax.ppermute(before[-1], axis, up))
        behind.append(lax.ppermute(behind[-1], axis, down))
    top = lax.ppermute(before[3][:half], axis, up)
    bottom = lax.ppermute(behind[3][half:], axis, down)
    behind[2:3], before[2:3] = [in_hbm(behind[2])], [in_hbm(before[2])]
    return own, behind[1], behind[2], behind[3], top, bottom, before[3], before[2], before[1]


def whole(shape):
    return pl.BlockSpec(shape, lambda *_: (0,) * len(shape))


def hbm(shape, dtype=BF16):
    return pltpu.HBM(shape, dtype)


def in_hbm(value):
    return pltpu.with_memory_space_constraint(value, pltpu.HBM)


def call(kernel, grid, in_specs, out_specs, out_shape, flops, scratch=(), limit=LIMIT):
    return pl.pallas_call(
        kernel,
        grid_spec=pltpu.PrefetchScalarGridSpec(
            num_scalar_prefetch=1,
            grid=grid,
            in_specs=in_specs,
            out_specs=out_specs,
            scratch_shapes=list(scratch),
        ),
        out_shape=out_shape,
        compiler_params=pltpu.CompilerParams(vmem_limit_bytes=limit * MIB),
        cost_estimate=pl.CostEstimate(flops=flops, bytes_accessed=10 * MIB, transcendentals=0),
    )


def place(index, blocks, store):
    rows = blocks[0].shape[0]
    for k, block in enumerate(blocks):
        start = pl.multiple_of(lax.rem(index + k, len(blocks)) * rows, rows)
        store(start, block)


def place_eight(index, blocks, store):
    steps = (0, 1, 2, 3, 4, 4, 5, 6, 7)
    for block, step in zip(blocks, steps):
        z = lax.rem(index[0] + step, NZ)
        first = NY // 2 if block is blocks[5] else 0
        for k in range(block.shape[0] // 16):
            y = lax.rem(index[1] + first + k, NY)
            start = pl.multiple_of(y * NZ * 16 + z * 16, 16)
            store(start, block[k * 16 : (k + 1) * 16, :])


def gate_up_kernel(index, tok_a, *refs):
    blocks, (gate_a, gate_b, up_a, up_b, out, tok_b) = refs[:9], refs[9:]
    step = pl.program_id(0)

    @pl.when(step == 0)
    def _():
        def store(start, value):
            tok_b[pl.ds(start, 16), :] = value

        place_eight(index, blocks, store)

    tile = gate_a.shape[1]
    gate = dot(tok_a[...], gate_a[...], NN) + dot(tok_b[...], gate_b[...], NN)
    out[:, :tile] = gate.astype(BF16)
    up = dot(tok_a[...], up_a[...], NN) + dot(tok_b[...], up_b[...], NN)
    out[:, tile:] = up.astype(BF16)


def columns(rows, width, at):
    return pl.BlockSpec((rows, width), lambda *_: (0, at))


def gate_up_product(index, own, blocks, gate_a, gate_b, up_a, up_b):
    rows = own.shape[0]
    width, cols = gate_a.shape
    weight = pl.BlockSpec((width, TILE), lambda j, _: (0, j))
    return call(
        gate_up_kernel,
        (cols // TILE,),
        [columns(rows, width, 0)]
        + [columns(block.shape[0], width, 0) for block in blocks]
        + [weight] * 4,
        [pl.BlockSpec((rows, 2 * TILE), lambda j, _: (0, j)), whole((rows, width))],
        [hbm((rows, 2 * cols)), hbm((rows, width))],
        8 * rows * width * cols,
    )(index, own, *blocks, gate_a, gate_b, up_a, up_b)


def hidden_term_kernel(index, grad_a, *refs):
    blocks, (down_a, down_b, out, grad_b) = refs[:9], refs[9:]

    @pl.when(pl.program_id(0) == 0)
    def _():
        def store(start, value):
            grad_b[pl.ds(start, 16), :] = value

        place_eight(index, blocks, store)

    total = dot(grad_a[...], down_a[...], NT) + dot(grad_b[...], down_b[...], NT)
    out[...] = total.astype(BF16)


def hidden_term_product(index, own, blocks, down_a, down_b):
    rows = own.shape[0]
    cols, width = down_a.shape
    tile = 384
    weight = pl.BlockSpec((tile, width), lambda j, _: (j, 0))
    return call(
        hidden_term_kernel,
        (cols // tile,),
        [columns(rows, width, 1)]
        + [columns(block.shape[0], width, 1) for block in blocks]
        + [weight, weight],
        [pl.BlockSpec((rows, tile), lambda j, _: (0, j)), whole((rows, width))],
        [hbm((rows, cols)), hbm((rows, width))],
        4 * rows * width * cols,
    )(index, own, *blocks, down_a, down_b)


def mixed_kernel(index, *refs):
    blocks, (down_a, down_b, out, hidden) = refs[:NX], refs[NX:]
    step = pl.program_id(0)

    @pl.when(step == 0)
    def _():
        def store(start, value):
            hidden[pl.ds(start, value.shape[0]), :] = value[...]

        place(index[0], blocks, store)

    tile = down_a.shape[1]
    out[:, :tile] = dot(hidden[...], down_a[...], NN).astype(BF16)
    out[:, tile:] = dot(hidden[...], down_b[...], NN).astype(BF16)


def mixed_product(index, blocks, down_a, down_b):
    rows, depth = blocks[0].shape
    width = down_a.shape[1]
    shape = (4 * rows, depth)
    return call(
        mixed_kernel,
        (width // TILE,),
        [whole(block.shape) for block in blocks]
        + [pl.BlockSpec((depth, TILE), lambda j, _: (0, j))] * 2,
        [pl.BlockSpec((4 * rows, 2 * TILE), lambda j, _: (0, j)), whole(shape)],
        [hbm((4 * rows, 2 * width)), hbm(shape)],
        16 * rows * depth * width,
    )(index, *blocks, down_a, down_b)


def input_kernel(index, *refs):
    blocks, (gate_a, up_a, gate_b, up_b, out, pre_gate, pre_up) = refs[:NX], refs[NX:]
    step = pl.program_id(0)
    cols = blocks[0].shape[1] // 2

    @pl.when(step == 0)
    def _():
        def store(start, value):
            pre_gate[pl.ds(start, value.shape[0]), :] = value[:, :cols]
            pre_up[pl.ds(start, value.shape[0]), :] = value[:, cols:]

        place(index[0], blocks, store)

    tile = gate_a.shape[0]
    mine = dot(pre_gate[...], gate_a[...], NT) + dot(pre_up[...], up_a[...], NT)
    out[:, :tile] = mine.astype(BF16)
    other = dot(pre_gate[...], gate_b[...], NT) + dot(pre_up[...], up_b[...], NT)
    out[:, tile:] = other.astype(BF16)


def input_product(index, blocks, gate_a, up_a, gate_b, up_b):
    rows = blocks[0].shape[0]
    width, cols = gate_a.shape
    weight = pl.BlockSpec((TILE, cols), lambda j, _: (j, 0))
    half = hbm((4 * rows, cols))
    return call(
        input_kernel,
        (width // TILE,),
        [whole(block.shape) for block in blocks] + [weight] * 4,
        [pl.BlockSpec((4 * rows, 2 * TILE), lambda j, _: (0, j))] + [whole((4 * rows, cols))] * 2,
        [hbm((4 * rows, 2 * width)), half, half],
        32 * rows * cols * width,
    )(index, *blocks, gate_a, up_a, gate_b, up_b)


def total_of(terms):
    total = terms[0].astype(F32)
    for k in range(1, terms.shape[0]):
        total = total + terms[k].astype(F32)
    return total


def hidden_kernel(index, terms, gate_up, hidden):
    del index
    total = total_of(terms)
    gate_up[...] = total
    for k in range(hidden.shape[1] // TILE):
        gate = total[:, 2 * k * TILE : (2 * k + 1) * TILE]
        up = total[:, (2 * k + 1) * TILE : (2 * k + 2) * TILE]
        hidden[:, k * TILE : (k + 1) * TILE] = (gate * jax.nn.sigmoid(gate) * up).astype(BF16)


def hidden_of(index, terms):
    _, rows, cols = terms.shape
    return call(
        hidden_kernel,
        (1,),
        [whole(terms.shape)],
        [whole((rows, cols)), whole((rows, cols // 2))],
        [
            hbm((rows, cols), F32),
            jax.ShapeDtypeStruct((rows, cols // 2), BF16),
        ],
        16 * rows * cols,
    )(index, terms)


def pre_kernel(index, terms, gate_up, out):
    del index
    total = total_of(terms)
    cols = total.shape[1]
    for k in range(cols // TILE):
        hidden_grad = total[:, k * TILE : (k + 1) * TILE]
        gate = gate_up[:, 2 * k * TILE : (2 * k + 1) * TILE]
        up = gate_up[:, (2 * k + 1) * TILE : (2 * k + 2) * TILE]
        sig = jax.nn.sigmoid(gate)
        pre_gate = hidden_grad * up * sig * (1.0 + gate * (1.0 - sig))
        out[:, k * TILE : (k + 1) * TILE] = pre_gate.astype(BF16)
        out[:, cols + k * TILE : cols + (k + 1) * TILE] = (hidden_grad * gate * sig).astype(BF16)


def pre_grads(index, terms, gate_up):
    return call(
        pre_kernel,
        (1,),
        [whole(terms.shape), whole(gate_up.shape)],
        whole(gate_up.shape),
        jax.ShapeDtypeStruct(gate_up.shape, BF16),
        16 * gate_up.size,
    )(index, terms, gate_up)


def store_sum(terms, out):
    width = out.shape[1] // 2
    for k in range(width // TILE):
        mine = terms[:, :, 2 * k * TILE : (2 * k + 1) * TILE]
        other = terms[:, :, (2 * k + 1) * TILE : (2 * k + 2) * TILE]
        out[:, k * TILE : (k + 1) * TILE] = total_of(mine).astype(BF16)
        out[:, width + k * TILE : width + (k + 1) * TILE] = total_of(other).astype(BF16)


def sum_kernel(index, terms, out):
    del index
    store_sum(terms, out)


def sum_of(index, terms):
    _, rows, cols = terms.shape
    return call(
        sum_kernel,
        (1,),
        [whole(terms.shape)],
        whole((rows, cols)),
        hbm((rows, cols)),
        8 * rows * cols,
    )(index, terms)


def split_kernel(index, terms, near, far, total):
    store_sum(terms, total)
    rows = near.shape[0] // 4
    for k in range(4):
        for step, out in ((k + NZ - 1, near), (k + 3, far)):
            start = pl.multiple_of(lax.rem(index[0] + step, NZ) * rows, 16)
            out[k * rows : (k + 1) * rows, :] = total[pl.ds(start, rows), :]


def split_sum(index, terms):
    _, rows, cols = terms.shape
    half = (rows // 2, cols)
    return call(
        split_kernel,
        (1,),
        [whole(terms.shape)],
        [whole(half)] * 2,
        [jax.ShapeDtypeStruct(half, BF16)] * 2,
        8 * rows * cols,
        [pltpu.VMEM((rows, cols), BF16)],
    )(index, terms)


def fold_kernel(index, near, far, *outs):
    del index
    total = (near[...].astype(F32) + far[...].astype(F32)).astype(BF16)
    rows = outs[0].shape[0]
    for k, out in enumerate(outs):
        out[...] = total[k * rows : (k + 1) * rows, :]


def fold(index, near, far):
    rows, cols = near.shape
    block = (rows // 4, cols)
    return call(
        fold_kernel,
        (1,),
        [whole(near.shape)] * 2,
        [whole(block)] * 4,
        [jax.ShapeDtypeStruct(block, BF16)] * 4,
        8 * rows * cols,
    )(index, near, far)


def body(tokens, gate_weight, up_weight, down_weight, out_grad):
    core = lax.axis_index("row") % NC
    x = (lax.axis_index("row") // NC).astype(jnp.int32).reshape(1)
    col = lax.axis_index("col")
    zy = jnp.stack([col // NY, col % NY]).astype(jnp.int32)
    half = tokens.shape[0] // NC
    width = tokens.shape[1]

    def halves(value):
        mine = lax.dynamic_slice_in_dim(value, core * half, half, 0)
        other = lax.dynamic_slice_in_dim(value, (1 - core) * half, half, 0)
        return mine, swap_core(other)

    def join(value):
        mine = value[:, :width]
        got = swap_core(value[:, width:])
        first = jnp.where(core == 0, mine, got)
        second = jnp.where(core == 0, got, mine)
        return jnp.concatenate([first, second], axis=0)

    tok_a, tok_b = halves(tokens)
    grad_a, grad_b = halves(out_grad)
    own = jnp.concatenate([tok_a, grad_a], axis=1)
    other = jnp.concatenate([tok_b, grad_b], axis=1)
    gate_own, gate_other = in_hbm(gate_weight), in_hbm(swap_core(gate_weight))
    up_own, up_other = in_hbm(up_weight), in_hbm(swap_core(up_weight))
    down_own, down_other = in_hbm(down_weight), in_hbm(swap_core(down_weight))

    other_y = jnp.concatenate(gather_blocks(other, "col", Y_STEP), axis=0)
    other_blocks = ring_eight(other_y, "col", Z_UP, Z_DOWN)
    own_z = share(own, "col", Z_GROUPS)
    own_all = share(after(own_z, other_blocks[1], other_blocks[8]), "col", Y_GROUPS)

    gate_up_term, tok_other = gate_up_product(
        zy, own_all, other_blocks, gate_own, gate_other, up_own, up_other
    )
    gate_up, hidden_own = hidden_of(x, exchange(gate_up_term, "row", X_GROUPS))
    hidden_term, grad_other = hidden_term_product(
        zy, own_all, other_blocks, down_own, down_other
    )
    pre_own = pre_grads(x, exchange(hidden_term, "row", X_GROUPS), in_hbm(gate_up))

    hidden_blocks = gather_blocks(hidden_own, "row", X_STEP)
    mixed_term, hidden = mixed_product(after(x, pre_own), hidden_blocks, down_own, down_other)
    pre_blocks = gather_blocks(after(pre_own, *hidden_blocks[1:]), "row", X_STEP)
    input_term, pre_gate, pre_up = input_product(
        after(x, mixed_term), pre_blocks, gate_own, up_own, gate_other, up_other
    )
    mixed_y = exchange(mixed_term, "col", Y_GROUPS)
    input_y = exchange(after(input_term, mixed_y), "col", Y_GROUPS)
    def all_tokens(value):
        return jnp.concatenate([value, swap_core(value)], axis=0)

    tok_rows = jnp.concatenate([own_all[:, :width], swap_core(tok_other)], axis=0)
    grad_rows = jnp.concatenate([own_all[:, width:], swap_core(grad_other)], axis=0)
    down_grad = dot(all_tokens(hidden), grad_rows, TN).astype(BF16)
    gate_grad = dot(tok_rows, all_tokens(pre_gate), TN).astype(BF16)
    up_grad = dot(tok_rows, all_tokens(pre_up), TN).astype(BF16)
    near, far = split_sum(zy, mixed_y)
    previous, mine, following, second = fold(zy, near, lax.ppermute(far, "col", Z_STEP[4]))
    mixed_sum = mine.astype(F32)
    for block, step in ((previous, NZ - 1), (following, 1), (second, 2)):
        mixed_sum += lax.ppermute(block, "col", Z_STEP[step]).astype(F32)
    mixed = join(mixed_sum.astype(BF16))
    input_sum = sum_of(x, after(input_y, mixed))
    input_sum = after(exchange(input_sum, "col", Z_GROUPS), down_grad, gate_grad, up_grad)
    input_grad = join(input_sum.astype(F32).sum(0).astype(BF16))
    return (mixed, input_grad, gate_grad, up_grad, down_grad)


def solution(mesh):
    in_specs = (P("col", "row"), P("row", "col"), P("row", "col"), P("col", "row"), P("col", "row"))
    out_specs = (
        P("col", "row"),
        P("col", "row"),
        P("row", "col"),
        P("row", "col"),
        P("col", "row"),
    )
    return jax.shard_map(body, mesh=mesh, in_specs=in_specs, out_specs=out_specs, check_vma=False)
```

profile of v0, /device:TPU:1, one launch (start us, length us, event | category | flops | bytes accessed | tf_op | source)
XLA Modules:
  0.0 216.8 jit_solution(9403808412033092802)
XLA Ops:
  0.7 0.8 constant_dynamic-slice_fusion.1
  1.4 0.8 constant_dynamic-slice_fusion
  2.2 0.8 tile.4
  3.1 9.0 %all-to-all-start = ((bf16[8,16,2048]{2,1,0:T(8,128)(2,1)}), bf16[8,16,2048]{2,1,0:T(8,128)(2,1)S(1)}, u32[]{:S(2)}, u32[]{:S(2)}) async-start(bf16[8,16,2048]{2,1,0:T(8,128)(2,1)} %tile.4), calls=%async_computation | async-start | bytes 1048576 | tf_op jit(solution)/shard_map/all_to_all | solution.py:46
  12.1 1.0 collective-permute-start
  13.1 0.8 collective-permute-done
  14.3 1.3 collective-permute-start.4
  15.6 2.6 %collective-permute-start.3 = (bf16[16,2048]{1,0:T(8,128)(2,1)S(1)}, bf16[16,2048]{1,0:T(8,128)(2,1)S(1)}, u32[]{:S(2)}, u32[]{:S(2)}) collective-permute-start(bf16[16,2048]{1,0:T(8,128)(2,1)S(1)} %constant_dynamic-update-slice_fusion), channel_id=1, source_target_pairs={{0,2},{1,3},{2,0},{3,1},{4,6},{5,7},{6,4},{7,5},{8,10},{9,11},{10,... | collective-permute-start | bytes 196616 | tf_op jit(solution)/shard_map/ppermute | solution.py:61
  18.2 1.1 collective-permute-start.2
  19.2 2.4 %collective-permute-done.3 = bf16[16,2048]{1,0:T(8,128)(2,1)S(1)} collective-permute-done((bf16[16,2048]{1,0:T(8,128)(2,1)S(1)}, bf16[16,2048]{1,0:T(8,128)(2,1)S(1)}, u32[]{:S(2)}, u32[]{:S(2)}) %collective-permute-start.3) | collective-permute-done | bytes 65568 | tf_op jit(solution)/shard_map/ppermute | solution.py:61
  21.7 1.8 collective-permute-start.6
  23.5 1.3 collective-permute-start.5
  24.8 1.8 collective-permute-start.14
  26.6 6.2 %collective-permute-done.6.refs_8_ = bf16[64,2048]{1,0:T(8,128)(2,1)S(1)} collective-permute-done((bf16[64,2048]{1,0:T(8,128)(2,1)S(1)}, bf16[64,2048]{1,0:T(8,128)(2,1)S(1)}, u32[]{:S(2)}, u32[]{:S(2)}) %collective-permute-start.6) | collective-permute-done | bytes 262176 | tf_op jit(solution)/shard_map/ppermute | solution.py:68
  32.8 1.6 tile.5
  34.4 3.6 %all-to-all-start.1 = ((bf16[4,128,2048]{2,1,0:T(8,128)(2,1)}), bf16[4,128,2048]{2,1,0:T(8,128)(2,1)S(1)}, u32[]{:S(2)}, u32[]{:S(2)}) async-start(bf16[4,128,2048]{2,1,0:T(8,128)(2,1)} %tile.5), calls=%async_computation.1 | async-start | bytes 4194304 | tf_op jit(solution)/shard_map/all_to_all | solution.py:46
  38.2 2.6 %collective-permute-start.7 = (bf16[64,2048]{1,0:T(8,128)(2,1)S(1)}, bf16[64,2048]{1,0:T(8,128)(2,1)S(1)}, u32[]{:S(2)}, u32[]{:S(2)}) collective-permute-start(bf16[64,2048]{1,0:T(8,128)(2,1)S(1)} %collective-permute-done.5.refs_1_), channel_id=1, source_target_pairs={{4,0},{5,1},{6,2},{7,3},{8,4},{9,5},{10,6},{11,7},{12,8},{13,9},{1... | collective-permute-start | bytes 786440 | tf_op jit(solution)/shard_map/ppermute | solution.py:69
  40.7 4.8 %collective-permute-done.9.refs_7_ = bf16[64,2048]{1,0:T(8,128)(2,1)S(1)} collective-permute-done((bf16[64,2048]{1,0:T(8,128)(2,1)S(1)}, bf16[64,2048]{1,0:T(8,128)(2,1)S(1)}, u32[]{:S(2)}, u32[]{:S(2)}) %collective-permute-start.9) | collective-permute-done | bytes 262176 | tf_op jit(solution)/shard_map/ppermute | solution.py:68
  45.6 2.7 %collective-permute-start.8 = (bf16[64,2048]{1,0:T(8,128)(2,1)S(1)}, bf16[64,2048]{1,0:T(8,128)(2,1)S(1)}, u32[]{:S(2)}, u32[]{:S(2)}) collective-permute-start(bf16[64,2048]{1,0:T(8,128)(2,1)S(1)} %collective-permute-done.7.refs_2_), channel_id=1, source_target_pairs={{4,0},{5,1},{6,2},{7,3},{8,4},{9,5},{10,6},{11,7},{12,8},{13,9},{1... | collective-permute-start | bytes 786440 | tf_op jit(solution)/shard_map/ppermute | solution.py:69
  48.3 3.0 %collective-permute-start.13 = (bf16[768,1024]{1,0:T(8,128)(2,1)}, bf16[768,1024]{1,0:T(8,128)(2,1)}, u32[]{:S(2)}, u32[]{:S(2)}) collective-permute-start(bf16[768,1024]{1,0:T(8,128)(2,1)} %refs_4_.2), channel_id=1, source_target_pairs={{0,32},{32,0},{64,96},{96,64},{128,160},{160,128},{192,224},{224,1... | collective-permute-start | bytes 4718600 | tf_op jit(solution)/shard_map/ppermute | solution.py:41
  51.2 1.1 collective-permute-done.10.refs_6_
  52.3 0.7 slice.32
  53.0 0.7 slice.33
  53.6 2.7 %collective-permute-start.12 = (bf16[32,2048]{1,0:T(8,128)(2,1)}, bf16[32,2048]{1,0:T(8,128)(2,1)}, u32[]{:S(2)}, u32[]{:S(2)}) collective-permute-start(bf16[32,2048]{1,0:T(8,128)(2,1)} %slice.33), channel_id=1, source_target_pairs={{4,0},{5,1},{6,2},{7,3},{8,4},{9,5},{10,6},{11,7},{12,8},{13,9},{1... | collective-permute-start | bytes 393224 | tf_op jit(solution)/shard_map/ppermute | solution.py:71
  56.4 2.1 collective-permute-done.11.refs_4_
  58.6 4.1 %all-to-all-done.1 = bf16[4,128,2048]{2,1,0:T(8,128)(2,1)S(1)} async-done(((bf16[4,128,2048]{2,1,0:T(8,128)(2,1)}), bf16[4,128,2048]{2,1,0:T(8,128)(2,1)S(1)}, u32[]{:S(2)}, u32[]{:S(2)}) %all-to-all-start.1) | async-done | bytes 2097184 | tf_op jit(solution)/shard_map/all_to_all | solution.py:46
  62.7 7.4 %shard_map.93 = (bf16[512,1536]{1,0:T(8,128)(2,1)}, bf16[512,1024]{1,0:T(8,128)(2,1)}) custom-call(s32[2]{0:T(128)S(1)} %pad_add_fusion.index, bf16[512,2048]{1,0:T(8,128)(2,1)S(1)} %bitcast.10, bf16[64,2048]{1,0:T(8,128)(2,1)S(1)} %pad_maximum_fusion.3.refs_0_, bf16[64,2048]{1,0:T(8,128)(2,1)S(1)} %collective-permute-done.5.refs_1_, ...), custom_call_target="tpu_custom_call" | custom-call | flops 3221225472 | bytes 10485760 | tf_op jit(solution)/shard_map/pallas_call | solution.py:148
  70.0 4.4 %all-to-all-start.3 = ((bf16[4,128,1536]{2,1,0:T(8,128)(2,1)}), bf16[4,128,1536]{2,1,0:T(8,128)(2,1)}, u32[]{:S(2)}, u32[]{:S(2)}) async-start(bf16[4,128,1536]{2,1,0:T(8,128)(2,1)} %bitcast.17), calls=%async_computation.3 | async-start | bytes 3145728 | tf_op jit(solution)/shard_map/all_to_all | solution.py:46
  74.4 5.5 %shard_map.92 = (bf16[512,768]{1,0:T(8,128)(2,1)}, bf16[512,1024]{1,0:T(8,128)(2,1)}) custom-call(s32[2]{0:T(128)S(1)} %pad_add_fusion.index, bf16[512,2048]{1,0:T(8,128)(2,1)S(1)} %bitcast.11, bf16[64,2048]{1,0:T(8,128)(2,1)S(1)} %pad_maximum_fusion.3.refs_0_, bf16[64,2048]{1,0:T(8,128)(2,1)S(1)} %collective-permute-done.5.refs_1_, ...), custom_call_target="tpu_custom_call" | custom-call | flops 1610612736 | bytes 10485760 | tf_op jit(solution)/shard_map/pallas_call | solution.py:179
  79.9 12.8 %all-to-all-done.3.terms = bf16[4,128,1536]{2,1,0:T(8,128)(2,1)} async-done(((bf16[4,128,1536]{2,1,0:T(8,128)(2,1)}), bf16[4,128,1536]{2,1,0:T(8,128)(2,1)}, u32[]{:S(2)}, u32[]{:S(2)}) %all-to-all-start.3) | async-done | bytes 1572896 | tf_op jit(solution)/shard_map/all_to_all | solution.py:46
  92.7 3.5 %all-to-all-start.2 = ((bf16[4,128,768]{2,1,0:T(8,128)(2,1)}), bf16[4,128,768]{2,1,0:T(8,128)(2,1)S(1)}, u32[]{:S(2)}, u32[]{:S(2)}) async-start(bf16[4,128,768]{2,1,0:T(8,128)(2,1)} %bitcast.18), calls=%async_computation.2 | async-start | bytes 1572864 | tf_op jit(solution)/shard_map/all_to_all | solution.py:46
  96.2 2.5 %shard_map.94 = (f32[128,1536]{1,0:T(8,128)}, bf16[128,768]{1,0:T(8,128)(2,1)S(1)}) custom-call(s32[1]{0:T(128)} %bitcast.2.index, bf16[4,128,1536]{2,1,0:T(8,128)(2,1)} %all-to-all-done.3.terms), custom_call_target="tpu_custom_call" | custom-call | flops 3145728 | bytes 10485760 | tf_op jit(solution)/shard_map/pallas_call | solution.py:276
  98.7 1.4 collective-permute-start.18
  100.1 2.4 %collective-permute-start.17 = (bf16[128,768]{1,0:T(8,128)(2,1)S(1)}, bf16[128,768]{1,0:T(8,128)(2,1)}, u32[]{:S(2)}, u32[]{:S(2)}) collective-permute-start(bf16[128,768]{1,0:T(8,128)(2,1)S(1)} %get-tuple-element.34.refs_0_), channel_id=1, source_target_pairs={{0,128},{32,160},{64,192},{96,224},{128,0},{160,32},{192,64},{224,... | collective-permute-start | bytes 589832 | tf_op jit(solution)/shard_map/ppermute | solution.py:61
  102.5 1.2 collective-permute-start.16
  103.7 1.1 all-to-all-done.2.terms
  104.8 1.4 shard_map.95.refs_0_
  106.2 2.5 %collective-permute-done.18.refs_3_ = bf16[128,768]{1,0:T(8,128)(2,1)} collective-permute-done((bf16[128,768]{1,0:T(8,128)(2,1)S(1)}, bf16[128,768]{1,0:T(8,128)(2,1)}, u32[]{:S(2)}, u32[]{:S(2)}) %collective-permute-start.18) | collective-permute-done | bytes 196640 | tf_op jit(solution)/shard_map/ppermute | solution.py:61
  108.7 4.6 %collective-permute-done.17.refs_2_ = bf16[128,768]{1,0:T(8,128)(2,1)} collective-permute-done((bf16[128,768]{1,0:T(8,128)(2,1)S(1)}, bf16[128,768]{1,0:T(8,128)(2,1)}, u32[]{:S(2)}, u32[]{:S(2)}) %collective-permute-start.17) | collective-permute-done | bytes 196640 | tf_op jit(solution)/shard_map/ppermute | solution.py:61
  113.6 5.4 %shard_map.96 = (bf16[512,2048]{1,0:T(8,128)(2,1)}, bf16[512,768]{1,0:T(8,128)(2,1)}) custom-call(s32[1]{0:T(128)} %bitcast.2.index, bf16[128,768]{1,0:T(8,128)(2,1)S(1)} %get-tuple-element.34.refs_0_, bf16[128,768]{1,0:T(8,128)(2,1)} %collective-permute-done.16.refs_1_, bf16[128,768]{1,0:T(8,128)(2,1)} %collective-permute-done.17.refs_2_, ...), custom_call_target="tpu_custom_call" | custom-call | flops 1610612736 | bytes 10485760 | tf_op jit(solution)/shard_map/pallas_call | solution.py:211
  119.0 4.5 %all-to-all-start.4 = ((bf16[4,128,2048]{2,1,0:T(8,128)(2,1)}), bf16[4,128,2048]{2,1,0:T(8,128)(2,1)}, u32[]{:S(2)}, u32[]{:S(2)}) async-start(bf16[4,128,2048]{2,1,0:T(8,128)(2,1)} %bitcast.15), calls=%async_computation.4 | async-start | bytes 4194304 | tf_op jit(solution)/shard_map/all_to_all | solution.py:46
  123.4 0.9 collective-permute-start.26
  124.3 4.1 %collective-permute-start.25 = (bf16[128,1536]{1,0:T(8,128)(2,1)S(1)}, bf16[128,1536]{1,0:T(8,128)(2,1)S(1)}, u32[]{:S(2)}, u32[]{:S(2)}) collective-permute-start(bf16[128,1536]{1,0:T(8,128)(2,1)S(1)} %shard_map.95.refs_0_), channel_id=1, source_target_pairs={{0,128},{32,160},{64,192},{96,224},{128,0},{160,32},{192,64},{224,... | collective-permute-start | bytes 1179656 | tf_op jit(solution)/shard_map/ppermute | solution.py:61
  128.3 4.6 %collective-permute-done.26.refs_3_ = bf16[128,1536]{1,0:T(8,128)(2,1)S(1)} collective-permute-done((bf16[128,1536]{1,0:T(8,128)(2,1)S(1)}, bf16[128,1536]{1,0:T(8,128)(2,1)S(1)}, u32[]{:S(2)}, u32[]{:S(2)}) %collective-permute-start.26) | collective-permute-done | bytes 393248 | tf_op jit(solution)/shard_map/ppermute | solution.py:61
  132.9 11.5 %collective-permute-done.25.refs_2_ = bf16[128,1536]{1,0:T(8,128)(2,1)S(1)} collective-permute-done((bf16[128,1536]{1,0:T(8,128)(2,1)S(1)}, bf16[128,1536]{1,0:T(8,128)(2,1)S(1)}, u32[]{:S(2)}, u32[]{:S(2)}) %collective-permute-start.25) | collective-permute-done | bytes 393248 | tf_op jit(solution)/shard_map/ppermute | solution.py:61
  144.8 7.2 %shard_map.99 = (bf16[512,2048]{1,0:T(8,128)(2,1)}, bf16[512,768]{1,0:T(8,128)(2,1)}, bf16[512,768]{1,0:T(8,128)(2,1)}) custom-call(s32[1]{0:T(128)} %bitcast.2.index, bf16[128,1536]{1,0:T(8,128)(2,1)S(1)} %shard_map.95.refs_0_, bf16[128,1536]{1,0:T(8,128)(2,1)S(1)} %collective-permute-done.24.refs_1_, ...), custom_call_target="tpu_custom_call" | custom-call | flops 3221225472 | bytes 10485760 | tf_op jit(solution)/shard_map/pallas_call | solution.py:247
  152.0 4.5 %all-to-all-start.5 = ((bf16[4,128,2048]{2,1,0:T(8,128)(2,1)}), bf16[4,128,2048]{2,1,0:T(8,128)(2,1)}, u32[]{:S(2)}, u32[]{:S(2)}) async-start(bf16[4,128,2048]{2,1,0:T(8,128)(2,1)} %bitcast.14), calls=%async_computation.5 | async-start | bytes 4194304 | tf_op jit(solution)/shard_map/all_to_all | solution.py:46
  156.5 2.5 %shard_map.97 = (bf16[64,2048]{1,0:T(8,128)(2,1)S(1)}, bf16[64,2048]{1,0:T(8,128)(2,1)S(1)}) custom-call(s32[2]{0:T(128)S(1)} %pad_add_fusion.index, bf16[4,128,2048]{2,1,0:T(8,128)(2,1)} %all-to-all-done.4.terms), custom_call_target="tpu_custom_call" | custom-call | flops 2097152 | bytes 10485760 | tf_op jit(solution)/shard_map/pallas_call | solution.py:352
  159.0 1.5 collective-permute-start.19
  160.5 8.2 %collective-permute-done.19.far = bf16[64,2048]{1,0:T(8,128)(2,1)S(1)} collective-permute-done((bf16[64,2048]{1,0:T(8,128)(2,1)S(1)}, bf16[64,2048]{1,0:T(8,128)(2,1)S(1)}, u32[]{:S(2)}, u32[]{:S(2)}) %collective-permute-start.19) | collective-permute-done | bytes 262176 | tf_op jit(solution)/shard_map/ppermute | solution.py:443
  169.4 2.1 collective-permute-start.20
  171.5 5.7 %collective-permute-start.21 = (bf16[16,2048]{1,0:T(8,128)(2,1)S(1)}, bf16[16,2048]{1,0:T(8,128)(2,1)S(1)}, u32[]{:S(2)}, u32[]{:S(2)}) collective-permute-start(bf16[16,2048]{1,0:T(8,128)(2,1)S(1)} %get-tuple-element.40), channel_id=1, source_target_pairs={{0,4},{1,5},{2,6},{3,7},{4,8},{5,9},{6,10},{7,11},{8,12},{9,13},{1... | collective-permute-start | bytes 196616 | tf_op jit(solution)/shard_map/ppermute | solution.py:446
  177.2 3.2 %collective-permute-start.22 = (bf16[16,2048]{1,0:T(8,128)(2,1)S(1)}, bf16[16,2048]{1,0:T(8,128)(2,1)S(1)}, u32[]{:S(2)}, u32[]{:S(2)}) collective-permute-start(bf16[16,2048]{1,0:T(8,128)(2,1)S(1)} %get-tuple-element.41), channel_id=1, source_target_pairs={{0,8},{1,9},{2,10},{3,11},{4,12},{5,13},{6,14},{7,15},{8,16},{9,17... | collective-permute-start | bytes 196616 | tf_op jit(solution)/shard_map/ppermute | solution.py:446
  180.4 1.7 collective-permute-start.29
  182.6 3.1 %collective-permute-start.30 = (bf16[512,768]{1,0:T(8,128)(2,1)}, bf16[512,768]{1,0:T(8,128)(2,1)}, u32[]{:S(2)}, u32[]{:S(2)}) collective-permute-start(bf16[512,768]{1,0:T(8,128)(2,1)} %get-tuple-element.50), channel_id=1, source_target_pairs={{0,32},{32,0},{64,96},{96,64},{128,160},{160,128},{192,224},{224,1... | collective-permute-start | bytes 2359304 | tf_op jit(solution)/shard_map/ppermute | solution.py:41
  185.8 1.1 collective-permute-start.23
  187.0 1.2 fusion.19
  189.2 2.7 %shard_map.100 = bf16[128,2048]{1,0:T(8,128)(2,1)} custom-call(s32[1]{0:T(128)} %bitcast.2.index, bf16[4,128,2048]{2,1,0:T(8,128)(2,1)} %all-to-all-done.5.terms), custom_call_target="tpu_custom_call" | custom-call | flops 2097152 | bytes 10485760 | tf_op jit(solution)/shard_map/pallas_call | solution.py:330
  191.9 4.8 %all-to-all-start.6 = ((bf16[8,16,2048]{2,1,0:T(8,128)(2,1)}), bf16[8,16,2048]{2,1,0:T(8,128)(2,1)S(1)}, u32[]{:S(2)}, u32[]{:S(2)}) async-start(bf16[8,16,2048]{2,1,0:T(8,128)(2,1)} %bitcast.16), calls=%async_computation.6 | async-start | bytes 1048576 | tf_op jit(solution)/shard_map/all_to_all | solution.py:46
  196.7 5.0 %fusion.4 = bf16[768,1024]{1,0:T(8,128)(2,1)} fusion(bf16[512,1024]{1,0:T(8,128)(2,1)} %collective-permute-done.28, bf16[512,1024]{1,0:T(8,128)(2,1)} %get-tuple-element.54, bf16[512,768]{1,0:T(8,128)(2,1)} %collective-permute-done.27, bf16[512,768]{1,0:T(8,128)(2,1)} %get-tuple-element.47), kind=kOutput, calls=%fused_computation.5 | convolution fusion | flops 1618739200 | bytes 5242880 | tf_op jit(solution)/shard_map/dot_general | solution.py:37
  201.7 4.7 %convolution_convert_fusion.1 = bf16[1024,768]{1,0:T(8,128)(2,1)} fusion(bf16[512,768]{1,0:T(8,128)(2,1)} %collective-permute-done.30, bf16[512,768]{1,0:T(8,128)(2,1)} %get-tuple-element.50, bf16[512,1024]{1,0:T(8,128)(2,1)} %collective-permute-done.29, bf16[512,1024]{1,0:T(8,128)(2,1)S(1)} %get-tuple-element.53), kind=kOutput, calls=%fused_computation.7 | convolution fusion | flops 1618739200 | bytes 5242880 | tf_op jit(solution)/shard_map/dot_general | solution.py:37
  206.4 4.7 %convolution_convert_fusion = bf16[1024,768]{1,0:T(8,128)(2,1)} fusion(bf16[512,768]{1,0:T(8,128)(2,1)} %collective-permute-done.31, bf16[512,768]{1,0:T(8,128)(2,1)} %get-tuple-element.51, bf16[512,1024]{1,0:T(8,128)(2,1)} %collective-permute-done.29, bf16[512,1024]{1,0:T(8,128)(2,1)S(1)} %get-tuple-element.53), kind=kOutput, calls=%fused_computation.6 | convolution fusion | flops 1618739200 | bytes 5242880 | tf_op jit(solution)/shard_map/dot_general | solution.py:37
  211.1 3.6 %all-to-all-done.6 = bf16[8,16,2048]{2,1,0:T(8,128)(2,1)S(1)} async-done(((bf16[8,16,2048]{2,1,0:T(8,128)(2,1)}), bf16[8,16,2048]{2,1,0:T(8,128)(2,1)S(1)}, u32[]{:S(2)}, u32[]{:S(2)}) %all-to-all-start.6) | async-done | bytes 524320 | tf_op jit(solution)/shard_map/all_to_all | solution.py:46
  215.3 0.9 collective-permute-done.32
  (52 shorter events, 4.9 us)
Async XLA Ops:
  3.1 29.7 %all-to-all-start = ((bf16[8,16,2048]{2,1,0:T(8,128)(2,1)}), bf16[8,16,2048]{2,1,0:T(8,128)(2,1)S(1)}, u32[]{:S(2)}, u32[]{:S(2)}) async-start(bf16[8,16,2048]{2,1,0:T(8,128)(2,1)} %tile.4), calls=%async_computation | async-start | bytes 1048576 | tf_op jit(solution)/shard_map/all_to_all | solution.py:46
  12.1 1.8 collective-permute-start
  13.0 1.2 collective-permute-start.1
  14.3 5.0 %collective-permute-start.4 = (bf16[16,2048]{1,0:T(8,128)(2,1)S(1)}, bf16[16,2048]{1,0:T(8,128)(2,1)S(1)}, u32[]{:S(2)}, u32[]{:S(2)}) collective-permute-start(bf16[16,2048]{1,0:T(8,128)(2,1)S(1)} %constant_dynamic-update-slice_fusion), channel_id=1, source_target_pairs={{0,1},{1,2},{2,3},{3,0},{4,5},{5,6},{6,7},{7,4},{8,9},{9,10},{10,1... | collective-permute-start | bytes 196616 | tf_op jit(solution)/shard_map/ppermute | solution.py:61
  15.6 6.1 %collective-permute-start.3 = (bf16[16,2048]{1,0:T(8,128)(2,1)S(1)}, bf16[16,2048]{1,0:T(8,128)(2,1)S(1)}, u32[]{:S(2)}, u32[]{:S(2)}) collective-permute-start(bf16[16,2048]{1,0:T(8,128)(2,1)S(1)} %constant_dynamic-update-slice_fusion), channel_id=1, source_target_pairs={{0,2},{1,3},{2,0},{3,1},{4,6},{5,7},{6,4},{7,5},{8,10},{9,11},{10,... | collective-permute-start | bytes 196616 | tf_op jit(solution)/shard_map/ppermute | solution.py:61
  18.2 3.5 %collective-permute-start.2 = (bf16[16,2048]{1,0:T(8,128)(2,1)S(1)}, bf16[16,2048]{1,0:T(8,128)(2,1)S(1)}, u32[]{:S(2)}, u32[]{:S(2)}) collective-permute-start(bf16[16,2048]{1,0:T(8,128)(2,1)S(1)} %constant_dynamic-update-slice_fusion), channel_id=1, source_target_pairs={{0,3},{1,0},{2,1},{3,2},{4,7},{5,4},{6,5},{7,6},{8,11},{9,8},{10,9... | collective-permute-start | bytes 196616 | tf_op jit(solution)/shard_map/ppermute | solution.py:61
  21.7 11.1 %collective-permute-start.6 = (bf16[64,2048]{1,0:T(8,128)(2,1)S(1)}, bf16[64,2048]{1,0:T(8,128)(2,1)S(1)}, u32[]{:S(2)}, u32[]{:S(2)}) collective-permute-start(bf16[64,2048]{1,0:T(8,128)(2,1)S(1)} %pad_maximum_fusion.3.refs_0_), channel_id=1, source_target_pairs={{0,4},{1,5},{2,6},{3,7},{4,8},{5,9},{6,10},{7,11},{8,12},{9,13},{1... | collective-permute-start | bytes 786440 | tf_op jit(solution)/shard_map/ppermute | solution.py:68
  23.5 9.3 %collective-permute-start.5 = (bf16[64,2048]{1,0:T(8,128)(2,1)S(1)}, bf16[64,2048]{1,0:T(8,128)(2,1)S(1)}, u32[]{:S(2)}, u32[]{:S(2)}) collective-permute-start(bf16[64,2048]{1,0:T(8,128)(2,1)S(1)} %pad_maximum_fusion.3.refs_0_), channel_id=1, source_target_pairs={{4,0},{5,1},{6,2},{7,3},{8,4},{9,5},{10,6},{11,7},{12,8},{13,9},{1... | collective-permute-start | bytes 786440 | tf_op jit(solution)/shard_map/ppermute | solution.py:69
  24.8 33.8 %collective-permute-start.14 = (bf16[1024,768]{1,0:T(8,128)(2,1)}, bf16[1024,768]{1,0:T(8,128)(2,1)}, u32[]{:S(2)}, u32[]{:S(2)}) collective-permute-start(bf16[1024,768]{1,0:T(8,128)(2,1)} %refs_4_.3), channel_id=1, source_target_pairs={{0,32},{32,0},{64,96},{96,64},{128,160},{160,128},{192,224},{224,1... | collective-permute-start | bytes 4718600 | tf_op jit(solution)/shard_map/ppermute | solution.py:41
  26.6 32.0 %collective-permute-start.15 = (bf16[1024,768]{1,0:T(8,128)(2,1)}, bf16[1024,768]{1,0:T(8,128)(2,1)}, u32[]{:S(2)}, u32[]{:S(2)}) collective-permute-start(bf16[1024,768]{1,0:T(8,128)(2,1)} %refs_5_.1), channel_id=1, source_target_pairs={{0,32},{32,0},{64,96},{96,64},{128,160},{160,128},{192,224},{224,1... | collective-permute-start | bytes 4718600 | tf_op jit(solution)/shard_map/ppermute | solution.py:41
  34.4 28.3 %all-to-all-start.1 = ((bf16[4,128,2048]{2,1,0:T(8,128)(2,1)}), bf16[4,128,2048]{2,1,0:T(8,128)(2,1)S(1)}, u32[]{:S(2)}, u32[]{:S(2)}) async-start(bf16[4,128,2048]{2,1,0:T(8,128)(2,1)} %tile.5), calls=%async_computation.1 | async-start | bytes 4194304 | tf_op jit(solution)/shard_map/all_to_all | solution.py:46
  38.0 7.6 %collective-permute-start.9 = (bf16[64,2048]{1,0:T(8,128)(2,1)S(1)}, bf16[64,2048]{1,0:T(8,128)(2,1)S(1)}, u32[]{:S(2)}, u32[]{:S(2)}) collective-permute-start(bf16[64,2048]{1,0:T(8,128)(2,1)S(1)} %collective-permute-done.6.refs_8_), channel_id=1, source_target_pairs={{0,4},{1,5},{2,6},{3,7},{4,8},{5,9},{6,10},{7,11},{8,12},{9,13},{1... | collective-permute-start | bytes 786440 | tf_op jit(solution)/shard_map/ppermute | solution.py:68
  38.2 7.4 %collective-permute-start.7 = (bf16[64,2048]{1,0:T(8,128)(2,1)S(1)}, bf16[64,2048]{1,0:T(8,128)(2,1)S(1)}, u32[]{:S(2)}, u32[]{:S(2)}) collective-permute-start(bf16[64,2048]{1,0:T(8,128)(2,1)S(1)} %collective-permute-done.5.refs_1_), channel_id=1, source_target_pairs={{4,0},{5,1},{6,2},{7,3},{8,4},{9,5},{10,6},{11,7},{12,8},{13,9},{1... | collective-permute-start | bytes 786440 | tf_op jit(solution)/shard_map/ppermute | solution.py:69
  45.6 2.7 %copy-start = (bf16[64,2048]{1,0:T(8,128)(2,1)}, bf16[64,2048]{1,0:T(8,128)(2,1)S(1)}, u32[]{:S(2)}) copy-start(bf16[64,2048]{1,0:T(8,128)(2,1)S(1)} %collective-permute-done.9.refs_7_) | copy-start | bytes 786436
  45.6 6.7 %collective-permute-start.10 = (bf16[64,2048]{1,0:T(8,128)(2,1)S(1)}, bf16[64,2048]{1,0:T(8,128)(2,1)S(1)}, u32[]{:S(2)}, u32[]{:S(2)}) collective-permute-start(bf16[64,2048]{1,0:T(8,128)(2,1)S(1)} %collective-permute-done.9.refs_7_), channel_id=1, source_target_pairs={{0,4},{1,5},{2,6},{3,7},{4,8},{5,9},{6,10},{7,11},{8,12},{9,13},{1... | collective-permute-start | bytes 786440 | tf_op jit(solution)/shard_map/ppermute | solution.py:68
  45.6 7.4 %copy-start.1 = (bf16[64,2048]{1,0:T(8,128)(2,1)}, bf16[64,2048]{1,0:T(8,128)(2,1)S(1)}, u32[]{:S(2)}) copy-start(bf16[64,2048]{1,0:T(8,128)(2,1)S(1)} %collective-permute-done.7.refs_2_) | copy-start | bytes 786436
  45.6 7.4 %collective-permute-start.8 = (bf16[64,2048]{1,0:T(8,128)(2,1)S(1)}, bf16[64,2048]{1,0:T(8,128)(2,1)S(1)}, u32[]{:S(2)}, u32[]{:S(2)}) collective-permute-start(bf16[64,2048]{1,0:T(8,128)(2,1)S(1)} %collective-permute-done.7.refs_2_), channel_id=1, source_target_pairs={{4,0},{5,1},{6,2},{7,3},{8,4},{9,5},{10,6},{11,7},{12,8},{13,9},{1... | collective-permute-start | bytes 786440 | tf_op jit(solution)/shard_map/ppermute | solution.py:69
  48.3 26.2 %collective-permute-start.13 = (bf16[768,1024]{1,0:T(8,128)(2,1)}, bf16[768,1024]{1,0:T(8,128)(2,1)}, u32[]{:S(2)}, u32[]{:S(2)}) collective-permute-start(bf16[768,1024]{1,0:T(8,128)(2,1)} %refs_4_.2), channel_id=1, source_target_pairs={{0,32},{32,0},{64,96},{96,64},{128,160},{160,128},{192,224},{224,1... | collective-permute-start | bytes 4718600 | tf_op jit(solution)/shard_map/ppermute | solution.py:41
  53.0 5.5 %collective-permute-start.11 = (bf16[32,2048]{1,0:T(8,128)(2,1)}, bf16[32,2048]{1,0:T(8,128)(2,1)S(1)}, u32[]{:S(2)}, u32[]{:S(2)}) collective-permute-start(bf16[32,2048]{1,0:T(8,128)(2,1)} %slice.32), channel_id=1, source_target_pairs={{0,4},{1,5},{2,6},{3,7},{4,8},{5,9},{6,10},{7,11},{8,12},{9,13},{1... | collective-permute-start | bytes 393224 | tf_op jit(solution)/shard_map/ppermute | solution.py:70
  53.6 4.9 %collective-permute-start.12 = (bf16[32,2048]{1,0:T(8,128)(2,1)}, bf16[32,2048]{1,0:T(8,128)(2,1)}, u32[]{:S(2)}, u32[]{:S(2)}) collective-permute-start(bf16[32,2048]{1,0:T(8,128)(2,1)} %slice.33), channel_id=1, source_target_pairs={{4,0},{5,1},{6,2},{7,3},{8,4},{9,5},{10,6},{11,7},{12,8},{13,9},{1... | collective-permute-start | bytes 393224 | tf_op jit(solution)/shard_map/ppermute | solution.py:71
  70.0 22.6 %all-to-all-start.3 = ((bf16[4,128,1536]{2,1,0:T(8,128)(2,1)}), bf16[4,128,1536]{2,1,0:T(8,128)(2,1)}, u32[]{:S(2)}, u32[]{:S(2)}) async-start(bf16[4,128,1536]{2,1,0:T(8,128)(2,1)} %bitcast.17), calls=%async_computation.3 | async-start | bytes 3145728 | tf_op jit(solution)/shard_map/all_to_all | solution.py:46
  92.7 12.1 %all-to-all-start.2 = ((bf16[4,128,768]{2,1,0:T(8,128)(2,1)}), bf16[4,128,768]{2,1,0:T(8,128)(2,1)S(1)}, u32[]{:S(2)}, u32[]{:S(2)}) async-start(bf16[4,128,768]{2,1,0:T(8,128)(2,1)} %bitcast.18), calls=%async_computation.2 | async-start | bytes 1572864 | tf_op jit(solution)/shard_map/all_to_all | solution.py:46
  98.7 10.1 %collective-permute-start.18 = (bf16[128,768]{1,0:T(8,128)(2,1)S(1)}, bf16[128,768]{1,0:T(8,128)(2,1)}, u32[]{:S(2)}, u32[]{:S(2)}) collective-permute-start(bf16[128,768]{1,0:T(8,128)(2,1)S(1)} %get-tuple-element.34.refs_0_), channel_id=1, source_target_pairs={{0,64},{32,96},{64,128},{96,160},{128,192},{160,224},{192,0},{224,... | collective-permute-start | bytes 589832 | tf_op jit(solution)/shard_map/ppermute | solution.py:61
  100.1 13.3 %collective-permute-start.17 = (bf16[128,768]{1,0:T(8,128)(2,1)S(1)}, bf16[128,768]{1,0:T(8,128)(2,1)}, u32[]{:S(2)}, u32[]{:S(2)}) collective-permute-start(bf16[128,768]{1,0:T(8,128)(2,1)S(1)} %get-tuple-element.34.refs_0_), channel_id=1, source_target_pairs={{0,128},{32,160},{64,192},{96,224},{128,0},{160,32},{192,64},{224,... | collective-permute-start | bytes 589832 | tf_op jit(solution)/shard_map/ppermute | solution.py:61
  102.5 11.1 %collective-permute-start.16 = (bf16[128,768]{1,0:T(8,128)(2,1)S(1)}, bf16[128,768]{1,0:T(8,128)(2,1)}, u32[]{:S(2)}, u32[]{:S(2)}) collective-permute-start(bf16[128,768]{1,0:T(8,128)(2,1)S(1)} %get-tuple-element.34.refs_0_), channel_id=1, source_target_pairs={{0,192},{32,224},{64,0},{96,32},{128,64},{160,96},{192,128},{224,1... | collective-permute-start | bytes 589832 | tf_op jit(solution)/shard_map/ppermute | solution.py:61
  119.0 33.1 %all-to-all-start.4 = ((bf16[4,128,2048]{2,1,0:T(8,128)(2,1)}), bf16[4,128,2048]{2,1,0:T(8,128)(2,1)}, u32[]{:S(2)}, u32[]{:S(2)}) async-start(bf16[4,128,2048]{2,1,0:T(8,128)(2,1)} %bitcast.15), calls=%async_computation.4 | async-start | bytes 4194304 | tf_op jit(solution)/shard_map/all_to_all | solution.py:46
  123.4 9.5 %collective-permute-start.26 = (bf16[128,1536]{1,0:T(8,128)(2,1)S(1)}, bf16[128,1536]{1,0:T(8,128)(2,1)S(1)}, u32[]{:S(2)}, u32[]{:S(2)}) collective-permute-start(bf16[128,1536]{1,0:T(8,128)(2,1)S(1)} %shard_map.95.refs_0_), channel_id=1, source_target_pairs={{0,64},{32,96},{64,128},{96,160},{128,192},{160,224},{192,0},{224,... | collective-permute-start | bytes 1179656 | tf_op jit(solution)/shard_map/ppermute | solution.py:61
  124.3 20.2 %collective-permute-start.25 = (bf16[128,1536]{1,0:T(8,128)(2,1)S(1)}, bf16[128,1536]{1,0:T(8,128)(2,1)S(1)}, u32[]{:S(2)}, u32[]{:S(2)}) collective-permute-start(bf16[128,1536]{1,0:T(8,128)(2,1)S(1)} %shard_map.95.refs_0_), channel_id=1, source_target_pairs={{0,128},{32,160},{64,192},{96,224},{128,0},{160,32},{192,64},{224,... | collective-permute-start | bytes 1179656 | tf_op jit(solution)/shard_map/ppermute | solution.py:61
  128.3 16.5 %collective-permute-start.24 = (bf16[128,1536]{1,0:T(8,128)(2,1)S(1)}, bf16[128,1536]{1,0:T(8,128)(2,1)S(1)}, u32[]{:S(2)}, u32[]{:S(2)}) collective-permute-start(bf16[128,1536]{1,0:T(8,128)(2,1)S(1)} %shard_map.95.refs_0_), channel_id=1, source_target_pairs={{0,192},{32,224},{64,0},{96,32},{128,64},{160,96},{192,128},{224,1... | collective-permute-start | bytes 1179656 | tf_op jit(solution)/shard_map/ppermute | solution.py:61
  152.0 37.2 %all-to-all-start.5 = ((bf16[4,128,2048]{2,1,0:T(8,128)(2,1)}), bf16[4,128,2048]{2,1,0:T(8,128)(2,1)}, u32[]{:S(2)}, u32[]{:S(2)}) async-start(bf16[4,128,2048]{2,1,0:T(8,128)(2,1)} %bitcast.14), calls=%async_computation.5 | async-start | bytes 4194304 | tf_op jit(solution)/shard_map/all_to_all | solution.py:46
  159.0 9.8 %collective-permute-start.19 = (bf16[64,2048]{1,0:T(8,128)(2,1)S(1)}, bf16[64,2048]{1,0:T(8,128)(2,1)S(1)}, u32[]{:S(2)}, u32[]{:S(2)}) collective-permute-start(bf16[64,2048]{1,0:T(8,128)(2,1)S(1)} %get-tuple-element.37), channel_id=1, source_target_pairs={{0,16},{1,17},{2,18},{3,19},{4,20},{5,21},{6,22},{7,23},{8,24},{9,... | collective-permute-start | bytes 786440 | tf_op jit(solution)/shard_map/ppermute | solution.py:443
  169.4 12.7 %collective-permute-start.20 = (bf16[16,2048]{1,0:T(8,128)(2,1)S(1)}, bf16[16,2048]{1,0:T(8,128)(2,1)S(1)}, u32[]{:S(2)}, u32[]{:S(2)}) collective-permute-start(bf16[16,2048]{1,0:T(8,128)(2,1)S(1)} %get-tuple-element.39), channel_id=1, source_target_pairs={{0,28},{1,29},{2,30},{3,31},{4,0},{5,1},{6,2},{7,3},{8,4},{9,5},{1... | collective-permute-start | bytes 196616 | tf_op jit(solution)/shard_map/ppermute | solution.py:446
  171.5 11.1 %collective-permute-start.21 = (bf16[16,2048]{1,0:T(8,128)(2,1)S(1)}, bf16[16,2048]{1,0:T(8,128)(2,1)S(1)}, u32[]{:S(2)}, u32[]{:S(2)}) collective-permute-start(bf16[16,2048]{1,0:T(8,128)(2,1)S(1)} %get-tuple-element.40), channel_id=1, source_target_pairs={{0,4},{1,5},{2,6},{3,7},{4,8},{5,9},{6,10},{7,11},{8,12},{9,13},{1... | collective-permute-start | bytes 196616 | tf_op jit(solution)/shard_map/ppermute | solution.py:446
  177.2 8.6 %collective-permute-start.22 = (bf16[16,2048]{1,0:T(8,128)(2,1)S(1)}, bf16[16,2048]{1,0:T(8,128)(2,1)S(1)}, u32[]{:S(2)}, u32[]{:S(2)}) collective-permute-start(bf16[16,2048]{1,0:T(8,128)(2,1)S(1)} %get-tuple-element.41), channel_id=1, source_target_pairs={{0,8},{1,9},{2,10},{3,11},{4,12},{5,13},{6,14},{7,15},{8,16},{9,17... | collective-permute-start | bytes 196616 | tf_op jit(solution)/shard_map/ppermute | solution.py:446
  180.4 21.3 %collective-permute-start.29 = (bf16[512,1024]{1,0:T(8,128)(2,1)}, bf16[512,1024]{1,0:T(8,128)(2,1)}, u32[]{:S(2)}, u32[]{:S(2)}) collective-permute-start(bf16[512,1024]{1,0:T(8,128)(2,1)} %get-tuple-element.49), channel_id=1, source_target_pairs={{0,32},{32,0},{64,96},{96,64},{128,160},{160,128},{192,224},{224,1... | collective-permute-start | bytes 3145736 | tf_op jit(solution)/shard_map/ppermute | solution.py:41
  182.1 14.5 %collective-permute-start.28 = (bf16[512,1024]{1,0:T(8,128)(2,1)}, bf16[512,1024]{1,0:T(8,128)(2,1)}, u32[]{:S(2)}, u32[]{:S(2)}) collective-permute-start(bf16[512,1024]{1,0:T(8,128)(2,1)} %get-tuple-element.48), channel_id=1, source_target_pairs={{0,32},{32,0},{64,96},{96,64},{128,160},{160,128},{192,224},{224,1... | collective-permute-start | bytes 3145736 | tf_op jit(solution)/shard_map/ppermute | solution.py:41
  182.1 14.5 %collective-permute-start.27 = (bf16[512,768]{1,0:T(8,128)(2,1)}, bf16[512,768]{1,0:T(8,128)(2,1)}, u32[]{:S(2)}, u32[]{:S(2)}) collective-permute-start(bf16[512,768]{1,0:T(8,128)(2,1)} %get-tuple-element.47), channel_id=1, source_target_pairs={{0,32},{32,0},{64,96},{96,64},{128,160},{160,128},{192,224},{224,1... | collective-permute-start | bytes 2359304 | tf_op jit(solution)/shard_map/ppermute | solution.py:41
  182.6 19.0 %collective-permute-start.30 = (bf16[512,768]{1,0:T(8,128)(2,1)}, bf16[512,768]{1,0:T(8,128)(2,1)}, u32[]{:S(2)}, u32[]{:S(2)}) collective-permute-start(bf16[512,768]{1,0:T(8,128)(2,1)} %get-tuple-element.50), channel_id=1, source_target_pairs={{0,32},{32,0},{64,96},{96,64},{128,160},{160,128},{192,224},{224,1... | collective-permute-start | bytes 2359304 | tf_op jit(solution)/shard_map/ppermute | solution.py:41
  185.8 2.4 %collective-permute-start.23 = (bf16[16,1024]{1,0:T(8,128)(2,1)S(1)}, bf16[16,1024]{1,0:T(8,128)(2,1)S(1)}, u32[]{:S(2)}, u32[]{:S(2)}) collective-permute-start(bf16[16,1024]{1,0:T(8,128)(2,1)S(1)} %slice.35), channel_id=1, source_target_pairs={{0,32},{32,0},{64,96},{96,64},{128,160},{160,128},{192,224},{224,1... | collective-permute-start | bytes 98312 | tf_op jit(solution)/shard_map/ppermute | solution.py:41
  188.2 18.2 %collective-permute-start.31 = (bf16[512,768]{1,0:T(8,128)(2,1)}, bf16[512,768]{1,0:T(8,128)(2,1)}, u32[]{:S(2)}, u32[]{:S(2)}) collective-permute-start(bf16[512,768]{1,0:T(8,128)(2,1)} %get-tuple-element.51), channel_id=1, source_target_pairs={{0,32},{32,0},{64,96},{96,64},{128,160},{160,128},{192,224},{224,1... | collective-permute-start | bytes 2359304 | tf_op jit(solution)/shard_map/ppermute | solution.py:41
  191.9 22.7 %all-to-all-start.6 = ((bf16[8,16,2048]{2,1,0:T(8,128)(2,1)}), bf16[8,16,2048]{2,1,0:T(8,128)(2,1)S(1)}, u32[]{:S(2)}, u32[]{:S(2)}) async-start(bf16[8,16,2048]{2,1,0:T(8,128)(2,1)} %bitcast.16), calls=%async_computation.6 | async-start | bytes 1048576 | tf_op jit(solution)/shard_map/all_to_all | solution.py:46
  214.7 1.4 collective-permute-start.32
where the time goes:
time: 218 us; the launch traced here: 217 us
  starting transfers between devices  86.1 us (39%)
  waiting for transfers between devices  72.3 us (33%)
  Pallas kernels  35.1 us (16%)
  matrix products  14.4 us (7%)
  local copies, waits for them, and re-layouts  6.56 us (3%)
    all_to_all x7, starting transfers between devices, exchange(): lax.all_to_all(value, axis, 0, 0, axis_index_groups=groups, tiled=True)  34.2 us
    ppermute x9, waiting for transfers between devices, gather_blocks(): lax.ppermute(own, axis, steps[count - k])  26.3 us
    all_to_all x7, waiting for transfers between devices, exchange(): lax.all_to_all(value, axis, 0, 0, axis_index_groups=groups, tiled=True)  21.6 us
    ppermute x9, starting transfers between devices, gather_blocks(): lax.ppermute(own, axis, steps[count - k])  14.9 us
    dot_general x3, matrix products, dot(): return lax.dot_general(left, right, dims, preferred_element_type=F32)  14.4 us
    ppermute x12, starting transfers between devices, swap_core(): return lax.ppermute(value, 'row', CORE_PAIRS)  13.3 us
    ppermute x3, waiting for transfers between devices, ring_eight(): before.append(lax.ppermute(before[-1], axis, up))  12.1 us
    ppermute x3, starting transfers between devices, body(): mixed_sum += lax.ppermute(block, 'col', Z_STEP[step]).astype(F32)  11 us
  transfers between devices with their start and end apart: 40, of which 20 were waited for; matrix products, arithmetic and copies ran while one was open for 9% of the time, Pallas kernels for 14%

commit v1 on v0

--- a/solution.py
+++ b/solution.py
@@ -158,7 +158,8 @@
 
 
 def hidden_term_kernel(index, grad_a, *refs):
-    blocks, (down_a, down_b, out, grad_b) = refs[:9], refs[9:]
+    blocks, (down_a, down_b) = refs[:9], refs[9:11]
+    outs, (grad_b, total) = refs[11 : 11 + NX], refs[11 + NX :]
 
     @pl.when(pl.program_id(0) == 0)
     def _():
@@ -167,8 +168,12 @@
 
         place_eight(index, blocks, store)
 
-    total = dot(grad_a[...], down_a[...], NT) + dot(grad_b[...], down_b[...], NT)
-    out[...] = total.astype(BF16)
+    term = dot(grad_a[...], down_a[...], NT) + dot(grad_b[...], down_b[...], NT)
+    total[...] = term.astype(BF16)
+    rows = outs[0].shape[0]
+    for k, out in enumerate(outs):
+        start = pl.multiple_of(lax.rem(index[2] + k, NX) * rows, rows)
+        out[...] = total[pl.ds(start, rows), :]
 
 
 def hidden_term_product(index, own, blocks, down_a, down_b):
@@ -182,9 +187,10 @@
         [columns(rows, width, 1)]
         + [columns(block.shape[0], width, 1) for block in blocks]
         + [weight, weight],
-        [pl.BlockSpec((rows, tile), lambda j, _: (0, j)), whole((rows, width))],
-        [hbm((rows, cols)), hbm((rows, width))],
+        [pl.BlockSpec((rows // NX, tile), lambda j, _: (0, j))] * NX + [whole((rows, width))],
+        [hbm((rows // NX, cols))] * NX + [hbm((rows, width))],
         4 * rows * width * cols,
+        [pltpu.VMEM((rows, tile), BF16)],
     )(index, own, *blocks, down_a, down_b)
 
 
@@ -286,12 +292,14 @@
     )(index, terms)
 
 
-def pre_kernel(index, terms, gate_up, out):
+def pre_kernel(index, *refs):
     del index
-    total = total_of(terms)
-    cols = total.shape[1]
+    terms, (gate_up, out) = refs[:NX], refs[NX:]
+    cols = terms[0].shape[1]
     for k in range(cols // TILE):
-        hidden_grad = total[:, k * TILE : (k + 1) * TILE]
+        hidden_grad = terms[0][:, k * TILE : (k + 1) * TILE].astype(F32)
+        for term in terms[1:]:
+            hidden_grad = hidden_grad + term[:, k * TILE : (k + 1) * TILE].astype(F32)
         gate = gate_up[:, 2 * k * TILE : (2 * k + 1) * TILE]
         up = gate_up[:, (2 * k + 1) * TILE : (2 * k + 2) * TILE]
         sig = jax.nn.sigmoid(gate)
@@ -304,11 +312,11 @@
     return call(
         pre_kernel,
         (1,),
-        [whole(terms.shape), whole(gate_up.shape)],
+        [whole(term.shape) for term in terms] + [whole(gate_up.shape)],
         whole(gate_up.shape),
         jax.ShapeDtypeStruct(gate_up.shape, BF16),
         16 * gate_up.size,
-    )(index, terms, gate_up)
+    )(index, *terms, gate_up)
 
 
 def store_sum(terms, out):
@@ -385,7 +393,7 @@
     core = lax.axis_index("row") % NC
     x = (lax.axis_index("row") // NC).astype(jnp.int32).reshape(1)
     col = lax.axis_index("col")
-    zy = jnp.stack([col // NY, col % NY]).astype(jnp.int32)
+    zyx = jnp.stack([col // NY, col % NY, lax.axis_index("row") // NC]).astype(jnp.int32)
     half = tokens.shape[0] // NC
     width = tokens.shape[1]
 
@@ -415,13 +423,16 @@
     own_all = share(after(own_z, other_blocks[1], other_blocks[8]), "col", Y_GROUPS)
 
     gate_up_term, tok_other = gate_up_product(
-        zy, own_all, other_blocks, gate_own, gate_other, up_own, up_other
+        zyx, own_all, other_blocks, gate_own, gate_other, up_own, up_other
     )
     gate_up, hidden_own = hidden_of(x, exchange(gate_up_term, "row", X_GROUPS))
-    hidden_term, grad_other = hidden_term_product(
-        zy, own_all, other_blocks, down_own, down_other
-    )
-    pre_own = pre_grads(x, exchange(hidden_term, "row", X_GROUPS), in_hbm(gate_up))
+    *hidden_terms, grad_other = hidden_term_product(
+        zyx, own_all, other_blocks, down_own, down_other
+    )
+    hidden_terms = [in_hbm(hidden_terms[0])] + [
+        lax.ppermute(hidden_terms[k], "row", X_STEP[k]) for k in range(1, NX)
+    ]
+    pre_own = pre_grads(x, hidden_terms, in_hbm(gate_up))
 
     hidden_blocks = gather_blocks(hidden_own, "row", X_STEP)
     mixed_term, hidden = mixed_product(after(x, pre_own), hidden_blocks, down_own, down_other)
@@ -439,8 +450,10 @@
     down_grad = dot(all_tokens(hidden), grad_rows, TN).astype(BF16)
     gate_grad = dot(tok_rows, all_tokens(pre_gate), TN).astype(BF16)
     up_grad = dot(tok_rows, all_tokens(pre_up), TN).astype(BF16)
-    near, far = split_sum(zy, mixed_y)
-    previous, mine, following, second = fold(zy, near, lax.ppermute(far, "col", Z_STEP[4]))
+    near, far = split_sum(zyx, mixed_y)
+    previous, mine, following, second = fold(
+        zyx, near, after(lax.ppermute(far, "col", Z_STEP[4]), down_grad)
+    )
     mixed_sum = mine.astype(F32)
     for block, step in ((previous, NZ - 1), (following, 1), (second, 2)):
         mixed_sum += lax.ppermute(block, "col", Z_STEP[step]).astype(F32)

time: 218 us -> 213 us (0.977)
  waiting for transfers between devices: 72.3 us -> 67 us
    ppermute x0 -> x3, starting transfers between devices: none -> 5.01 us  [body(): lax.ppermute(hidden_terms[k], 'row', X_STEP[k])]
    ppermute x1, waiting for transfers between devices: 8.23 us -> 3.43 us  [body(): lax.ppermute(far, 'col', Z_STEP[4])]
    ppermute x9, waiting for transfers between devices: 26.3 us -> 21.6 us  [gather_blocks(): lax.ppermute(own, axis, steps[count - k])]
    ppermute x9, starting transfers between devices: 14.9 us -> 11 us  [gather_blocks(): lax.ppermute(own, axis, steps[count - k])]
    ppermute x0 -> x3, waiting for transfers between devices: none -> 2.87 us  [body(): lax.ppermute(hidden_terms[k], 'row', X_STEP[k])]
    all_to_all x7 -> x6, starting transfers between devices: 34.2 us -> 31.3 us  [exchange(): lax.all_to_all(value, axis, 0, 0, axis_index_groups=groups, tiled=True)]
    all_to_all x7 -> x6, waiting for transfers between devices: 21.6 us -> 20.7 us  [exchange(): lax.all_to_all(value, axis, 0, 0, axis_index_groups=groups, tiled=True)]
  transfers between devices with their start and end apart: 40 -> 42, of which waited for: 20 -> 21; matrix products, arithmetic and copies ran while one was open for 9% -> 9% of each run, Pallas kernels for 14% -> 14%
where the time goes in v1:
time: 213 us; the launch traced here: 212 us
  starting transfers between devices  86.5 us (41%)
  waiting for transfers between devices  67 us (31%)
  Pallas kernels  35.2 us (17%)
  matrix products  13.5 us (6%)
  local copies, waits for them, and re-layouts  7.3 us (3%)
    all_to_all x6, starting transfers between devices, exchange(): lax.all_to_all(value, axis, 0, 0, axis_index_groups=groups, tiled=True)  31.3 us
    ppermute x9, waiting for transfers between devices, gather_blocks(): lax.ppermute(own, axis, steps[count - k])  21.6 us
    all_to_all x6, waiting for transfers between devices, exchange(): lax.all_to_all(value, axis, 0, 0, axis_index_groups=groups, tiled=True)  20.7 us
    ppermute x12, starting transfers between devices, swap_core(): return lax.ppermute(value, 'row', CORE_PAIRS)  15.1 us
    dot_general x3, matrix products, dot(): return lax.dot_general(left, right, dims, preferred_element_type=F32)  13.5 us
    ppermute x3, waiting for transfers between devices, ring_eight(): before.append(lax.ppermute(before[-1], axis, up))  12.9 us
    ppermute x3, starting transfers between devices, body(): mixed_sum += lax.ppermute(block, 'col', Z_STEP[step]).astype(F32)  11.6 us
    ppermute x9, starting transfers between devices, gather_blocks(): lax.ppermute(own, axis, steps[count - k])  11 us
  transfers between devices with their start and end apart: 42, of which 21 were waited for; matrix products, arithmetic and copies ran while one was open for 9% of the time, Pallas kernels for 14%

profile of v1, /device:TPU:1, one launch (start us, length us, event | category | flops | bytes accessed | tf_op | source)
XLA Modules:
  0.0 211.8 jit_solution(2899735145819931697)
XLA Ops:
  0.7 0.8 constant_dynamic-slice_fusion.1
  1.4 0.8 constant_dynamic-slice_fusion
  2.2 0.8 tile.4
  3.1 9.0 %all-to-all-start = ((bf16[8,16,2048]{2,1,0:T(8,128)(2,1)}), bf16[8,16,2048]{2,1,0:T(8,128)(2,1)S(1)}, u32[]{:S(2)}, u32[]{:S(2)}) async-start(bf16[8,16,2048]{2,1,0:T(8,128)(2,1)} %tile.4), calls=%async_computation | async-start | bytes 1048576 | tf_op jit(solution)/shard_map/all_to_all | solution.py:46
  12.1 1.0 collective-permute-start
  13.1 0.8 collective-permute-done
  14.3 1.3 collective-permute-start.4
  15.6 2.6 %collective-permute-start.3 = (bf16[16,2048]{1,0:T(8,128)(2,1)S(1)}, bf16[16,2048]{1,0:T(8,128)(2,1)S(1)}, u32[]{:S(2)}, u32[]{:S(2)}) collective-permute-start(bf16[16,2048]{1,0:T(8,128)(2,1)S(1)} %constant_dynamic-update-slice_fusion), channel_id=1, source_target_pairs={{0,2},{1,3},{2,0},{3,1},{4,6},{5,7},{6,4},{7,5},{8,10},{9,11},{10,... | collective-permute-start | bytes 196616 | tf_op jit(solution)/shard_map/ppermute | solution.py:61
  18.2 1.1 collective-permute-start.2
  19.2 2.4 %collective-permute-done.3 = bf16[16,2048]{1,0:T(8,128)(2,1)S(1)} collective-permute-done((bf16[16,2048]{1,0:T(8,128)(2,1)S(1)}, bf16[16,2048]{1,0:T(8,128)(2,1)S(1)}, u32[]{:S(2)}, u32[]{:S(2)}) %collective-permute-start.3) | collective-permute-done | bytes 65568 | tf_op jit(solution)/shard_map/ppermute | solution.py:61
  21.7 1.8 collective-permute-start.6
  23.5 1.3 collective-permute-start.5
  24.8 1.8 collective-permute-start.17
  26.6 6.2 %collective-permute-done.6.refs_8_ = bf16[64,2048]{1,0:T(8,128)(2,1)S(1)} collective-permute-done((bf16[64,2048]{1,0:T(8,128)(2,1)S(1)}, bf16[64,2048]{1,0:T(8,128)(2,1)S(1)}, u32[]{:S(2)}, u32[]{:S(2)}) %collective-permute-start.6) | collective-permute-done | bytes 262176 | tf_op jit(solution)/shard_map/ppermute | solution.py:68
  32.8 1.6 tile.5
  34.4 3.6 %all-to-all-start.1 = ((bf16[4,128,2048]{2,1,0:T(8,128)(2,1)}), bf16[4,128,2048]{2,1,0:T(8,128)(2,1)S(1)}, u32[]{:S(2)}, u32[]{:S(2)}) async-start(bf16[4,128,2048]{2,1,0:T(8,128)(2,1)} %tile.5), calls=%async_computation.1 | async-start | bytes 4194304 | tf_op jit(solution)/shard_map/all_to_all | solution.py:46
  38.2 2.6 %collective-permute-start.7 = (bf16[64,2048]{1,0:T(8,128)(2,1)S(1)}, bf16[64,2048]{1,0:T(8,128)(2,1)S(1)}, u32[]{:S(2)}, u32[]{:S(2)}) collective-permute-start(bf16[64,2048]{1,0:T(8,128)(2,1)S(1)} %collective-permute-done.5.refs_1_), channel_id=1, source_target_pairs={{4,0},{5,1},{6,2},{7,3},{8,4},{9,5},{10,6},{11,7},{12,8},{13,9},{1... | collective-permute-start | bytes 786440 | tf_op jit(solution)/shard_map/ppermute | solution.py:69
  40.8 2.1 collective-permute-start.13
  42.8 2.8 %collective-permute-done.9.refs_7_ = bf16[64,2048]{1,0:T(8,128)(2,1)S(1)} collective-permute-done((bf16[64,2048]{1,0:T(8,128)(2,1)S(1)}, bf16[64,2048]{1,0:T(8,128)(2,1)S(1)}, u32[]{:S(2)}, u32[]{:S(2)}) %collective-permute-start.9) | collective-permute-done | bytes 262176 | tf_op jit(solution)/shard_map/ppermute | solution.py:68
  46.3 2.1 collective-permute-start.8
  48.4 3.9 %collective-permute-done.10.refs_6_ = bf16[64,2048]{1,0:T(8,128)(2,1)S(1)} collective-permute-done((bf16[64,2048]{1,0:T(8,128)(2,1)S(1)}, bf16[64,2048]{1,0:T(8,128)(2,1)S(1)}, u32[]{:S(2)}, u32[]{:S(2)}) %collective-permute-start.10) | collective-permute-done | bytes 262176 | tf_op jit(solution)/shard_map/ppermute | solution.py:68
  53.7 2.7 %collective-permute-start.12 = (bf16[32,2048]{1,0:T(8,128)(2,1)}, bf16[32,2048]{1,0:T(8,128)(2,1)}, u32[]{:S(2)}, u32[]{:S(2)}) collective-permute-start(bf16[32,2048]{1,0:T(8,128)(2,1)} %slice.33), channel_id=1, source_target_pairs={{4,0},{5,1},{6,2},{7,3},{8,4},{9,5},{10,6},{11,7},{12,8},{13,9},{1... | collective-permute-start | bytes 393224 | tf_op jit(solution)/shard_map/ppermute | solution.py:71
  56.4 2.1 collective-permute-done.11.refs_4_
  58.6 4.1 %all-to-all-done.1 = bf16[4,128,2048]{2,1,0:T(8,128)(2,1)S(1)} async-done(((bf16[4,128,2048]{2,1,0:T(8,128)(2,1)}), bf16[4,128,2048]{2,1,0:T(8,128)(2,1)S(1)}, u32[]{:S(2)}, u32[]{:S(2)}) %all-to-all-start.1) | async-done | bytes 2097184 | tf_op jit(solution)/shard_map/all_to_all | solution.py:46
  62.7 7.4 %shard_map.93 = (bf16[512,1536]{1,0:T(8,128)(2,1)}, bf16[512,1024]{1,0:T(8,128)(2,1)}) custom-call(s32[3]{0:T(128)S(1)} %pad_add_fusion.index, bf16[512,2048]{1,0:T(8,128)(2,1)S(1)} %bitcast.9, bf16[64,2048]{1,0:T(8,128)(2,1)S(1)} %pad_maximum_fusion.3.refs_0_, bf16[64,2048]{1,0:T(8,128)(2,1)S(1)} %collective-permute-done.5.refs_1_, ...), custom_call_target="tpu_custom_call" | custom-call | flops 3221225472 | bytes 10485760 | tf_op jit(solution)/shard_map/pallas_call | solution.py:148
  70.1 4.3 %all-to-all-start.2 = ((bf16[4,128,1536]{2,1,0:T(8,128)(2,1)}), bf16[4,128,1536]{2,1,0:T(8,128)(2,1)}, u32[]{:S(2)}, u32[]{:S(2)}) async-start(bf16[4,128,1536]{2,1,0:T(8,128)(2,1)} %bitcast.16), calls=%async_computation.2 | async-start | bytes 3145728 | tf_op jit(solution)/shard_map/all_to_all | solution.py:46
  74.4 5.6 %shard_map.92 = (bf16[128,768]{1,0:T(8,128)(2,1)}, bf16[128,768]{1,0:T(8,128)(2,1)}, bf16[128,768]{1,0:T(8,128)(2,1)}, bf16[128,768]{1,0:T(8,128)(2,1)}, bf16[512,1024]{1,0:T(8,128)(2,1)}) custom-call(s32[3]{0:T(128)S(1)} %pad_add_fusion.index, bf16[512,2048]{1,0:T(8,128)(2,1)S(1)} %bitcast.10, bf16[64,2048]{1,0:T(8,128)(2,1)S(1)} %pad_maximum_fusion.3.refs_0_, ...), custom_call_target="tpu_custom_call" | custom-call | flops 1610612736 | bytes 10485760 | tf_op jit(solution)/shard_map/pallas_call | solution.py:184
  80.1 1.4 collective-permute-start.14
  81.5 2.4 %collective-permute-start.15 = (bf16[128,768]{1,0:T(8,128)(2,1)}, bf16[128,768]{1,0:T(8,128)(2,1)S(1)}, u32[]{:S(2)}, u32[]{:S(2)}) collective-permute-start(bf16[128,768]{1,0:T(8,128)(2,1)} %get-tuple-element.36), channel_id=1, source_target_pairs={{0,128},{32,160},{64,192},{96,224},{128,0},{160,32},{192,64},{224,... | collective-permute-start | bytes 589832 | tf_op jit(solution)/shard_map/ppermute | solution.py:433
  83.9 1.2 collective-permute-start.16
  85.1 7.7 %all-to-all-done.2.terms = bf16[4,128,1536]{2,1,0:T(8,128)(2,1)} async-done(((bf16[4,128,1536]{2,1,0:T(8,128)(2,1)}), bf16[4,128,1536]{2,1,0:T(8,128)(2,1)}, u32[]{:S(2)}, u32[]{:S(2)}) %all-to-all-start.2) | async-done | bytes 1572896 | tf_op jit(solution)/shard_map/all_to_all | solution.py:46
  92.7 2.5 %shard_map.94 = (f32[128,1536]{1,0:T(8,128)}, bf16[128,768]{1,0:T(8,128)(2,1)S(1)}) custom-call(s32[1]{0:T(128)} %bitcast.2.index, bf16[4,128,1536]{2,1,0:T(8,128)(2,1)} %all-to-all-done.2.terms), custom_call_target="tpu_custom_call" | custom-call | flops 3145728 | bytes 10485760 | tf_op jit(solution)/shard_map/pallas_call | solution.py:282
  95.5 1.8 collective-permute-start.20
  97.9 2.9 %collective-permute-done.15.refs_2_ = bf16[128,768]{1,0:T(8,128)(2,1)S(1)} collective-permute-done((bf16[128,768]{1,0:T(8,128)(2,1)}, bf16[128,768]{1,0:T(8,128)(2,1)S(1)}, u32[]{:S(2)}, u32[]{:S(2)}) %collective-permute-start.15) | collective-permute-done | bytes 196640 | tf_op jit(solution)/shard_map/ppermute | solution.py:433
  100.8 1.5 shard_map.95.refs_0_
  102.3 2.3 %collective-permute-done.21.refs_3_ = bf16[128,768]{1,0:T(8,128)(2,1)S(1)} collective-permute-done((bf16[128,768]{1,0:T(8,128)(2,1)S(1)}, bf16[128,768]{1,0:T(8,128)(2,1)S(1)}, u32[]{:S(2)}, u32[]{:S(2)}) %collective-permute-start.21) | collective-permute-done | bytes 196640 | tf_op jit(solution)/shard_map/ppermute | solution.py:61
  104.6 4.6 %collective-permute-done.20.refs_2_ = bf16[128,768]{1,0:T(8,128)(2,1)S(1)} collective-permute-done((bf16[128,768]{1,0:T(8,128)(2,1)S(1)}, bf16[128,768]{1,0:T(8,128)(2,1)S(1)}, u32[]{:S(2)}, u32[]{:S(2)}) %collective-permute-start.20) | collective-permute-done | bytes 196640 | tf_op jit(solution)/shard_map/ppermute | solution.py:61
  109.2 5.2 %shard_map.96 = (bf16[512,2048]{1,0:T(8,128)(2,1)}, bf16[512,768]{1,0:T(8,128)(2,1)}) custom-call(s32[1]{0:T(128)} %bitcast.2.index, bf16[128,768]{1,0:T(8,128)(2,1)S(1)} %get-tuple-element.41.refs_0_, bf16[128,768]{1,0:T(8,128)(2,1)S(1)} %collective-permute-done.19.refs_1_, bf16[128,768]{1,0:T(8,128)(2,1)S(1)} %collective-permute-done.20.refs_2_, ...), custom_call_target="tpu_custom_call" | custom-call | flops 1610612736 | bytes 10485760 | tf_op jit(solution)/shard_map/pallas_call | solution.py:217
  114.4 4.4 %all-to-all-start.3 = ((bf16[4,128,2048]{2,1,0:T(8,128)(2,1)}), bf16[4,128,2048]{2,1,0:T(8,128)(2,1)}, u32[]{:S(2)}, u32[]{:S(2)}) async-start(bf16[4,128,2048]{2,1,0:T(8,128)(2,1)} %bitcast.14), calls=%async_computation.3 | async-start | bytes 4194304 | tf_op jit(solution)/shard_map/all_to_all | solution.py:46
  119.0 1.3 collective-permute-start.30
  120.2 2.0 collective-permute-start.29
  122.2 4.3 %collective-permute-start.24 = (bf16[512,1024]{1,0:T(8,128)(2,1)}, bf16[512,1024]{1,0:T(8,128)(2,1)}, u32[]{:S(2)}, u32[]{:S(2)}) collective-permute-start(bf16[512,1024]{1,0:T(8,128)(2,1)} %get-tuple-element.46), channel_id=1, source_target_pairs={{0,32},{32,0},{64,96},{96,64},{128,160},{160,128},{192,224},{224,1... | collective-permute-start | bytes 3145736 | tf_op jit(solution)/shard_map/ppermute | solution.py:41
  126.5 5.4 %collective-permute-done.31.refs_3_ = bf16[128,1536]{1,0:T(8,128)(2,1)S(1)} collective-permute-done((bf16[128,1536]{1,0:T(8,128)(2,1)S(1)}, bf16[128,1536]{1,0:T(8,128)(2,1)S(1)}, u32[]{:S(2)}, u32[]{:S(2)}) %collective-permute-start.31) | collective-permute-done | bytes 393248 | tf_op jit(solution)/shard_map/ppermute | solution.py:61
  131.9 0.9 collective-permute-done.30.refs_2_
  132.8 6.0 %collective-permute-done.29.refs_1_ = bf16[128,1536]{1,0:T(8,128)(2,1)S(1)} collective-permute-done((bf16[128,1536]{1,0:T(8,128)(2,1)S(1)}, bf16[128,1536]{1,0:T(8,128)(2,1)S(1)}, u32[]{:S(2)}, u32[]{:S(2)}) %collective-permute-start.29) | collective-permute-done | bytes 393248 | tf_op jit(solution)/shard_map/ppermute | solution.py:61
  138.8 7.2 %shard_map.99 = (bf16[512,2048]{1,0:T(8,128)(2,1)}, bf16[512,768]{1,0:T(8,128)(2,1)}, bf16[512,768]{1,0:T(8,128)(2,1)}) custom-call(s32[1]{0:T(128)} %bitcast.2.index, bf16[128,1536]{1,0:T(8,128)(2,1)S(1)} %shard_map.95.refs_0_, bf16[128,1536]{1,0:T(8,128)(2,1)S(1)} %collective-permute-done.29.refs_1_, ...), custom_call_target="tpu_custom_call" | custom-call | flops 3221225472 | bytes 10485760 | tf_op jit(solution)/shard_map/pallas_call | solution.py:253
  146.0 4.7 %all-to-all-start.4 = ((bf16[4,128,2048]{2,1,0:T(8,128)(2,1)}), bf16[4,128,2048]{2,1,0:T(8,128)(2,1)}, u32[]{:S(2)}, u32[]{:S(2)}) async-start(bf16[4,128,2048]{2,1,0:T(8,128)(2,1)} %bitcast.13), calls=%async_computation.4 | async-start | bytes 4194304 | tf_op jit(solution)/shard_map/all_to_all | solution.py:46
  150.7 1.2 fusion.19
  151.9 2.5 %shard_map.97 = (bf16[64,2048]{1,0:T(8,128)(2,1)S(1)}, bf16[64,2048]{1,0:T(8,128)(2,1)S(1)}) custom-call(s32[3]{0:T(128)S(1)} %pad_add_fusion.index, bf16[4,128,2048]{2,1,0:T(8,128)(2,1)} %all-to-all-done.3.terms), custom_call_target="tpu_custom_call" | custom-call | flops 2097152 | bytes 10485760 | tf_op jit(solution)/shard_map/pallas_call | solution.py:360
  154.4 1.9 collective-permute-start.22
  156.3 4.5 %fusion.4 = bf16[768,1024]{1,0:T(8,128)(2,1)} fusion(bf16[512,1024]{1,0:T(8,128)(2,1)} %collective-permute-done.24, bf16[512,1024]{1,0:T(8,128)(2,1)S(1)} %get-tuple-element.62, bf16[512,768]{1,0:T(8,128)(2,1)} %collective-permute-done.23, bf16[512,768]{1,0:T(8,128)(2,1)S(1)} %copy-done.5), kind=kOutput, calls=%fused_computation.5 | convolution fusion | flops 1618739200 | bytes 5242880 | tf_op jit(solution)/shard_map/dot_general | solution.py:37
  160.8 3.4 %collective-permute-done.22.far = bf16[64,2048]{1,0:T(8,128)(2,1)S(1)} collective-permute-done((bf16[64,2048]{1,0:T(8,128)(2,1)S(1)}, bf16[64,2048]{1,0:T(8,128)(2,1)S(1)}, u32[]{:S(2)}, u32[]{:S(2)}) %collective-permute-start.22) | collective-permute-done | bytes 262176 | tf_op jit(solution)/shard_map/ppermute | solution.py:455
  164.8 2.8 %collective-permute-start.25 = (bf16[16,2048]{1,0:T(8,128)(2,1)S(1)}, bf16[16,2048]{1,0:T(8,128)(2,1)S(1)}, u32[]{:S(2)}, u32[]{:S(2)}) collective-permute-start(bf16[16,2048]{1,0:T(8,128)(2,1)S(1)} %get-tuple-element.49), channel_id=1, source_target_pairs={{0,28},{1,29},{2,30},{3,31},{4,0},{5,1},{6,2},{7,3},{8,4},{9,5},{1... | collective-permute-start | bytes 196616 | tf_op jit(solution)/shard_map/ppermute | solution.py:459
  167.6 4.3 %collective-permute-start.26 = (bf16[16,2048]{1,0:T(8,128)(2,1)S(1)}, bf16[16,2048]{1,0:T(8,128)(2,1)S(1)}, u32[]{:S(2)}, u32[]{:S(2)}) collective-permute-start(bf16[16,2048]{1,0:T(8,128)(2,1)S(1)} %get-tuple-element.50), channel_id=1, source_target_pairs={{0,4},{1,5},{2,6},{3,7},{4,8},{5,9},{6,10},{7,11},{8,12},{9,13},{1... | collective-permute-start | bytes 196616 | tf_op jit(solution)/shard_map/ppermute | solution.py:459
  171.9 4.6 %collective-permute-start.27 = (bf16[16,2048]{1,0:T(8,128)(2,1)S(1)}, bf16[16,2048]{1,0:T(8,128)(2,1)S(1)}, u32[]{:S(2)}, u32[]{:S(2)}) collective-permute-start(bf16[16,2048]{1,0:T(8,128)(2,1)S(1)} %get-tuple-element.51), channel_id=1, source_target_pairs={{0,8},{1,9},{2,10},{3,11},{4,12},{5,13},{6,14},{7,15},{8,16},{9,17... | collective-permute-start | bytes 196616 | tf_op jit(solution)/shard_map/ppermute | solution.py:459
  176.5 1.3 collective-permute-start.32
  178.5 3.9 %collective-permute-start.28 = (bf16[16,1024]{1,0:T(8,128)(2,1)S(1)}, bf16[16,1024]{1,0:T(8,128)(2,1)S(1)}, u32[]{:S(2)}, u32[]{:S(2)}) collective-permute-start(bf16[16,1024]{1,0:T(8,128)(2,1)S(1)} %slice.36), channel_id=1, source_target_pairs={{0,32},{32,0},{64,96},{96,64},{128,160},{160,128},{192,224},{224,1... | collective-permute-start | bytes 98312 | tf_op jit(solution)/shard_map/ppermute | solution.py:41
  182.4 0.8 collective-permute-done.28
  183.8 2.7 %shard_map.100 = bf16[128,2048]{1,0:T(8,128)(2,1)} custom-call(s32[1]{0:T(128)} %bitcast.2.index, bf16[4,128,2048]{2,1,0:T(8,128)(2,1)} %all-to-all-done.4.terms), custom_call_target="tpu_custom_call" | custom-call | flops 2097152 | bytes 10485760 | tf_op jit(solution)/shard_map/pallas_call | solution.py:338
  186.5 5.2 %all-to-all-start.5 = ((bf16[8,16,2048]{2,1,0:T(8,128)(2,1)}), bf16[8,16,2048]{2,1,0:T(8,128)(2,1)S(1)}, u32[]{:S(2)}, u32[]{:S(2)}) async-start(bf16[8,16,2048]{2,1,0:T(8,128)(2,1)} %bitcast.15), calls=%async_computation.5 | async-start | bytes 1048576 | tf_op jit(solution)/shard_map/all_to_all | solution.py:46
  191.7 4.5 %convolution_convert_fusion.1 = bf16[1024,768]{1,0:T(8,128)(2,1)} fusion(bf16[512,768]{1,0:T(8,128)(2,1)S(1)} %collective-permute-done.33, bf16[512,768]{1,0:T(8,128)(2,1)} %get-tuple-element.58, bf16[512,1024]{1,0:T(8,128)(2,1)} %collective-permute-done.32, bf16[512,1024]{1,0:T(8,128)(2,1)S(1)} %copy-done), kind=kOutput, calls=%fused_computation.7 | convolution fusion | flops 1618739200 | bytes 5242880 | tf_op jit(solution)/shard_map/dot_general | solution.py:37
  196.3 4.5 %convolution_convert_fusion = bf16[1024,768]{1,0:T(8,128)(2,1)} fusion(bf16[512,768]{1,0:T(8,128)(2,1)} %collective-permute-done.34, bf16[512,768]{1,0:T(8,128)(2,1)S(1)} %copy-done.4, bf16[512,1024]{1,0:T(8,128)(2,1)} %collective-permute-done.32, bf16[512,1024]{1,0:T(8,128)(2,1)S(1)} %copy-done), kind=kOutput, calls=%fused_computation.6 | convolution fusion | flops 1618739200 | bytes 5242880 | tf_op jit(solution)/shard_map/dot_general | solution.py:37
  200.7 8.9 %all-to-all-done.5 = bf16[8,16,2048]{2,1,0:T(8,128)(2,1)S(1)} async-done(((bf16[8,16,2048]{2,1,0:T(8,128)(2,1)}), bf16[8,16,2048]{2,1,0:T(8,128)(2,1)S(1)}, u32[]{:S(2)}, u32[]{:S(2)}) %all-to-all-start.5) | async-done | bytes 524320 | tf_op jit(solution)/shard_map/all_to_all | solution.py:46
  210.3 0.9 collective-permute-done.35
  (64 shorter events, 7.2 us)
Async XLA Ops:
  3.1 29.7 %all-to-all-start = ((bf16[8,16,2048]{2,1,0:T(8,128)(2,1)}), bf16[8,16,2048]{2,1,0:T(8,128)(2,1)S(1)}, u32[]{:S(2)}, u32[]{:S(2)}) async-start(bf16[8,16,2048]{2,1,0:T(8,128)(2,1)} %tile.4), calls=%async_computation | async-start | bytes 1048576 | tf_op jit(solution)/shard_map/all_to_all | solution.py:46
  12.1 1.8 collective-permute-start
  13.0 1.2 collective-permute-start.1
  14.3 5.0 %collective-permute-start.4 = (bf16[16,2048]{1,0:T(8,128)(2,1)S(1)}, bf16[16,2048]{1,0:T(8,128)(2,1)S(1)}, u32[]{:S(2)}, u32[]{:S(2)}) collective-permute-start(bf16[16,2048]{1,0:T(8,128)(2,1)S(1)} %constant_dynamic-update-slice_fusion), channel_id=1, source_target_pairs={{0,1},{1,2},{2,3},{3,0},{4,5},{5,6},{6,7},{7,4},{8,9},{9,10},{10,1... | collective-permute-start | bytes 196616 | tf_op jit(solution)/shard_map/ppermute | solution.py:61
  15.6 6.1 %collective-permute-start.3 = (bf16[16,2048]{1,0:T(8,128)(2,1)S(1)}, bf16[16,2048]{1,0:T(8,128)(2,1)S(1)}, u32[]{:S(2)}, u32[]{:S(2)}) collective-permute-start(bf16[16,2048]{1,0:T(8,128)(2,1)S(1)} %constant_dynamic-update-slice_fusion), channel_id=1, source_target_pairs={{0,2},{1,3},{2,0},{3,1},{4,6},{5,7},{6,4},{7,5},{8,10},{9,11},{10,... | collective-permute-start | bytes 196616 | tf_op jit(solution)/shard_map/ppermute | solution.py:61
  18.2 3.5 %collective-permute-start.2 = (bf16[16,2048]{1,0:T(8,128)(2,1)S(1)}, bf16[16,2048]{1,0:T(8,128)(2,1)S(1)}, u32[]{:S(2)}, u32[]{:S(2)}) collective-permute-start(bf16[16,2048]{1,0:T(8,128)(2,1)S(1)} %constant_dynamic-update-slice_fusion), channel_id=1, source_target_pairs={{0,3},{1,0},{2,1},{3,2},{4,7},{5,4},{6,5},{7,6},{8,11},{9,8},{10,9... | collective-permute-start | bytes 196616 | tf_op jit(solution)/shard_map/ppermute | solution.py:61
  21.7 11.1 %collective-permute-start.6 = (bf16[64,2048]{1,0:T(8,128)(2,1)S(1)}, bf16[64,2048]{1,0:T(8,128)(2,1)S(1)}, u32[]{:S(2)}, u32[]{:S(2)}) collective-permute-start(bf16[64,2048]{1,0:T(8,128)(2,1)S(1)} %pad_maximum_fusion.3.refs_0_), channel_id=1, source_target_pairs={{0,4},{1,5},{2,6},{3,7},{4,8},{5,9},{6,10},{7,11},{8,12},{9,13},{1... | collective-permute-start | bytes 786440 | tf_op jit(solution)/shard_map/ppermute | solution.py:68
  23.5 9.3 %collective-permute-start.5 = (bf16[64,2048]{1,0:T(8,128)(2,1)S(1)}, bf16[64,2048]{1,0:T(8,128)(2,1)S(1)}, u32[]{:S(2)}, u32[]{:S(2)}) collective-permute-start(bf16[64,2048]{1,0:T(8,128)(2,1)S(1)} %pad_maximum_fusion.3.refs_0_), channel_id=1, source_target_pairs={{4,0},{5,1},{6,2},{7,3},{8,4},{9,5},{10,6},{11,7},{12,8},{13,9},{1... | collective-permute-start | bytes 786440 | tf_op jit(solution)/shard_map/ppermute | solution.py:69
  24.8 33.8 %collective-permute-start.17 = (bf16[1024,768]{1,0:T(8,128)(2,1)}, bf16[1024,768]{1,0:T(8,128)(2,1)}, u32[]{:S(2)}, u32[]{:S(2)}) collective-permute-start(bf16[1024,768]{1,0:T(8,128)(2,1)} %refs_4_.3), channel_id=1, source_target_pairs={{0,32},{32,0},{64,96},{96,64},{128,160},{160,128},{192,224},{224,1... | collective-permute-start | bytes 4718600 | tf_op jit(solution)/shard_map/ppermute | solution.py:41
  26.6 32.0 %collective-permute-start.18 = (bf16[1024,768]{1,0:T(8,128)(2,1)}, bf16[1024,768]{1,0:T(8,128)(2,1)}, u32[]{:S(2)}, u32[]{:S(2)}) collective-permute-start(bf16[1024,768]{1,0:T(8,128)(2,1)} %refs_5_.1), channel_id=1, source_target_pairs={{0,32},{32,0},{64,96},{96,64},{128,160},{160,128},{192,224},{224,1... | collective-permute-start | bytes 4718600 | tf_op jit(solution)/shard_map/ppermute | solution.py:41
  34.4 28.3 %all-to-all-start.1 = ((bf16[4,128,2048]{2,1,0:T(8,128)(2,1)}), bf16[4,128,2048]{2,1,0:T(8,128)(2,1)S(1)}, u32[]{:S(2)}, u32[]{:S(2)}) async-start(bf16[4,128,2048]{2,1,0:T(8,128)(2,1)} %tile.5), calls=%async_computation.1 | async-start | bytes 4194304 | tf_op jit(solution)/shard_map/all_to_all | solution.py:46
  38.0 7.6 %collective-permute-start.9 = (bf16[64,2048]{1,0:T(8,128)(2,1)S(1)}, bf16[64,2048]{1,0:T(8,128)(2,1)S(1)}, u32[]{:S(2)}, u32[]{:S(2)}) collective-permute-start(bf16[64,2048]{1,0:T(8,128)(2,1)S(1)} %collective-permute-done.6.refs_8_), channel_id=1, source_target_pairs={{0,4},{1,5},{2,6},{3,7},{4,8},{5,9},{6,10},{7,11},{8,12},{9,13},{1... | collective-permute-start | bytes 786440 | tf_op jit(solution)/shard_map/ppermute | solution.py:68
  38.2 7.4 %collective-permute-start.7 = (bf16[64,2048]{1,0:T(8,128)(2,1)S(1)}, bf16[64,2048]{1,0:T(8,128)(2,1)S(1)}, u32[]{:S(2)}, u32[]{:S(2)}) collective-permute-start(bf16[64,2048]{1,0:T(8,128)(2,1)S(1)} %collective-permute-done.5.refs_1_), channel_id=1, source_target_pairs={{4,0},{5,1},{6,2},{7,3},{8,4},{9,5},{10,6},{11,7},{12,8},{13,9},{1... | collective-permute-start | bytes 786440 | tf_op jit(solution)/shard_map/ppermute | solution.py:69
  40.8 33.7 %collective-permute-start.13 = (bf16[768,1024]{1,0:T(8,128)(2,1)}, bf16[768,1024]{1,0:T(8,128)(2,1)}, u32[]{:S(2)}, u32[]{:S(2)}) collective-permute-start(bf16[768,1024]{1,0:T(8,128)(2,1)} %refs_4_.2), channel_id=1, source_target_pairs={{0,32},{32,0},{64,96},{96,64},{128,160},{160,128},{192,224},{224,1... | collective-permute-start | bytes 4718600 | tf_op jit(solution)/shard_map/ppermute | solution.py:41
  45.6 0.7 copy-start.1
  45.6 6.7 %collective-permute-start.10 = (bf16[64,2048]{1,0:T(8,128)(2,1)S(1)}, bf16[64,2048]{1,0:T(8,128)(2,1)S(1)}, u32[]{:S(2)}, u32[]{:S(2)}) collective-permute-start(bf16[64,2048]{1,0:T(8,128)(2,1)S(1)} %collective-permute-done.9.refs_7_), channel_id=1, source_target_pairs={{0,4},{1,5},{2,6},{3,7},{4,8},{5,9},{6,10},{7,11},{8,12},{9,13},{1... | collective-permute-start | bytes 786440 | tf_op jit(solution)/shard_map/ppermute | solution.py:68
  46.3 6.7 %copy-start.2 = (bf16[64,2048]{1,0:T(8,128)(2,1)}, bf16[64,2048]{1,0:T(8,128)(2,1)S(1)}, u32[]{:S(2)}) copy-start(bf16[64,2048]{1,0:T(8,128)(2,1)S(1)} %collective-permute-done.7.refs_2_) | copy-start | bytes 786436
  46.3 6.7 %collective-permute-start.8 = (bf16[64,2048]{1,0:T(8,128)(2,1)S(1)}, bf16[64,2048]{1,0:T(8,128)(2,1)S(1)}, u32[]{:S(2)}, u32[]{:S(2)}) collective-permute-start(bf16[64,2048]{1,0:T(8,128)(2,1)S(1)} %collective-permute-done.7.refs_2_), channel_id=1, source_target_pairs={{4,0},{5,1},{6,2},{7,3},{8,4},{9,5},{10,6},{11,7},{12,8},{13,9},{1... | collective-permute-start | bytes 786440 | tf_op jit(solution)/shard_map/ppermute | solution.py:69
  53.0 5.5 %collective-permute-start.11 = (bf16[32,2048]{1,0:T(8,128)(2,1)}, bf16[32,2048]{1,0:T(8,128)(2,1)S(1)}, u32[]{:S(2)}, u32[]{:S(2)}) collective-permute-start(bf16[32,2048]{1,0:T(8,128)(2,1)} %slice.32), channel_id=1, source_target_pairs={{0,4},{1,5},{2,6},{3,7},{4,8},{5,9},{6,10},{7,11},{8,12},{9,13},{1... | collective-permute-start | bytes 393224 | tf_op jit(solution)/shard_map/ppermute | solution.py:70
  53.7 4.9 %collective-permute-start.12 = (bf16[32,2048]{1,0:T(8,128)(2,1)}, bf16[32,2048]{1,0:T(8,128)(2,1)}, u32[]{:S(2)}, u32[]{:S(2)}) collective-permute-start(bf16[32,2048]{1,0:T(8,128)(2,1)} %slice.33), channel_id=1, source_target_pairs={{4,0},{5,1},{6,2},{7,3},{8,4},{9,5},{10,6},{11,7},{12,8},{13,9},{1... | collective-permute-start | bytes 393224 | tf_op jit(solution)/shard_map/ppermute | solution.py:71
  70.1 22.7 %all-to-all-start.2 = ((bf16[4,128,1536]{2,1,0:T(8,128)(2,1)}), bf16[4,128,1536]{2,1,0:T(8,128)(2,1)}, u32[]{:S(2)}, u32[]{:S(2)}) async-start(bf16[4,128,1536]{2,1,0:T(8,128)(2,1)} %bitcast.16), calls=%async_computation.2 | async-start | bytes 3145728 | tf_op jit(solution)/shard_map/all_to_all | solution.py:46
  80.1 17.2 %collective-permute-start.14 = (bf16[128,768]{1,0:T(8,128)(2,1)}, bf16[128,768]{1,0:T(8,128)(2,1)S(1)}, u32[]{:S(2)}, u32[]{:S(2)}) collective-permute-start(bf16[128,768]{1,0:T(8,128)(2,1)} %get-tuple-element.35), channel_id=1, source_target_pairs={{0,64},{32,96},{64,128},{96,160},{128,192},{160,224},{192,0},{224,... | collective-permute-start | bytes 589832 | tf_op jit(solution)/shard_map/ppermute | solution.py:433
  81.5 19.3 %collective-permute-start.15 = (bf16[128,768]{1,0:T(8,128)(2,1)}, bf16[128,768]{1,0:T(8,128)(2,1)S(1)}, u32[]{:S(2)}, u32[]{:S(2)}) collective-permute-start(bf16[128,768]{1,0:T(8,128)(2,1)} %get-tuple-element.36), channel_id=1, source_target_pairs={{0,128},{32,160},{64,192},{96,224},{128,0},{160,32},{192,64},{224,... | collective-permute-start | bytes 589832 | tf_op jit(solution)/shard_map/ppermute | solution.py:433
  83.9 16.9 %collective-permute-start.16 = (bf16[128,768]{1,0:T(8,128)(2,1)}, bf16[128,768]{1,0:T(8,128)(2,1)S(1)}, u32[]{:S(2)}, u32[]{:S(2)}) collective-permute-start(bf16[128,768]{1,0:T(8,128)(2,1)} %get-tuple-element.37), channel_id=1, source_target_pairs={{0,192},{32,224},{64,0},{96,32},{128,64},{160,96},{192,128},{224,1... | collective-permute-start | bytes 589832 | tf_op jit(solution)/shard_map/ppermute | solution.py:433
  95.2 9.4 %collective-permute-start.21 = (bf16[128,768]{1,0:T(8,128)(2,1)S(1)}, bf16[128,768]{1,0:T(8,128)(2,1)S(1)}, u32[]{:S(2)}, u32[]{:S(2)}) collective-permute-start(bf16[128,768]{1,0:T(8,128)(2,1)S(1)} %get-tuple-element.41.refs_0_), channel_id=1, source_target_pairs={{0,64},{32,96},{64,128},{96,160},{128,192},{160,224},{192,0},{224,... | collective-permute-start | bytes 589832 | tf_op jit(solution)/shard_map/ppermute | solution.py:61
  95.5 13.7 %collective-permute-start.20 = (bf16[128,768]{1,0:T(8,128)(2,1)S(1)}, bf16[128,768]{1,0:T(8,128)(2,1)S(1)}, u32[]{:S(2)}, u32[]{:S(2)}) collective-permute-start(bf16[128,768]{1,0:T(8,128)(2,1)S(1)} %get-tuple-element.41.refs_0_), channel_id=1, source_target_pairs={{0,128},{32,160},{64,192},{96,224},{128,0},{160,32},{192,64},{224,... | collective-permute-start | bytes 589832 | tf_op jit(solution)/shard_map/ppermute | solution.py:61
  97.3 11.9 %collective-permute-start.19 = (bf16[128,768]{1,0:T(8,128)(2,1)S(1)}, bf16[128,768]{1,0:T(8,128)(2,1)S(1)}, u32[]{:S(2)}, u32[]{:S(2)}) collective-permute-start(bf16[128,768]{1,0:T(8,128)(2,1)S(1)} %get-tuple-element.41.refs_0_), channel_id=1, source_target_pairs={{0,192},{32,224},{64,0},{96,32},{128,64},{160,96},{192,128},{224,1... | collective-permute-start | bytes 589832 | tf_op jit(solution)/shard_map/ppermute | solution.py:61
  114.4 31.6 %all-to-all-start.3 = ((bf16[4,128,2048]{2,1,0:T(8,128)(2,1)}), bf16[4,128,2048]{2,1,0:T(8,128)(2,1)}, u32[]{:S(2)}, u32[]{:S(2)}) async-start(bf16[4,128,2048]{2,1,0:T(8,128)(2,1)} %bitcast.14), calls=%async_computation.3 | async-start | bytes 4194304 | tf_op jit(solution)/shard_map/all_to_all | solution.py:46
  118.9 13.0 %collective-permute-start.31 = (bf16[128,1536]{1,0:T(8,128)(2,1)S(1)}, bf16[128,1536]{1,0:T(8,128)(2,1)S(1)}, u32[]{:S(2)}, u32[]{:S(2)}) collective-permute-start(bf16[128,1536]{1,0:T(8,128)(2,1)S(1)} %shard_map.95.refs_0_), channel_id=1, source_target_pairs={{0,64},{32,96},{64,128},{96,160},{128,192},{160,224},{192,0},{224,... | collective-permute-start | bytes 1179656 | tf_op jit(solution)/shard_map/ppermute | solution.py:61
  119.0 13.8 %collective-permute-start.30 = (bf16[128,1536]{1,0:T(8,128)(2,1)S(1)}, bf16[128,1536]{1,0:T(8,128)(2,1)S(1)}, u32[]{:S(2)}, u32[]{:S(2)}) collective-permute-start(bf16[128,1536]{1,0:T(8,128)(2,1)S(1)} %shard_map.95.refs_0_), channel_id=1, source_target_pairs={{0,128},{32,160},{64,192},{96,224},{128,0},{160,32},{192,64},{224,... | collective-permute-start | bytes 1179656 | tf_op jit(solution)/shard_map/ppermute | solution.py:61
  120.2 18.5 %collective-permute-start.29 = (bf16[128,1536]{1,0:T(8,128)(2,1)S(1)}, bf16[128,1536]{1,0:T(8,128)(2,1)S(1)}, u32[]{:S(2)}, u32[]{:S(2)}) collective-permute-start(bf16[128,1536]{1,0:T(8,128)(2,1)S(1)} %shard_map.95.refs_0_), channel_id=1, source_target_pairs={{0,192},{32,224},{64,0},{96,32},{128,64},{160,96},{192,128},{224,1... | collective-permute-start | bytes 1179656 | tf_op jit(solution)/shard_map/ppermute | solution.py:61
  122.2 34.1 %collective-permute-start.24 = (bf16[512,1024]{1,0:T(8,128)(2,1)}, bf16[512,1024]{1,0:T(8,128)(2,1)}, u32[]{:S(2)}, u32[]{:S(2)}) collective-permute-start(bf16[512,1024]{1,0:T(8,128)(2,1)} %get-tuple-element.46), channel_id=1, source_target_pairs={{0,32},{32,0},{64,96},{96,64},{128,160},{160,128},{192,224},{224,1... | collective-permute-start | bytes 3145736 | tf_op jit(solution)/shard_map/ppermute | solution.py:41
  126.5 29.8 %collective-permute-start.23 = (bf16[512,768]{1,0:T(8,128)(2,1)}, bf16[512,768]{1,0:T(8,128)(2,1)}, u32[]{:S(2)}, u32[]{:S(2)}) collective-permute-start(bf16[512,768]{1,0:T(8,128)(2,1)} %get-tuple-element.45), channel_id=1, source_target_pairs={{0,32},{32,0},{64,96},{96,64},{128,160},{160,128},{192,224},{224,1... | collective-permute-start | bytes 2359304 | tf_op jit(solution)/shard_map/ppermute | solution.py:41
  146.0 37.8 %all-to-all-start.4 = ((bf16[4,128,2048]{2,1,0:T(8,128)(2,1)}), bf16[4,128,2048]{2,1,0:T(8,128)(2,1)}, u32[]{:S(2)}, u32[]{:S(2)}) async-start(bf16[4,128,2048]{2,1,0:T(8,128)(2,1)} %bitcast.13), calls=%async_computation.4 | async-start | bytes 4194304 | tf_op jit(solution)/shard_map/all_to_all | solution.py:46
  151.9 4.4 %copy-start.5 = (bf16[512,768]{1,0:T(8,128)(2,1)S(1)}, bf16[512,768]{1,0:T(8,128)(2,1)}, u32[]{:S(2)}) copy-start(bf16[512,768]{1,0:T(8,128)(2,1)} %get-tuple-element.45) | copy-start | bytes 2359300
  154.4 9.8 %collective-permute-start.22 = (bf16[64,2048]{1,0:T(8,128)(2,1)S(1)}, bf16[64,2048]{1,0:T(8,128)(2,1)S(1)}, u32[]{:S(2)}, u32[]{:S(2)}) collective-permute-start(bf16[64,2048]{1,0:T(8,128)(2,1)S(1)} %get-tuple-element.44), channel_id=1, source_target_pairs={{0,16},{1,17},{2,18},{3,19},{4,20},{5,21},{6,22},{7,23},{8,24},{9,... | collective-permute-start | bytes 786440 | tf_op jit(solution)/shard_map/ppermute | solution.py:455
  156.3 20.2 %copy-start.3 = (bf16[512,1024]{1,0:T(8,128)(2,1)S(1)}, bf16[512,1024]{1,0:T(8,128)(2,1)}, u32[]{:S(2)}) copy-start(bf16[512,1024]{1,0:T(8,128)(2,1)} %get-tuple-element.57) | copy-start | bytes 3145732
  164.8 13.0 %collective-permute-start.25 = (bf16[16,2048]{1,0:T(8,128)(2,1)S(1)}, bf16[16,2048]{1,0:T(8,128)(2,1)S(1)}, u32[]{:S(2)}, u32[]{:S(2)}) collective-permute-start(bf16[16,2048]{1,0:T(8,128)(2,1)S(1)} %get-tuple-element.49), channel_id=1, source_target_pairs={{0,28},{1,29},{2,30},{3,31},{4,0},{5,1},{6,2},{7,3},{8,4},{9,5},{1... | collective-permute-start | bytes 196616 | tf_op jit(solution)/shard_map/ppermute | solution.py:459
  167.6 10.2 %collective-permute-start.26 = (bf16[16,2048]{1,0:T(8,128)(2,1)S(1)}, bf16[16,2048]{1,0:T(8,128)(2,1)S(1)}, u32[]{:S(2)}, u32[]{:S(2)}) collective-permute-start(bf16[16,2048]{1,0:T(8,128)(2,1)S(1)} %get-tuple-element.50), channel_id=1, source_target_pairs={{0,4},{1,5},{2,6},{3,7},{4,8},{5,9},{6,10},{7,11},{8,12},{9,13},{1... | collective-permute-start | bytes 196616 | tf_op jit(solution)/shard_map/ppermute | solution.py:459
  171.9 6.5 %collective-permute-start.27 = (bf16[16,2048]{1,0:T(8,128)(2,1)S(1)}, bf16[16,2048]{1,0:T(8,128)(2,1)S(1)}, u32[]{:S(2)}, u32[]{:S(2)}) collective-permute-start(bf16[16,2048]{1,0:T(8,128)(2,1)S(1)} %get-tuple-element.51), channel_id=1, source_target_pairs={{0,8},{1,9},{2,10},{3,11},{4,12},{5,13},{6,14},{7,15},{8,16},{9,17... | collective-permute-start | bytes 196616 | tf_op jit(solution)/shard_map/ppermute | solution.py:459
  176.5 15.2 %collective-permute-start.32 = (bf16[512,1024]{1,0:T(8,128)(2,1)S(1)}, bf16[512,1024]{1,0:T(8,128)(2,1)}, u32[]{:S(2)}, u32[]{:S(2)}) collective-permute-start(bf16[512,1024]{1,0:T(8,128)(2,1)S(1)} %copy-done.3), channel_id=1, source_target_pairs={{0,32},{32,0},{64,96},{96,64},{128,160},{160,128},{192,224},{224,1... | collective-permute-start | bytes 3145736 | tf_op jit(solution)/shard_map/ppermute | solution.py:41
  177.8 13.9 %collective-permute-start.33 = (bf16[512,768]{1,0:T(8,128)(2,1)}, bf16[512,768]{1,0:T(8,128)(2,1)S(1)}, u32[]{:S(2)}, u32[]{:S(2)}) collective-permute-start(bf16[512,768]{1,0:T(8,128)(2,1)} %get-tuple-element.58), channel_id=1, source_target_pairs={{0,32},{32,0},{64,96},{96,64},{128,160},{160,128},{192,224},{224,1... | collective-permute-start | bytes 2359304 | tf_op jit(solution)/shard_map/ppermute | solution.py:41
  178.4 13.3 %copy-start = (bf16[512,1024]{1,0:T(8,128)(2,1)S(1)}, bf16[512,1024]{1,0:T(8,128)(2,1)}, u32[]{:S(2)}) copy-start(bf16[512,1024]{1,0:T(8,128)(2,1)} %get-tuple-element.61) | copy-start | bytes 3145732
  178.5 4.7 %collective-permute-start.28 = (bf16[16,1024]{1,0:T(8,128)(2,1)S(1)}, bf16[16,1024]{1,0:T(8,128)(2,1)S(1)}, u32[]{:S(2)}, u32[]{:S(2)}) collective-permute-start(bf16[16,1024]{1,0:T(8,128)(2,1)S(1)} %slice.36), channel_id=1, source_target_pairs={{0,32},{32,0},{64,96},{96,64},{128,160},{160,128},{192,224},{224,1... | collective-permute-start | bytes 98312 | tf_op jit(solution)/shard_map/ppermute | solution.py:41
  182.3 14.0 %collective-permute-start.34 = (bf16[512,768]{1,0:T(8,128)(2,1)}, bf16[512,768]{1,0:T(8,128)(2,1)}, u32[]{:S(2)}, u32[]{:S(2)}) collective-permute-start(bf16[512,768]{1,0:T(8,128)(2,1)} %get-tuple-element.59), channel_id=1, source_target_pairs={{0,32},{32,0},{64,96},{96,64},{128,160},{160,128},{192,224},{224,1... | collective-permute-start | bytes 2359304 | tf_op jit(solution)/shard_map/ppermute | solution.py:41
  186.5 23.2 %all-to-all-start.5 = ((bf16[8,16,2048]{2,1,0:T(8,128)(2,1)}), bf16[8,16,2048]{2,1,0:T(8,128)(2,1)S(1)}, u32[]{:S(2)}, u32[]{:S(2)}) async-start(bf16[8,16,2048]{2,1,0:T(8,128)(2,1)} %bitcast.15), calls=%async_computation.5 | async-start | bytes 1048576 | tf_op jit(solution)/shard_map/all_to_all | solution.py:46
  191.7 4.5 %copy-start.4 = (bf16[512,768]{1,0:T(8,128)(2,1)S(1)}, bf16[512,768]{1,0:T(8,128)(2,1)}, u32[]{:S(2)}) copy-start(bf16[512,768]{1,0:T(8,128)(2,1)} %get-tuple-element.59) | copy-start | bytes 2359300
  209.8 1.4 collective-permute-start.35

commit v2 on v1

--- a/solution.py
+++ b/solution.py
@@ -179,7 +179,7 @@
 def hidden_term_product(index, own, blocks, down_a, down_b):
     rows = own.shape[0]
     cols, width = down_a.shape
-    tile = 384
+    tile = 256
     weight = pl.BlockSpec((tile, width), lambda j, _: (j, 0))
     return call(
         hidden_term_kernel,
@@ -449,17 +449,17 @@
     grad_rows = jnp.concatenate([own_all[:, width:], swap_core(grad_other)], axis=0)
     down_grad = dot(all_tokens(hidden), grad_rows, TN).astype(BF16)
     gate_grad = dot(tok_rows, all_tokens(pre_gate), TN).astype(BF16)
-    up_grad = dot(tok_rows, all_tokens(pre_up), TN).astype(BF16)
+    input_sum = sum_of(x, after(input_y, down_grad, gate_grad))
+    up_grad = dot(tok_rows, after(all_tokens(pre_up), input_sum), TN).astype(BF16)
     near, far = split_sum(zyx, mixed_y)
     previous, mine, following, second = fold(
-        zyx, near, after(lax.ppermute(far, "col", Z_STEP[4]), down_grad)
+        zyx, near, after(lax.ppermute(far, "col", Z_STEP[4]), up_grad)
     )
     mixed_sum = mine.astype(F32)
     for block, step in ((previous, NZ - 1), (following, 1), (second, 2)):
         mixed_sum += lax.ppermute(block, "col", Z_STEP[step]).astype(F32)
     mixed = join(mixed_sum.astype(BF16))
-    input_sum = sum_of(x, after(input_y, mixed))
-    input_sum = after(exchange(input_sum, "col", Z_GROUPS), down_grad, gate_grad, up_grad)
+    input_sum = after(exchange(input_sum, "col", Z_GROUPS), up_grad, mixed)
     input_grad = join(input_sum.astype(F32).sum(0).astype(BF16))
     return (mixed, input_grad, gate_grad, up_grad, down_grad)
 

time: 213 us -> 212 us (level)
  starting transfers between devices: 86.5 us -> 82.1 us
  other arithmetic: 1.5 us -> 3.98 us
    ppermute x3, starting transfers between devices: 11.6 us -> 3.9 us  [body(): mixed_sum += lax.ppermute(block, 'col', Z_STEP[step]).astype(F32)]
    ppermute x3, waiting for transfers between devices: 0.59 us -> 7.62 us  [body(): mixed_sum += lax.ppermute(block, 'col', Z_STEP[step]).astype(F32)]
    all_to_all x6, waiting for transfers between devices: 20.7 us -> 15.2 us  [exchange(): lax.all_to_all(value, axis, 0, 0, axis_index_groups=groups, tiled=True)]
    ppermute x1, waiting for transfers between devices: 3.43 us -> 0.01 us  [body(): lax.ppermute(far, 'col', Z_STEP[4])]
    concatenate x0 -> x1, other arithmetic: none -> 2.48 us  [all_tokens(): return jnp.concatenate([value, swap_core(value)], axis=0)]
    all_to_all x6, starting transfers between devices: 31.3 us -> 33.5 us  [exchange(): lax.all_to_all(value, axis, 0, 0, axis_index_groups=groups, tiled=True)]
  transfers between devices with their start and end apart: 42 -> 42, of which waited for: 21 -> 23; matrix products, arithmetic and copies ran while one was open for 9% -> 9% of each run, Pallas kernels for 14% -> 14%
where the time goes in v2:
time: 212 us; the launch traced here: 209 us
  starting transfers between devices  82.1 us (39%)
  waiting for transfers between devices  66.5 us (31%)
  Pallas kernels  35.1 us (17%)
  matrix products  13.4 us (6%)
  local copies, waits for them, and re-layouts  7.35 us (3%)
  other arithmetic  3.98 us (2%)
    all_to_all x6, starting transfers between devices, exchange(): lax.all_to_all(value, axis, 0, 0, axis_index_groups=groups, tiled=True)  33.5 us
    ppermute x9, waiting for transfers between devices, gather_blocks(): lax.ppermute(own, axis, steps[count - k])  21.6 us
    ppermute x12, starting transfers between devices, swap_core(): return lax.ppermute(value, 'row', CORE_PAIRS)  15.8 us
    all_to_all x6, waiting for transfers between devices, exchange(): lax.all_to_all(value, axis, 0, 0, axis_index_groups=groups, tiled=True)  15.2 us
    dot_general x3, matrix products, dot(): return lax.dot_general(left, right, dims, preferred_element_type=F32)  13.4 us
    ppermute x3, waiting for transfers between devices, ring_eight(): before.append(lax.ppermute(before[-1], axis, up))  12.9 us
    ppermute x9, starting transfers between devices, gather_blocks(): lax.ppermute(own, axis, steps[count - k])  11 us
    ppermute x3, waiting for transfers between devices, body(): mixed_sum += lax.ppermute(block, 'col', Z_STEP[step]).astype(F32)  7.62 us
  transfers between devices with their start and end apart: 42, of which 23 were waited for; matrix products, arithmetic and copies ran while one was open for 9% of the time, Pallas kernels for 14%

profile of v2, /device:TPU:1, one launch (start us, length us, event | category | flops | bytes accessed | tf_op | source)
XLA Modules:
  0.0 209.2 jit_solution(2660813945797085221)
XLA Ops:
  2.2 0.8 tile.4
  3.1 9.0 %all-to-all-start = ((bf16[8,16,2048]{2,1,0:T(8,128)(2,1)}), bf16[8,16,2048]{2,1,0:T(8,128)(2,1)S(1)}, u32[]{:S(2)}, u32[]{:S(2)}) async-start(bf16[8,16,2048]{2,1,0:T(8,128)(2,1)} %tile.4), calls=%async_computation | async-start | bytes 1048576 | tf_op jit(solution)/shard_map/all_to_all | solution.py:46
  12.1 1.0 collective-permute-start
  14.3 1.3 collective-permute-start.4
  15.6 2.6 %collective-permute-start.3 = (bf16[16,2048]{1,0:T(8,128)(2,1)S(1)}, bf16[16,2048]{1,0:T(8,128)(2,1)S(1)}, u32[]{:S(2)}, u32[]{:S(2)}) collective-permute-start(bf16[16,2048]{1,0:T(8,128)(2,1)S(1)} %constant_dynamic-update-slice_fusion), channel_id=1, source_target_pairs={{0,2},{1,3},{2,0},{3,1},{4,6},{5,7},{6,4},{7,5},{8,10},{9,11},{10,... | collective-permute-start | bytes 196616 | tf_op jit(solution)/shard_map/ppermute | solution.py:61
  18.2 1.1 collective-permute-start.2
  19.2 2.4 %collective-permute-done.3 = bf16[16,2048]{1,0:T(8,128)(2,1)S(1)} collective-permute-done((bf16[16,2048]{1,0:T(8,128)(2,1)S(1)}, bf16[16,2048]{1,0:T(8,128)(2,1)S(1)}, u32[]{:S(2)}, u32[]{:S(2)}) %collective-permute-start.3) | collective-permute-done | bytes 65568 | tf_op jit(solution)/shard_map/ppermute | solution.py:61
  21.7 1.8 collective-permute-start.6
  23.5 1.3 collective-permute-start.5
  24.8 1.8 collective-permute-start.17
  26.6 6.2 %collective-permute-done.6.refs_8_ = bf16[64,2048]{1,0:T(8,128)(2,1)S(1)} collective-permute-done((bf16[64,2048]{1,0:T(8,128)(2,1)S(1)}, bf16[64,2048]{1,0:T(8,128)(2,1)S(1)}, u32[]{:S(2)}, u32[]{:S(2)}) %collective-permute-start.6) | collective-permute-done | bytes 262176 | tf_op jit(solution)/shard_map/ppermute | solution.py:68
  32.8 1.6 tile.5
  34.4 3.6 %all-to-all-start.1 = ((bf16[4,128,2048]{2,1,0:T(8,128)(2,1)}), bf16[4,128,2048]{2,1,0:T(8,128)(2,1)S(1)}, u32[]{:S(2)}, u32[]{:S(2)}) async-start(bf16[4,128,2048]{2,1,0:T(8,128)(2,1)} %tile.5), calls=%async_computation.1 | async-start | bytes 4194304 | tf_op jit(solution)/shard_map/all_to_all | solution.py:46
  38.2 2.6 %collective-permute-start.7 = (bf16[64,2048]{1,0:T(8,128)(2,1)S(1)}, bf16[64,2048]{1,0:T(8,128)(2,1)S(1)}, u32[]{:S(2)}, u32[]{:S(2)}) collective-permute-start(bf16[64,2048]{1,0:T(8,128)(2,1)S(1)} %collective-permute-done.5.refs_1_), channel_id=1, source_target_pairs={{4,0},{5,1},{6,2},{7,3},{8,4},{9,5},{10,6},{11,7},{12,8},{13,9},{1... | collective-permute-start | bytes 786440 | tf_op jit(solution)/shard_map/ppermute | solution.py:69
  40.8 2.1 collective-permute-start.13
  42.8 2.8 %collective-permute-done.9.refs_7_ = bf16[64,2048]{1,0:T(8,128)(2,1)S(1)} collective-permute-done((bf16[64,2048]{1,0:T(8,128)(2,1)S(1)}, bf16[64,2048]{1,0:T(8,128)(2,1)S(1)}, u32[]{:S(2)}, u32[]{:S(2)}) %collective-permute-start.9) | collective-permute-done | bytes 262176 | tf_op jit(solution)/shard_map/ppermute | solution.py:68
  46.3 2.1 collective-permute-start.8
  48.4 3.9 %collective-permute-done.10.refs_6_ = bf16[64,2048]{1,0:T(8,128)(2,1)S(1)} collective-permute-done((bf16[64,2048]{1,0:T(8,128)(2,1)S(1)}, bf16[64,2048]{1,0:T(8,128)(2,1)S(1)}, u32[]{:S(2)}, u32[]{:S(2)}) %collective-permute-start.10) | collective-permute-done | bytes 262176 | tf_op jit(solution)/shard_map/ppermute | solution.py:68
  53.7 2.7 %collective-permute-start.12 = (bf16[32,2048]{1,0:T(8,128)(2,1)}, bf16[32,2048]{1,0:T(8,128)(2,1)}, u32[]{:S(2)}, u32[]{:S(2)}) collective-permute-start(bf16[32,2048]{1,0:T(8,128)(2,1)} %slice.33), channel_id=1, source_target_pairs={{4,0},{5,1},{6,2},{7,3},{8,4},{9,5},{10,6},{11,7},{12,8},{13,9},{1... | collective-permute-start | bytes 393224 | tf_op jit(solution)/shard_map/ppermute | solution.py:71
  56.4 2.1 %collective-permute-done.11.refs_4_ = bf16[32,2048]{1,0:T(8,128)(2,1)S(1)} collective-permute-done((bf16[32,2048]{1,0:T(8,128)(2,1)}, bf16[32,2048]{1,0:T(8,128)(2,1)S(1)}, u32[]{:S(2)}, u32[]{:S(2)}) %collective-permute-start.11) | collective-permute-done | bytes 131104 | tf_op jit(solution)/shard_map/ppermute | solution.py:70
  58.6 4.1 %all-to-all-done.1 = bf16[4,128,2048]{2,1,0:T(8,128)(2,1)S(1)} async-done(((bf16[4,128,2048]{2,1,0:T(8,128)(2,1)}), bf16[4,128,2048]{2,1,0:T(8,128)(2,1)S(1)}, u32[]{:S(2)}, u32[]{:S(2)}) %all-to-all-start.1) | async-done | bytes 2097184 | tf_op jit(solution)/shard_map/all_to_all | solution.py:46
  62.7 7.4 %shard_map.93 = (bf16[512,1536]{1,0:T(8,128)(2,1)}, bf16[512,1024]{1,0:T(8,128)(2,1)}) custom-call(s32[3]{0:T(128)S(1)} %pad_add_fusion.index, bf16[512,2048]{1,0:T(8,128)(2,1)S(1)} %bitcast.10, bf16[64,2048]{1,0:T(8,128)(2,1)S(1)} %pad_maximum_fusion.4.refs_0_, bf16[64,2048]{1,0:T(8,128)(2,1)S(1)} %collective-permute-done.5.refs_1_, ...), custom_call_target="tpu_custom_call" | custom-call | flops 3221225472 | bytes 10485760 | tf_op jit(solution)/shard_map/pallas_call | solution.py:148
  70.1 4.3 %all-to-all-start.2 = ((bf16[4,128,1536]{2,1,0:T(8,128)(2,1)}), bf16[4,128,1536]{2,1,0:T(8,128)(2,1)}, u32[]{:S(2)}, u32[]{:S(2)}) async-start(bf16[4,128,1536]{2,1,0:T(8,128)(2,1)} %bitcast.17), calls=%async_computation.2 | async-start | bytes 3145728 | tf_op jit(solution)/shard_map/all_to_all | solution.py:46
  74.4 5.5 %shard_map.92 = (bf16[128,768]{1,0:T(8,128)(2,1)}, bf16[128,768]{1,0:T(8,128)(2,1)}, bf16[128,768]{1,0:T(8,128)(2,1)}, bf16[128,768]{1,0:T(8,128)(2,1)}, bf16[512,1024]{1,0:T(8,128)(2,1)}) custom-call(s32[3]{0:T(128)S(1)} %pad_add_fusion.index, bf16[512,2048]{1,0:T(8,128)(2,1)S(1)} %bitcast.11, bf16[64,2048]{1,0:T(8,128)(2,1)S(1)} %pad_maximum_fusion.4.refs_0_, ...), custom_call_target="tpu_custom_call" | custom-call | flops 1610612736 | bytes 10485760 | tf_op jit(solution)/shard_map/pallas_call | solution.py:184
  80.0 1.4 collective-permute-start.14
  81.4 2.4 %collective-permute-start.15 = (bf16[128,768]{1,0:T(8,128)(2,1)}, bf16[128,768]{1,0:T(8,128)(2,1)S(1)}, u32[]{:S(2)}, u32[]{:S(2)}) collective-permute-start(bf16[128,768]{1,0:T(8,128)(2,1)} %get-tuple-element.37), channel_id=1, source_target_pairs={{0,128},{32,160},{64,192},{96,224},{128,0},{160,32},{192,64},{224,... | collective-permute-start | bytes 589832 | tf_op jit(solution)/shard_map/ppermute | solution.py:433
  83.8 1.2 collective-permute-start.16
  85.0 7.7 %all-to-all-done.2.terms = bf16[4,128,1536]{2,1,0:T(8,128)(2,1)} async-done(((bf16[4,128,1536]{2,1,0:T(8,128)(2,1)}), bf16[4,128,1536]{2,1,0:T(8,128)(2,1)}, u32[]{:S(2)}, u32[]{:S(2)}) %all-to-all-start.2) | async-done | bytes 1572896 | tf_op jit(solution)/shard_map/all_to_all | solution.py:46
  92.7 2.5 %shard_map.94 = (f32[128,1536]{1,0:T(8,128)}, bf16[128,768]{1,0:T(8,128)(2,1)S(1)}) custom-call(s32[1]{0:T(128)} %bitcast.2.index, bf16[4,128,1536]{2,1,0:T(8,128)(2,1)} %all-to-all-done.2.terms), custom_call_target="tpu_custom_call" | custom-call | flops 3145728 | bytes 10485760 | tf_op jit(solution)/shard_map/pallas_call | solution.py:282
  95.5 1.8 collective-permute-start.20
  97.9 2.9 %collective-permute-done.15.refs_2_ = bf16[128,768]{1,0:T(8,128)(2,1)S(1)} collective-permute-done((bf16[128,768]{1,0:T(8,128)(2,1)}, bf16[128,768]{1,0:T(8,128)(2,1)S(1)}, u32[]{:S(2)}, u32[]{:S(2)}) %collective-permute-start.15) | collective-permute-done | bytes 196640 | tf_op jit(solution)/shard_map/ppermute | solution.py:433
  100.8 1.5 shard_map.95.refs_0_
  102.3 2.3 %collective-permute-done.21.refs_3_ = bf16[128,768]{1,0:T(8,128)(2,1)S(1)} collective-permute-done((bf16[128,768]{1,0:T(8,128)(2,1)S(1)}, bf16[128,768]{1,0:T(8,128)(2,1)S(1)}, u32[]{:S(2)}, u32[]{:S(2)}) %collective-permute-start.21) | collective-permute-done | bytes 196640 | tf_op jit(solution)/shard_map/ppermute | solution.py:61
  104.6 4.6 %collective-permute-done.20.refs_2_ = bf16[128,768]{1,0:T(8,128)(2,1)S(1)} collective-permute-done((bf16[128,768]{1,0:T(8,128)(2,1)S(1)}, bf16[128,768]{1,0:T(8,128)(2,1)S(1)}, u32[]{:S(2)}, u32[]{:S(2)}) %collective-permute-start.20) | collective-permute-done | bytes 196640 | tf_op jit(solution)/shard_map/ppermute | solution.py:61
  109.2 5.2 %shard_map.96 = (bf16[512,2048]{1,0:T(8,128)(2,1)}, bf16[512,768]{1,0:T(8,128)(2,1)}) custom-call(s32[1]{0:T(128)} %bitcast.2.index, bf16[128,768]{1,0:T(8,128)(2,1)S(1)} %get-tuple-element.42.refs_0_, bf16[128,768]{1,0:T(8,128)(2,1)S(1)} %collective-permute-done.19.refs_1_, bf16[128,768]{1,0:T(8,128)(2,1)S(1)} %collective-permute-done.20.refs_2_, ...), custom_call_target="tpu_custom_call" | custom-call | flops 1610612736 | bytes 10485760 | tf_op jit(solution)/shard_map/pallas_call | solution.py:217
  114.4 4.5 %all-to-all-start.3 = ((bf16[4,128,2048]{2,1,0:T(8,128)(2,1)}), bf16[4,128,2048]{2,1,0:T(8,128)(2,1)}, u32[]{:S(2)}, u32[]{:S(2)}) async-start(bf16[4,128,2048]{2,1,0:T(8,128)(2,1)} %bitcast.15), calls=%async_computation.3 | async-start | bytes 4194304 | tf_op jit(solution)/shard_map/all_to_all | solution.py:46
  119.0 1.3 collective-permute-start.25
  120.2 2.0 collective-permute-start.24
  122.2 4.3 %collective-permute-start.29 = (bf16[512,1024]{1,0:T(8,128)(2,1)}, bf16[512,1024]{1,0:T(8,128)(2,1)}, u32[]{:S(2)}, u32[]{:S(2)}) collective-permute-start(bf16[512,1024]{1,0:T(8,128)(2,1)} %get-tuple-element.53), channel_id=1, source_target_pairs={{0,32},{32,0},{64,96},{96,64},{128,160},{160,128},{192,224},{224,1... | collective-permute-start | bytes 3145736 | tf_op jit(solution)/shard_map/ppermute | solution.py:41
  126.5 5.2 %collective-permute-done.26.refs_3_ = bf16[128,1536]{1,0:T(8,128)(2,1)S(1)} collective-permute-done((bf16[128,1536]{1,0:T(8,128)(2,1)S(1)}, bf16[128,1536]{1,0:T(8,128)(2,1)S(1)}, u32[]{:S(2)}, u32[]{:S(2)}) %collective-permute-start.26) | collective-permute-done | bytes 393248 | tf_op jit(solution)/shard_map/ppermute | solution.py:61
  131.7 1.2 collective-permute-done.25.refs_2_
  132.9 5.9 %collective-permute-done.24.refs_1_ = bf16[128,1536]{1,0:T(8,128)(2,1)S(1)} collective-permute-done((bf16[128,1536]{1,0:T(8,128)(2,1)S(1)}, bf16[128,1536]{1,0:T(8,128)(2,1)S(1)}, u32[]{:S(2)}, u32[]{:S(2)}) %collective-permute-start.24) | collective-permute-done | bytes 393248 | tf_op jit(solution)/shard_map/ppermute | solution.py:61
  138.8 7.2 %shard_map.98 = (bf16[512,2048]{1,0:T(8,128)(2,1)}, bf16[512,768]{1,0:T(8,128)(2,1)}, bf16[512,768]{1,0:T(8,128)(2,1)}) custom-call(s32[1]{0:T(128)} %bitcast.2.index, bf16[128,1536]{1,0:T(8,128)(2,1)S(1)} %shard_map.95.refs_0_, bf16[128,1536]{1,0:T(8,128)(2,1)S(1)} %collective-permute-done.24.refs_1_, ...), custom_call_target="tpu_custom_call" | custom-call | flops 3221225472 | bytes 10485760 | tf_op jit(solution)/shard_map/pallas_call | solution.py:253
  146.0 4.5 %all-to-all-start.4 = ((bf16[4,128,2048]{2,1,0:T(8,128)(2,1)}), bf16[4,128,2048]{2,1,0:T(8,128)(2,1)}, u32[]{:S(2)}, u32[]{:S(2)}) async-start(bf16[4,128,2048]{2,1,0:T(8,128)(2,1)} %bitcast.14), calls=%async_computation.4 | async-start | bytes 4194304 | tf_op jit(solution)/shard_map/all_to_all | solution.py:46
  150.4 2.1 collective-permute-start.28
  153.3 1.3 collective-permute-done.28
  154.6 4.5 %fusion.4 = bf16[768,1024]{1,0:T(8,128)(2,1)} fusion(bf16[512,1024]{1,0:T(8,128)(2,1)} %collective-permute-done.29, bf16[512,1024]{1,0:T(8,128)(2,1)S(1)} %get-tuple-element.64, bf16[512,768]{1,0:T(8,128)(2,1)S(1)} %collective-permute-done.28, bf16[512,768]{1,0:T(8,128)(2,1)} %get-tuple-element.52), kind=kOutput, calls=%fused_computation.5 | convolution fusion | flops 1618739200 | bytes 5242880 | tf_op jit(solution)/shard_map/dot_general | solution.py:37
  159.1 2.5 %pad_maximum_fusion.1 = bf16[1024,768]{1,0:T(8,128)(2,1)} fusion(bf16[512,768]{1,0:T(8,128)(2,1)S(1)} %collective-permute-done.27, bf16[512,768]{1,0:T(8,128)(2,1)} %get-tuple-element.49), kind=kLoop, calls=%fused_computation.8 | loop fusion | flops 3145728 | bytes 3145728 | tf_op jit(solution)/shard_map/concatenate | solution.py:446
  161.6 1.1 copy-done.2
  162.6 4.2 %convolution_convert_fusion.1 = bf16[1024,768]{1,0:T(8,128)(2,1)} fusion(bf16[512,768]{1,0:T(8,128)(2,1)S(1)} %collective-permute-done.30, bf16[512,768]{1,0:T(8,128)(2,1)} %get-tuple-element.54, bf16[512,1024]{1,0:T(8,128)(2,1)S(1)} %collective-permute-done.23, bf16[512,1024]{1,0:T(8,128)(2,1)S(1)} %get-tuple-element.63), kind=kOutput, calls=%fused_computation.7 | convolution fusion | flops 1618739200 | bytes 5242880 | tf_op jit(solution)/shard_map/dot_general | solution.py:37
  166.8 2.5 %shard_map.97 = (bf16[64,2048]{1,0:T(8,128)(2,1)S(1)}, bf16[64,2048]{1,0:T(8,128)(2,1)S(1)}) custom-call(s32[3]{0:T(128)S(1)} %pad_add_fusion.index, bf16[4,128,2048]{2,1,0:T(8,128)(2,1)} %all-to-all-done.3.terms), custom_call_target="tpu_custom_call" | custom-call | flops 2097152 | bytes 10485760 | tf_op jit(solution)/shard_map/pallas_call | solution.py:360
  169.4 2.2 %collective-permute-start.22 = (bf16[64,2048]{1,0:T(8,128)(2,1)S(1)}, bf16[64,2048]{1,0:T(8,128)(2,1)S(1)}, u32[]{:S(2)}, u32[]{:S(2)}) collective-permute-start(bf16[64,2048]{1,0:T(8,128)(2,1)S(1)} %get-tuple-element.45), channel_id=1, source_target_pairs={{0,16},{1,17},{2,18},{3,19},{4,20},{5,21},{6,22},{7,23},{8,24},{9,... | collective-permute-start | bytes 786440 | tf_op jit(solution)/shard_map/ppermute | solution.py:456
  171.6 3.3 %all-to-all-done.4.terms = bf16[4,128,2048]{2,1,0:T(8,128)(2,1)} async-done(((bf16[4,128,2048]{2,1,0:T(8,128)(2,1)}), bf16[4,128,2048]{2,1,0:T(8,128)(2,1)}, u32[]{:S(2)}, u32[]{:S(2)}) %all-to-all-start.4) | async-done | bytes 2097184 | tf_op jit(solution)/shard_map/all_to_all | solution.py:46
  174.9 2.7 %shard_map.99 = bf16[128,2048]{1,0:T(8,128)(2,1)} custom-call(s32[1]{0:T(128)} %bitcast.2.index, bf16[4,128,2048]{2,1,0:T(8,128)(2,1)} %all-to-all-done.4.terms), custom_call_target="tpu_custom_call" | custom-call | flops 2097152 | bytes 10485760 | tf_op jit(solution)/shard_map/pallas_call | solution.py:338
  177.6 7.6 %all-to-all-start.5 = ((bf16[8,16,2048]{2,1,0:T(8,128)(2,1)}), bf16[8,16,2048]{2,1,0:T(8,128)(2,1)S(1)}, u32[]{:S(2)}, u32[]{:S(2)}) async-start(bf16[8,16,2048]{2,1,0:T(8,128)(2,1)} %bitcast.16), calls=%async_computation.5 | async-start | bytes 1048576 | tf_op jit(solution)/shard_map/all_to_all | solution.py:46
  185.2 4.7 %convolution_convert_fusion = bf16[1024,768]{1,0:T(8,128)(2,1)} fusion(bf16[1024,768]{1,0:T(8,128)(2,1)} %pad_maximum_fusion.1, bf16[512,1024]{1,0:T(8,128)(2,1)} %copy-done.2, bf16[512,1024]{1,0:T(8,128)(2,1)S(1)} %get-tuple-element.63), kind=kOutput, calls=%fused_computation.6 | convolution fusion | flops 1615593472 | bytes 5242880 | tf_op jit(solution)/shard_map/dot_general | solution.py:37
  190.6 2.7 %collective-permute-start.31 = (bf16[16,2048]{1,0:T(8,128)(2,1)S(1)}, bf16[16,2048]{1,0:T(8,128)(2,1)S(1)}, u32[]{:S(2)}, u32[]{:S(2)}) collective-permute-start(bf16[16,2048]{1,0:T(8,128)(2,1)S(1)} %get-tuple-element.59), channel_id=1, source_target_pairs={{0,28},{1,29},{2,30},{3,31},{4,0},{5,1},{6,2},{7,3},{8,4},{9,5},{1... | collective-permute-start | bytes 196616 | tf_op jit(solution)/shard_map/ppermute | solution.py:460
  193.3 1.2 collective-permute-start.33
  194.5 2.1 %collective-permute-done.31 = bf16[16,2048]{1,0:T(8,128)(2,1)S(1)} collective-permute-done((bf16[16,2048]{1,0:T(8,128)(2,1)S(1)}, bf16[16,2048]{1,0:T(8,128)(2,1)S(1)}, u32[]{:S(2)}, u32[]{:S(2)}) %collective-permute-start.31) | collective-permute-done | bytes 65568 | tf_op jit(solution)/shard_map/ppermute | solution.py:460
  196.6 3.0 %collective-permute-done.32 = bf16[16,2048]{1,0:T(8,128)(2,1)S(1)} collective-permute-done((bf16[16,2048]{1,0:T(8,128)(2,1)S(1)}, bf16[16,2048]{1,0:T(8,128)(2,1)S(1)}, u32[]{:S(2)}, u32[]{:S(2)}) %collective-permute-start.32) | collective-permute-done | bytes 65568 | tf_op jit(solution)/shard_map/ppermute | solution.py:460
  199.6 2.5 %collective-permute-done.33 = bf16[16,2048]{1,0:T(8,128)(2,1)S(1)} collective-permute-done((bf16[16,2048]{1,0:T(8,128)(2,1)S(1)}, bf16[16,2048]{1,0:T(8,128)(2,1)S(1)}, u32[]{:S(2)}, u32[]{:S(2)}) %collective-permute-start.33) | collective-permute-done | bytes 65568 | tf_op jit(solution)/shard_map/ppermute | solution.py:460
  202.1 3.5 %collective-permute-start.34 = (bf16[16,1024]{1,0:T(8,128)(2,1)S(1)}, bf16[16,1024]{1,0:T(8,128)(2,1)S(1)}, u32[]{:S(2)}, u32[]{:S(2)}) collective-permute-start(bf16[16,1024]{1,0:T(8,128)(2,1)S(1)} %slice.37), channel_id=1, source_target_pairs={{0,32},{32,0},{64,96},{96,64},{128,160},{160,128},{192,224},{224,1... | collective-permute-start | bytes 98312 | tf_op jit(solution)/shard_map/ppermute | solution.py:41
  205.7 0.9 collective-permute-done.34
  207.7 0.9 collective-permute-done.35
  (59 shorter events, 9.5 us)
Async XLA Ops:
  3.1 29.7 %all-to-all-start = ((bf16[8,16,2048]{2,1,0:T(8,128)(2,1)}), bf16[8,16,2048]{2,1,0:T(8,128)(2,1)S(1)}, u32[]{:S(2)}, u32[]{:S(2)}) async-start(bf16[8,16,2048]{2,1,0:T(8,128)(2,1)} %tile.4), calls=%async_computation | async-start | bytes 1048576 | tf_op jit(solution)/shard_map/all_to_all | solution.py:46
  12.1 1.8 collective-permute-start
  13.0 1.2 collective-permute-start.1
  14.3 5.0 %collective-permute-start.4 = (bf16[16,2048]{1,0:T(8,128)(2,1)S(1)}, bf16[16,2048]{1,0:T(8,128)(2,1)S(1)}, u32[]{:S(2)}, u32[]{:S(2)}) collective-permute-start(bf16[16,2048]{1,0:T(8,128)(2,1)S(1)} %constant_dynamic-update-slice_fusion), channel_id=1, source_target_pairs={{0,1},{1,2},{2,3},{3,0},{4,5},{5,6},{6,7},{7,4},{8,9},{9,10},{10,1... | collective-permute-start | bytes 196616 | tf_op jit(solution)/shard_map/ppermute | solution.py:61
  15.6 6.1 %collective-permute-start.3 = (bf16[16,2048]{1,0:T(8,128)(2,1)S(1)}, bf16[16,2048]{1,0:T(8,128)(2,1)S(1)}, u32[]{:S(2)}, u32[]{:S(2)}) collective-permute-start(bf16[16,2048]{1,0:T(8,128)(2,1)S(1)} %constant_dynamic-update-slice_fusion), channel_id=1, source_target_pairs={{0,2},{1,3},{2,0},{3,1},{4,6},{5,7},{6,4},{7,5},{8,10},{9,11},{10,... | collective-permute-start | bytes 196616 | tf_op jit(solution)/shard_map/ppermute | solution.py:61
  18.2 3.5 %collective-permute-start.2 = (bf16[16,2048]{1,0:T(8,128)(2,1)S(1)}, bf16[16,2048]{1,0:T(8,128)(2,1)S(1)}, u32[]{:S(2)}, u32[]{:S(2)}) collective-permute-start(bf16[16,2048]{1,0:T(8,128)(2,1)S(1)} %constant_dynamic-update-slice_fusion), channel_id=1, source_target_pairs={{0,3},{1,0},{2,1},{3,2},{4,7},{5,4},{6,5},{7,6},{8,11},{9,8},{10,9... | collective-permute-start | bytes 196616 | tf_op jit(solution)/shard_map/ppermute | solution.py:61
  21.7 11.1 %collective-permute-start.6 = (bf16[64,2048]{1,0:T(8,128)(2,1)S(1)}, bf16[64,2048]{1,0:T(8,128)(2,1)S(1)}, u32[]{:S(2)}, u32[]{:S(2)}) collective-permute-start(bf16[64,2048]{1,0:T(8,128)(2,1)S(1)} %pad_maximum_fusion.4.refs_0_), channel_id=1, source_target_pairs={{0,4},{1,5},{2,6},{3,7},{4,8},{5,9},{6,10},{7,11},{8,12},{9,13},{1... | collective-permute-start | bytes 786440 | tf_op jit(solution)/shard_map/ppermute | solution.py:68
  23.5 9.3 %collective-permute-start.5 = (bf16[64,2048]{1,0:T(8,128)(2,1)S(1)}, bf16[64,2048]{1,0:T(8,128)(2,1)S(1)}, u32[]{:S(2)}, u32[]{:S(2)}) collective-permute-start(bf16[64,2048]{1,0:T(8,128)(2,1)S(1)} %pad_maximum_fusion.4.refs_0_), channel_id=1, source_target_pairs={{4,0},{5,1},{6,2},{7,3},{8,4},{9,5},{10,6},{11,7},{12,8},{13,9},{1... | collective-permute-start | bytes 786440 | tf_op jit(solution)/shard_map/ppermute | solution.py:69
  24.8 33.8 %collective-permute-start.17 = (bf16[1024,768]{1,0:T(8,128)(2,1)}, bf16[1024,768]{1,0:T(8,128)(2,1)}, u32[]{:S(2)}, u32[]{:S(2)}) collective-permute-start(bf16[1024,768]{1,0:T(8,128)(2,1)} %refs_4_.3), channel_id=1, source_target_pairs={{0,32},{32,0},{64,96},{96,64},{128,160},{160,128},{192,224},{224,1... | collective-permute-start | bytes 4718600 | tf_op jit(solution)/shard_map/ppermute | solution.py:41
  26.6 32.0 %collective-permute-start.18 = (bf16[1024,768]{1,0:T(8,128)(2,1)}, bf16[1024,768]{1,0:T(8,128)(2,1)}, u32[]{:S(2)}, u32[]{:S(2)}) collective-permute-start(bf16[1024,768]{1,0:T(8,128)(2,1)} %refs_5_.1), channel_id=1, source_target_pairs={{0,32},{32,0},{64,96},{96,64},{128,160},{160,128},{192,224},{224,1... | collective-permute-start | bytes 4718600 | tf_op jit(solution)/shard_map/ppermute | solution.py:41
  34.4 28.3 %all-to-all-start.1 = ((bf16[4,128,2048]{2,1,0:T(8,128)(2,1)}), bf16[4,128,2048]{2,1,0:T(8,128)(2,1)S(1)}, u32[]{:S(2)}, u32[]{:S(2)}) async-start(bf16[4,128,2048]{2,1,0:T(8,128)(2,1)} %tile.5), calls=%async_computation.1 | async-start | bytes 4194304 | tf_op jit(solution)/shard_map/all_to_all | solution.py:46
  38.0 7.6 %collective-permute-start.9 = (bf16[64,2048]{1,0:T(8,128)(2,1)S(1)}, bf16[64,2048]{1,0:T(8,128)(2,1)S(1)}, u32[]{:S(2)}, u32[]{:S(2)}) collective-permute-start(bf16[64,2048]{1,0:T(8,128)(2,1)S(1)} %collective-permute-done.6.refs_8_), channel_id=1, source_target_pairs={{0,4},{1,5},{2,6},{3,7},{4,8},{5,9},{6,10},{7,11},{8,12},{9,13},{1... | collective-permute-start | bytes 786440 | tf_op jit(solution)/shard_map/ppermute | solution.py:68
  38.2 7.4 %collective-permute-start.7 = (bf16[64,2048]{1,0:T(8,128)(2,1)S(1)}, bf16[64,2048]{1,0:T(8,128)(2,1)S(1)}, u32[]{:S(2)}, u32[]{:S(2)}) collective-permute-start(bf16[64,2048]{1,0:T(8,128)(2,1)S(1)} %collective-permute-done.5.refs_1_), channel_id=1, source_target_pairs={{4,0},{5,1},{6,2},{7,3},{8,4},{9,5},{10,6},{11,7},{12,8},{13,9},{1... | collective-permute-start | bytes 786440 | tf_op jit(solution)/shard_map/ppermute | solution.py:69
  40.8 33.7 %collective-permute-start.13 = (bf16[768,1024]{1,0:T(8,128)(2,1)}, bf16[768,1024]{1,0:T(8,128)(2,1)}, u32[]{:S(2)}, u32[]{:S(2)}) collective-permute-start(bf16[768,1024]{1,0:T(8,128)(2,1)} %refs_4_.2), channel_id=1, source_target_pairs={{0,32},{32,0},{64,96},{96,64},{128,160},{160,128},{192,224},{224,1... | collective-permute-start | bytes 4718600 | tf_op jit(solution)/shard_map/ppermute | solution.py:41
  45.6 0.7 copy-start
  45.6 6.7 %collective-permute-start.10 = (bf16[64,2048]{1,0:T(8,128)(2,1)S(1)}, bf16[64,2048]{1,0:T(8,128)(2,1)S(1)}, u32[]{:S(2)}, u32[]{:S(2)}) collective-permute-start(bf16[64,2048]{1,0:T(8,128)(2,1)S(1)} %collective-permute-done.9.refs_7_), channel_id=1, source_target_pairs={{0,4},{1,5},{2,6},{3,7},{4,8},{5,9},{6,10},{7,11},{8,12},{9,13},{1... | collective-permute-start | bytes 786440 | tf_op jit(solution)/shard_map/ppermute | solution.py:68
  46.3 6.7 %copy-start.1 = (bf16[64,2048]{1,0:T(8,128)(2,1)}, bf16[64,2048]{1,0:T(8,128)(2,1)S(1)}, u32[]{:S(2)}) copy-start(bf16[64,2048]{1,0:T(8,128)(2,1)S(1)} %collective-permute-done.7.refs_2_) | copy-start | bytes 786436
  46.3 6.7 %collective-permute-start.8 = (bf16[64,2048]{1,0:T(8,128)(2,1)S(1)}, bf16[64,2048]{1,0:T(8,128)(2,1)S(1)}, u32[]{:S(2)}, u32[]{:S(2)}) collective-permute-start(bf16[64,2048]{1,0:T(8,128)(2,1)S(1)} %collective-permute-done.7.refs_2_), channel_id=1, source_target_pairs={{4,0},{5,1},{6,2},{7,3},{8,4},{9,5},{10,6},{11,7},{12,8},{13,9},{1... | collective-permute-start | bytes 786440 | tf_op jit(solution)/shard_map/ppermute | solution.py:69
  53.0 5.5 %collective-permute-start.11 = (bf16[32,2048]{1,0:T(8,128)(2,1)}, bf16[32,2048]{1,0:T(8,128)(2,1)S(1)}, u32[]{:S(2)}, u32[]{:S(2)}) collective-permute-start(bf16[32,2048]{1,0:T(8,128)(2,1)} %slice.32), channel_id=1, source_target_pairs={{0,4},{1,5},{2,6},{3,7},{4,8},{5,9},{6,10},{7,11},{8,12},{9,13},{1... | collective-permute-start | bytes 393224 | tf_op jit(solution)/shard_map/ppermute | solution.py:70
  53.7 4.9 %collective-permute-start.12 = (bf16[32,2048]{1,0:T(8,128)(2,1)}, bf16[32,2048]{1,0:T(8,128)(2,1)}, u32[]{:S(2)}, u32[]{:S(2)}) collective-permute-start(bf16[32,2048]{1,0:T(8,128)(2,1)} %slice.33), channel_id=1, source_target_pairs={{4,0},{5,1},{6,2},{7,3},{8,4},{9,5},{10,6},{11,7},{12,8},{13,9},{1... | collective-permute-start | bytes 393224 | tf_op jit(solution)/shard_map/ppermute | solution.py:71
  70.1 22.7 %all-to-all-start.2 = ((bf16[4,128,1536]{2,1,0:T(8,128)(2,1)}), bf16[4,128,1536]{2,1,0:T(8,128)(2,1)}, u32[]{:S(2)}, u32[]{:S(2)}) async-start(bf16[4,128,1536]{2,1,0:T(8,128)(2,1)} %bitcast.17), calls=%async_computation.2 | async-start | bytes 3145728 | tf_op jit(solution)/shard_map/all_to_all | solution.py:46
  80.0 17.3 %collective-permute-start.14 = (bf16[128,768]{1,0:T(8,128)(2,1)}, bf16[128,768]{1,0:T(8,128)(2,1)S(1)}, u32[]{:S(2)}, u32[]{:S(2)}) collective-permute-start(bf16[128,768]{1,0:T(8,128)(2,1)} %get-tuple-element.36), channel_id=1, source_target_pairs={{0,64},{32,96},{64,128},{96,160},{128,192},{160,224},{192,0},{224,... | collective-permute-start | bytes 589832 | tf_op jit(solution)/shard_map/ppermute | solution.py:433
  81.4 19.3 %collective-permute-start.15 = (bf16[128,768]{1,0:T(8,128)(2,1)}, bf16[128,768]{1,0:T(8,128)(2,1)S(1)}, u32[]{:S(2)}, u32[]{:S(2)}) collective-permute-start(bf16[128,768]{1,0:T(8,128)(2,1)} %get-tuple-element.37), channel_id=1, source_target_pairs={{0,128},{32,160},{64,192},{96,224},{128,0},{160,32},{192,64},{224,... | collective-permute-start | bytes 589832 | tf_op jit(solution)/shard_map/ppermute | solution.py:433
  83.8 16.9 %collective-permute-start.16 = (bf16[128,768]{1,0:T(8,128)(2,1)}, bf16[128,768]{1,0:T(8,128)(2,1)S(1)}, u32[]{:S(2)}, u32[]{:S(2)}) collective-permute-start(bf16[128,768]{1,0:T(8,128)(2,1)} %get-tuple-element.38), channel_id=1, source_target_pairs={{0,192},{32,224},{64,0},{96,32},{128,64},{160,96},{192,128},{224,1... | collective-permute-start | bytes 589832 | tf_op jit(solution)/shard_map/ppermute | solution.py:433
  95.2 9.4 %collective-permute-start.21 = (bf16[128,768]{1,0:T(8,128)(2,1)S(1)}, bf16[128,768]{1,0:T(8,128)(2,1)S(1)}, u32[]{:S(2)}, u32[]{:S(2)}) collective-permute-start(bf16[128,768]{1,0:T(8,128)(2,1)S(1)} %get-tuple-element.42.refs_0_), channel_id=1, source_target_pairs={{0,64},{32,96},{64,128},{96,160},{128,192},{160,224},{192,0},{224,... | collective-permute-start | bytes 589832 | tf_op jit(solution)/shard_map/ppermute | solution.py:61
  95.5 13.7 %collective-permute-start.20 = (bf16[128,768]{1,0:T(8,128)(2,1)S(1)}, bf16[128,768]{1,0:T(8,128)(2,1)S(1)}, u32[]{:S(2)}, u32[]{:S(2)}) collective-permute-start(bf16[128,768]{1,0:T(8,128)(2,1)S(1)} %get-tuple-element.42.refs_0_), channel_id=1, source_target_pairs={{0,128},{32,160},{64,192},{96,224},{128,0},{160,32},{192,64},{224,... | collective-permute-start | bytes 589832 | tf_op jit(solution)/shard_map/ppermute | solution.py:61
  97.3 11.9 %collective-permute-start.19 = (bf16[128,768]{1,0:T(8,128)(2,1)S(1)}, bf16[128,768]{1,0:T(8,128)(2,1)S(1)}, u32[]{:S(2)}, u32[]{:S(2)}) collective-permute-start(bf16[128,768]{1,0:T(8,128)(2,1)S(1)} %get-tuple-element.42.refs_0_), channel_id=1, source_target_pairs={{0,192},{32,224},{64,0},{96,32},{128,64},{160,96},{192,128},{224,1... | collective-permute-start | bytes 589832 | tf_op jit(solution)/shard_map/ppermute | solution.py:61
  114.4 31.6 %all-to-all-start.3 = ((bf16[4,128,2048]{2,1,0:T(8,128)(2,1)}), bf16[4,128,2048]{2,1,0:T(8,128)(2,1)}, u32[]{:S(2)}, u32[]{:S(2)}) async-start(bf16[4,128,2048]{2,1,0:T(8,128)(2,1)} %bitcast.15), calls=%async_computation.3 | async-start | bytes 4194304 | tf_op jit(solution)/shard_map/all_to_all | solution.py:46
  118.9 12.9 %collective-permute-start.26 = (bf16[128,1536]{1,0:T(8,128)(2,1)S(1)}, bf16[128,1536]{1,0:T(8,128)(2,1)S(1)}, u32[]{:S(2)}, u32[]{:S(2)}) collective-permute-start(bf16[128,1536]{1,0:T(8,128)(2,1)S(1)} %shard_map.95.refs_0_), channel_id=1, source_target_pairs={{0,64},{32,96},{64,128},{96,160},{128,192},{160,224},{192,0},{224,... | collective-permute-start | bytes 1179656 | tf_op jit(solution)/shard_map/ppermute | solution.py:61
  119.0 13.9 %collective-permute-start.25 = (bf16[128,1536]{1,0:T(8,128)(2,1)S(1)}, bf16[128,1536]{1,0:T(8,128)(2,1)S(1)}, u32[]{:S(2)}, u32[]{:S(2)}) collective-permute-start(bf16[128,1536]{1,0:T(8,128)(2,1)S(1)} %shard_map.95.refs_0_), channel_id=1, source_target_pairs={{0,128},{32,160},{64,192},{96,224},{128,0},{160,32},{192,64},{224,... | collective-permute-start | bytes 1179656 | tf_op jit(solution)/shard_map/ppermute | solution.py:61
  120.2 18.5 %collective-permute-start.24 = (bf16[128,1536]{1,0:T(8,128)(2,1)S(1)}, bf16[128,1536]{1,0:T(8,128)(2,1)S(1)}, u32[]{:S(2)}, u32[]{:S(2)}) collective-permute-start(bf16[128,1536]{1,0:T(8,128)(2,1)S(1)} %shard_map.95.refs_0_), channel_id=1, source_target_pairs={{0,192},{32,224},{64,0},{96,32},{128,64},{160,96},{192,128},{224,1... | collective-permute-start | bytes 1179656 | tf_op jit(solution)/shard_map/ppermute | solution.py:61
  122.2 31.1 %collective-permute-start.29 = (bf16[512,1024]{1,0:T(8,128)(2,1)}, bf16[512,1024]{1,0:T(8,128)(2,1)}, u32[]{:S(2)}, u32[]{:S(2)}) collective-permute-start(bf16[512,1024]{1,0:T(8,128)(2,1)} %get-tuple-element.53), channel_id=1, source_target_pairs={{0,32},{32,0},{64,96},{96,64},{128,160},{160,128},{192,224},{224,1... | collective-permute-start | bytes 3145736 | tf_op jit(solution)/shard_map/ppermute | solution.py:41
  146.0 28.9 %all-to-all-start.4 = ((bf16[4,128,2048]{2,1,0:T(8,128)(2,1)}), bf16[4,128,2048]{2,1,0:T(8,128)(2,1)}, u32[]{:S(2)}, u32[]{:S(2)}) async-start(bf16[4,128,2048]{2,1,0:T(8,128)(2,1)} %bitcast.14), calls=%async_computation.4 | async-start | bytes 4194304 | tf_op jit(solution)/shard_map/all_to_all | solution.py:46
  150.4 4.2 %collective-permute-start.28 = (bf16[512,768]{1,0:T(8,128)(2,1)}, bf16[512,768]{1,0:T(8,128)(2,1)S(1)}, u32[]{:S(2)}, u32[]{:S(2)}) collective-permute-start(bf16[512,768]{1,0:T(8,128)(2,1)} %get-tuple-element.52), channel_id=1, source_target_pairs={{0,32},{32,0},{64,96},{96,64},{128,160},{160,128},{192,224},{224,1... | collective-permute-start | bytes 2359304 | tf_op jit(solution)/shard_map/ppermute | solution.py:41
  152.5 9.1 %collective-permute-start.23 = (bf16[512,1024]{1,0:T(8,128)(2,1)}, bf16[512,1024]{1,0:T(8,128)(2,1)S(1)}, u32[]{:S(2)}, u32[]{:S(2)}) collective-permute-start(bf16[512,1024]{1,0:T(8,128)(2,1)} %get-tuple-element.46), channel_id=1, source_target_pairs={{0,32},{32,0},{64,96},{96,64},{128,160},{160,128},{192,224},{224,1... | collective-permute-start | bytes 3145736 | tf_op jit(solution)/shard_map/ppermute | solution.py:41
  152.6 6.5 %collective-permute-start.27 = (bf16[512,768]{1,0:T(8,128)(2,1)}, bf16[512,768]{1,0:T(8,128)(2,1)S(1)}, u32[]{:S(2)}, u32[]{:S(2)}) collective-permute-start(bf16[512,768]{1,0:T(8,128)(2,1)} %get-tuple-element.49), channel_id=1, source_target_pairs={{0,32},{32,0},{64,96},{96,64},{128,160},{160,128},{192,224},{224,1... | collective-permute-start | bytes 2359304 | tf_op jit(solution)/shard_map/ppermute | solution.py:41
  153.0 8.6 %collective-permute-start.30 = (bf16[512,768]{1,0:T(8,128)(2,1)}, bf16[512,768]{1,0:T(8,128)(2,1)S(1)}, u32[]{:S(2)}, u32[]{:S(2)}) collective-permute-start(bf16[512,768]{1,0:T(8,128)(2,1)} %get-tuple-element.54), channel_id=1, source_target_pairs={{0,32},{32,0},{64,96},{96,64},{128,160},{160,128},{192,224},{224,1... | collective-permute-start | bytes 2359304 | tf_op jit(solution)/shard_map/ppermute | solution.py:41
  161.6 1.1 copy-start.2
  169.4 20.6 %collective-permute-start.22 = (bf16[64,2048]{1,0:T(8,128)(2,1)S(1)}, bf16[64,2048]{1,0:T(8,128)(2,1)S(1)}, u32[]{:S(2)}, u32[]{:S(2)}) collective-permute-start(bf16[64,2048]{1,0:T(8,128)(2,1)S(1)} %get-tuple-element.45), channel_id=1, source_target_pairs={{0,16},{1,17},{2,18},{3,19},{4,20},{5,21},{6,22},{7,23},{8,24},{9,... | collective-permute-start | bytes 786440 | tf_op jit(solution)/shard_map/ppermute | solution.py:456
  177.6 29.6 %all-to-all-start.5 = ((bf16[8,16,2048]{2,1,0:T(8,128)(2,1)}), bf16[8,16,2048]{2,1,0:T(8,128)(2,1)S(1)}, u32[]{:S(2)}, u32[]{:S(2)}) async-start(bf16[8,16,2048]{2,1,0:T(8,128)(2,1)} %bitcast.16), calls=%async_computation.5 | async-start | bytes 1048576 | tf_op jit(solution)/shard_map/all_to_all | solution.py:46
  190.6 6.0 %collective-permute-start.31 = (bf16[16,2048]{1,0:T(8,128)(2,1)S(1)}, bf16[16,2048]{1,0:T(8,128)(2,1)S(1)}, u32[]{:S(2)}, u32[]{:S(2)}) collective-permute-start(bf16[16,2048]{1,0:T(8,128)(2,1)S(1)} %get-tuple-element.59), channel_id=1, source_target_pairs={{0,28},{1,29},{2,30},{3,31},{4,0},{5,1},{6,2},{7,3},{8,4},{9,5},{1... | collective-permute-start | bytes 196616 | tf_op jit(solution)/shard_map/ppermute | solution.py:460
  193.3 6.3 %collective-permute-start.32 = (bf16[16,2048]{1,0:T(8,128)(2,1)S(1)}, bf16[16,2048]{1,0:T(8,128)(2,1)S(1)}, u32[]{:S(2)}, u32[]{:S(2)}) collective-permute-start(bf16[16,2048]{1,0:T(8,128)(2,1)S(1)} %get-tuple-element.60), channel_id=1, source_target_pairs={{0,4},{1,5},{2,6},{3,7},{4,8},{5,9},{6,10},{7,11},{8,12},{9,13},{1... | collective-permute-start | bytes 196616 | tf_op jit(solution)/shard_map/ppermute | solution.py:460
  193.3 8.8 %collective-permute-start.33 = (bf16[16,2048]{1,0:T(8,128)(2,1)S(1)}, bf16[16,2048]{1,0:T(8,128)(2,1)S(1)}, u32[]{:S(2)}, u32[]{:S(2)}) collective-permute-start(bf16[16,2048]{1,0:T(8,128)(2,1)S(1)} %get-tuple-element.61), channel_id=1, source_target_pairs={{0,8},{1,9},{2,10},{3,11},{4,12},{5,13},{6,14},{7,15},{8,16},{9,17... | collective-permute-start | bytes 196616 | tf_op jit(solution)/shard_map/ppermute | solution.py:460
  202.1 4.4 %collective-permute-start.34 = (bf16[16,1024]{1,0:T(8,128)(2,1)S(1)}, bf16[16,1024]{1,0:T(8,128)(2,1)S(1)}, u32[]{:S(2)}, u32[]{:S(2)}) collective-permute-start(bf16[16,1024]{1,0:T(8,128)(2,1)S(1)} %slice.37), channel_id=1, source_target_pairs={{0,32},{32,0},{64,96},{96,64},{128,160},{160,128},{192,224},{224,1... | collective-permute-start | bytes 98312 | tf_op jit(solution)/shard_map/ppermute | solution.py:41
  207.3 1.3 collective-permute-start.35

commit v3 on v2

--- a/solution.py
+++ b/solution.py
@@ -420,7 +420,7 @@
     other_y = jnp.concatenate(gather_blocks(other, "col", Y_STEP), axis=0)
     other_blocks = ring_eight(other_y, "col", Z_UP, Z_DOWN)
     own_z = share(own, "col", Z_GROUPS)
-    own_all = share(after(own_z, other_blocks[1], other_blocks[8]), "col", Y_GROUPS)
+    own_all = share(after(own_z, other_y), "col", Y_GROUPS)
 
     gate_up_term, tok_other = gate_up_product(
         zyx, own_all, other_blocks, gate_own, gate_other, up_own, up_other

time: 212 us -> 208 us (0.981)
  waiting for transfers between devices: 66.5 us -> 59.7 us
  starting transfers between devices: 82.1 us -> 86.3 us
    ppermute x9, waiting for transfers between devices: 21.6 us -> 9.98 us  [gather_blocks(): lax.ppermute(own, axis, steps[count - k])]
    ppermute x12, starting transfers between devices: 15.8 us -> 24.3 us  [swap_core(): return lax.ppermute(value, 'row', CORE_PAIRS)]
    ppermute x3, waiting for transfers between devices: 7.62 us -> 11.4 us  [body(): mixed_sum += lax.ppermute(block, 'col', Z_STEP[step]).astype(F32)]
    ppermute x1, waiting for transfers between devices: 0.01 us -> 2.65 us  [body(): lax.ppermute(far, 'col', Z_STEP[4])]
    ppermute x1, starting transfers between devices: 2.22 us -> 0.09 us  [body(): lax.ppermute(far, 'col', Z_STEP[4])]
  transfers between devices with their start and end apart: 42 -> 42, of which waited for: 23 -> 21; matrix products, arithmetic and copies ran while one was open for 9% -> 10% of each run, Pallas kernels for 14% -> 14%
where the time goes in v3:
time: 208 us; the launch traced here: 207 us
  starting transfers between devices  86.3 us (41%)
  waiting for transfers between devices  59.7 us (29%)
  Pallas kernels  35.1 us (17%)
  matrix products  13.4 us (6%)
  local copies, waits for them, and re-layouts  7.34 us (4%)
  other arithmetic  3.98 us (2%)
    all_to_all x6, starting transfers between devices, exchange(): lax.all_to_all(value, axis, 0, 0, axis_index_groups=groups, tiled=True)  33.5 us
    ppermute x12, starting transfers between devices, swap_core(): return lax.ppermute(value, 'row', CORE_PAIRS)  24.3 us
    all_to_all x6, waiting for transfers between devices, exchange(): lax.all_to_all(value, axis, 0, 0, axis_index_groups=groups, tiled=True)  13.7 us
    dot_general x3, matrix products, dot(): return lax.dot_general(left, right, dims, preferred_element_type=F32)  13.4 us
    ppermute x3, waiting for transfers between devices, ring_eight(): before.append(lax.ppermute(before[-1], axis, up))  12 us
    ppermute x3, waiting for transfers between devices, body(): mixed_sum += lax.ppermute(block, 'col', Z_STEP[step]).astype(F32)  11.4 us
    ppermute x9, starting transfers between devices, gather_blocks(): lax.ppermute(own, axis, steps[count - k])  11.2 us
    ppermute x9, waiting for transfers between devices, gather_blocks(): lax.ppermute(own, axis, steps[count - k])  9.98 us
  transfers between devices with their start and end apart: 42, of which 21 were waited for; matrix products, arithmetic and copies ran while one was open for 10% of the time, Pallas kernels for 14%

profile of v3, /device:TPU:1, one launch (start us, length us, event | category | flops | bytes accessed | tf_op | source)
XLA Modules:
  0.0 206.6 jit_solution(17127645838645586642)
XLA Ops:
  0.7 0.8 constant_dynamic-slice_fusion.1
  1.4 0.8 constant_dynamic-slice_fusion
  2.2 0.8 tile.4
  3.1 9.0 %all-to-all-start = ((bf16[8,16,2048]{2,1,0:T(8,128)(2,1)}), bf16[8,16,2048]{2,1,0:T(8,128)(2,1)S(1)}, u32[]{:S(2)}, u32[]{:S(2)}) async-start(bf16[8,16,2048]{2,1,0:T(8,128)(2,1)} %tile.4), calls=%async_computation | async-start | bytes 1048576 | tf_op jit(solution)/shard_map/all_to_all | solution.py:46
  12.1 1.0 collective-permute-start
  13.1 0.8 collective-permute-done
  14.3 1.3 collective-permute-start.4
  15.6 2.6 %collective-permute-start.3 = (bf16[16,2048]{1,0:T(8,128)(2,1)S(1)}, bf16[16,2048]{1,0:T(8,128)(2,1)S(1)}, u32[]{:S(2)}, u32[]{:S(2)}) collective-permute-start(bf16[16,2048]{1,0:T(8,128)(2,1)S(1)} %constant_dynamic-update-slice_fusion), channel_id=1, source_target_pairs={{0,2},{1,3},{2,0},{3,1},{4,6},{5,7},{6,4},{7,5},{8,10},{9,11},{10,... | collective-permute-start | bytes 196616 | tf_op jit(solution)/shard_map/ppermute | solution.py:61
  18.2 1.1 collective-permute-start.2
  19.2 1.0 collective-permute-start.17
  20.3 1.4 collective-permute-done.3
  21.7 8.4 %all-to-all-done = bf16[8,16,2048]{2,1,0:T(8,128)(2,1)S(1)} async-done(((bf16[8,16,2048]{2,1,0:T(8,128)(2,1)}), bf16[8,16,2048]{2,1,0:T(8,128)(2,1)S(1)}, u32[]{:S(2)}, u32[]{:S(2)}) %all-to-all-start) | async-done | bytes 524320 | tf_op jit(solution)/shard_map/all_to_all | solution.py:46
  30.0 1.6 tile.5
  31.7 4.2 %all-to-all-start.1 = ((bf16[4,128,2048]{2,1,0:T(8,128)(2,1)}), bf16[4,128,2048]{2,1,0:T(8,128)(2,1)S(1)}, u32[]{:S(2)}, u32[]{:S(2)}) async-start(bf16[4,128,2048]{2,1,0:T(8,128)(2,1)} %tile.5), calls=%async_computation.1 | async-start | bytes 4194304 | tf_op jit(solution)/shard_map/all_to_all | solution.py:46
  35.9 2.7 %collective-permute-start.5 = (bf16[64,2048]{1,0:T(8,128)(2,1)S(1)}, bf16[64,2048]{1,0:T(8,128)(2,1)S(1)}, u32[]{:S(2)}, u32[]{:S(2)}) collective-permute-start(bf16[64,2048]{1,0:T(8,128)(2,1)S(1)} %pad_maximum_fusion.4.refs_0_), channel_id=1, source_target_pairs={{4,0},{5,1},{6,2},{7,3},{8,4},{9,5},{10,6},{11,7},{12,8},{13,9},{1... | collective-permute-start | bytes 786440 | tf_op jit(solution)/shard_map/ppermute | solution.py:69
  38.5 5.6 %collective-permute-done.8.refs_8_ = bf16[64,2048]{1,0:T(8,128)(2,1)S(1)} collective-permute-done((bf16[64,2048]{1,0:T(8,128)(2,1)S(1)}, bf16[64,2048]{1,0:T(8,128)(2,1)S(1)}, u32[]{:S(2)}, u32[]{:S(2)}) %collective-permute-start.8) | collective-permute-done | bytes 262176 | tf_op jit(solution)/shard_map/ppermute | solution.py:68
  44.1 2.7 %collective-permute-start.6 = (bf16[64,2048]{1,0:T(8,128)(2,1)S(1)}, bf16[64,2048]{1,0:T(8,128)(2,1)S(1)}, u32[]{:S(2)}, u32[]{:S(2)}) collective-permute-start(bf16[64,2048]{1,0:T(8,128)(2,1)S(1)} %collective-permute-done.5.refs_1_), channel_id=1, source_target_pairs={{4,0},{5,1},{6,2},{7,3},{8,4},{9,5},{10,6},{11,7},{12,8},{13,9},{1... | collective-permute-start | bytes 786440 | tf_op jit(solution)/shard_map/ppermute | solution.py:69
  46.8 2.2 %collective-permute-start.13 = (bf16[768,1024]{1,0:T(8,128)(2,1)}, bf16[768,1024]{1,0:T(8,128)(2,1)}, u32[]{:S(2)}, u32[]{:S(2)}) collective-permute-start(bf16[768,1024]{1,0:T(8,128)(2,1)} %refs_4_.2), channel_id=1, source_target_pairs={{0,32},{32,0},{64,96},{96,64},{128,160},{160,128},{192,224},{224,1... | collective-permute-start | bytes 4718600 | tf_op jit(solution)/shard_map/ppermute | solution.py:41
  49.0 2.4 %collective-permute-done.9.refs_7_ = bf16[64,2048]{1,0:T(8,128)(2,1)S(1)} collective-permute-done((bf16[64,2048]{1,0:T(8,128)(2,1)S(1)}, bf16[64,2048]{1,0:T(8,128)(2,1)S(1)}, u32[]{:S(2)}, u32[]{:S(2)}) %collective-permute-start.9) | collective-permute-done | bytes 262176 | tf_op jit(solution)/shard_map/ppermute | solution.py:68
  51.5 0.7 copy-done
  52.2 2.0 collective-permute-start.7
  54.2 4.0 %collective-permute-done.10.refs_6_ = bf16[64,2048]{1,0:T(8,128)(2,1)S(1)} collective-permute-done((bf16[64,2048]{1,0:T(8,128)(2,1)S(1)}, bf16[64,2048]{1,0:T(8,128)(2,1)S(1)}, u32[]{:S(2)}, u32[]{:S(2)}) %collective-permute-start.10) | collective-permute-done | bytes 262176 | tf_op jit(solution)/shard_map/ppermute | solution.py:68
  59.5 2.7 %collective-permute-start.12 = (bf16[32,2048]{1,0:T(8,128)(2,1)}, bf16[32,2048]{1,0:T(8,128)(2,1)}, u32[]{:S(2)}, u32[]{:S(2)}) collective-permute-start(bf16[32,2048]{1,0:T(8,128)(2,1)} %slice.33), channel_id=1, source_target_pairs={{4,0},{5,1},{6,2},{7,3},{8,4},{9,5},{10,6},{11,7},{12,8},{13,9},{1... | collective-permute-start | bytes 393224 | tf_op jit(solution)/shard_map/ppermute | solution.py:71
  62.3 1.8 collective-permute-done.11.refs_4_
  64.5 7.4 %shard_map.93 = (bf16[512,1536]{1,0:T(8,128)(2,1)}, bf16[512,1024]{1,0:T(8,128)(2,1)}) custom-call(s32[3]{0:T(128)S(1)} %pad_add_fusion.index, bf16[512,2048]{1,0:T(8,128)(2,1)S(1)} %bitcast.10, bf16[64,2048]{1,0:T(8,128)(2,1)S(1)} %pad_maximum_fusion.4.refs_0_, bf16[64,2048]{1,0:T(8,128)(2,1)S(1)} %collective-permute-done.5.refs_1_, ...), custom_call_target="tpu_custom_call" | custom-call | flops 3221225472 | bytes 10485760 | tf_op jit(solution)/shard_map/pallas_call | solution.py:148
  71.9 4.3 %all-to-all-start.2 = ((bf16[4,128,1536]{2,1,0:T(8,128)(2,1)}), bf16[4,128,1536]{2,1,0:T(8,128)(2,1)}, u32[]{:S(2)}, u32[]{:S(2)}) async-start(bf16[4,128,1536]{2,1,0:T(8,128)(2,1)} %bitcast.17), calls=%async_computation.2 | async-start | bytes 3145728 | tf_op jit(solution)/shard_map/all_to_all | solution.py:46
  76.2 5.5 %shard_map.92 = (bf16[128,768]{1,0:T(8,128)(2,1)}, bf16[128,768]{1,0:T(8,128)(2,1)}, bf16[128,768]{1,0:T(8,128)(2,1)}, bf16[128,768]{1,0:T(8,128)(2,1)}, bf16[512,1024]{1,0:T(8,128)(2,1)}) custom-call(s32[3]{0:T(128)S(1)} %pad_add_fusion.index, bf16[512,2048]{1,0:T(8,128)(2,1)S(1)} %bitcast.11, bf16[64,2048]{1,0:T(8,128)(2,1)S(1)} %pad_maximum_fusion.4.refs_0_, ...), custom_call_target="tpu_custom_call" | custom-call | flops 1610612736 | bytes 10485760 | tf_op jit(solution)/shard_map/pallas_call | solution.py:184
  81.8 1.4 collective-permute-start.14
  83.2 2.4 %collective-permute-start.15 = (bf16[128,768]{1,0:T(8,128)(2,1)}, bf16[128,768]{1,0:T(8,128)(2,1)S(1)}, u32[]{:S(2)}, u32[]{:S(2)}) collective-permute-start(bf16[128,768]{1,0:T(8,128)(2,1)} %get-tuple-element.37), channel_id=1, source_target_pairs={{0,128},{32,160},{64,192},{96,224},{128,0},{160,32},{192,64},{224,... | collective-permute-start | bytes 589832 | tf_op jit(solution)/shard_map/ppermute | solution.py:433
  85.6 1.2 collective-permute-start.16
  86.8 5.3 %all-to-all-done.2.terms = bf16[4,128,1536]{2,1,0:T(8,128)(2,1)} async-done(((bf16[4,128,1536]{2,1,0:T(8,128)(2,1)}), bf16[4,128,1536]{2,1,0:T(8,128)(2,1)}, u32[]{:S(2)}, u32[]{:S(2)}) %all-to-all-start.2) | async-done | bytes 1572896 | tf_op jit(solution)/shard_map/all_to_all | solution.py:46
  92.2 2.5 %shard_map.94 = (f32[128,1536]{1,0:T(8,128)}, bf16[128,768]{1,0:T(8,128)(2,1)S(1)}) custom-call(s32[1]{0:T(128)} %bitcast.2.index, bf16[4,128,1536]{2,1,0:T(8,128)(2,1)} %all-to-all-done.2.terms), custom_call_target="tpu_custom_call" | custom-call | flops 3145728 | bytes 10485760 | tf_op jit(solution)/shard_map/pallas_call | solution.py:282
  94.9 1.8 collective-permute-start.20
  97.3 3.6 %collective-permute-done.15.refs_2_ = bf16[128,768]{1,0:T(8,128)(2,1)S(1)} collective-permute-done((bf16[128,768]{1,0:T(8,128)(2,1)}, bf16[128,768]{1,0:T(8,128)(2,1)S(1)}, u32[]{:S(2)}, u32[]{:S(2)}) %collective-permute-start.15) | collective-permute-done | bytes 196640 | tf_op jit(solution)/shard_map/ppermute | solution.py:433
  100.9 1.5 shard_map.95.refs_0_
  102.4 4.0 %collective-permute-done.21.refs_3_ = bf16[128,768]{1,0:T(8,128)(2,1)S(1)} collective-permute-done((bf16[128,768]{1,0:T(8,128)(2,1)S(1)}, bf16[128,768]{1,0:T(8,128)(2,1)S(1)}, u32[]{:S(2)}, u32[]{:S(2)}) %collective-permute-start.21) | collective-permute-done | bytes 196640 | tf_op jit(solution)/shard_map/ppermute | solution.py:61
  106.4 2.8 %collective-permute-done.20.refs_2_ = bf16[128,768]{1,0:T(8,128)(2,1)S(1)} collective-permute-done((bf16[128,768]{1,0:T(8,128)(2,1)S(1)}, bf16[128,768]{1,0:T(8,128)(2,1)S(1)}, u32[]{:S(2)}, u32[]{:S(2)}) %collective-permute-start.20) | collective-permute-done | bytes 196640 | tf_op jit(solution)/shard_map/ppermute | solution.py:61
  109.2 5.2 %shard_map.96 = (bf16[512,2048]{1,0:T(8,128)(2,1)}, bf16[512,768]{1,0:T(8,128)(2,1)}) custom-call(s32[1]{0:T(128)} %bitcast.2.index, bf16[128,768]{1,0:T(8,128)(2,1)S(1)} %get-tuple-element.42.refs_0_, bf16[128,768]{1,0:T(8,128)(2,1)S(1)} %collective-permute-done.19.refs_1_, bf16[128,768]{1,0:T(8,128)(2,1)S(1)} %collective-permute-done.20.refs_2_, ...), custom_call_target="tpu_custom_call" | custom-call | flops 1610612736 | bytes 10485760 | tf_op jit(solution)/shard_map/pallas_call | solution.py:217
  114.4 4.5 %all-to-all-start.3 = ((bf16[4,128,2048]{2,1,0:T(8,128)(2,1)}), bf16[4,128,2048]{2,1,0:T(8,128)(2,1)}, u32[]{:S(2)}, u32[]{:S(2)}) async-start(bf16[4,128,2048]{2,1,0:T(8,128)(2,1)} %bitcast.15), calls=%async_computation.3 | async-start | bytes 4194304 | tf_op jit(solution)/shard_map/all_to_all | solution.py:46
  118.9 1.0 collective-permute-start.26
  119.9 1.0 collective-permute-start.25
  121.0 1.4 collective-permute-start.24
  122.4 8.7 %collective-permute-start.29 = (bf16[512,1024]{1,0:T(8,128)(2,1)}, bf16[512,1024]{1,0:T(8,128)(2,1)}, u32[]{:S(2)}, u32[]{:S(2)}) collective-permute-start(bf16[512,1024]{1,0:T(8,128)(2,1)} %get-tuple-element.53), channel_id=1, source_target_pairs={{0,32},{32,0},{64,96},{96,64},{128,160},{160,128},{192,224},{224,1... | collective-permute-start | bytes 3145736 | tf_op jit(solution)/shard_map/ppermute | solution.py:41
  131.2 0.8 collective-permute-done.26.refs_3_
  131.9 1.0 collective-permute-done.24.refs_1_
  132.9 7.2 %shard_map.98 = (bf16[512,2048]{1,0:T(8,128)(2,1)}, bf16[512,768]{1,0:T(8,128)(2,1)}, bf16[512,768]{1,0:T(8,128)(2,1)}) custom-call(s32[1]{0:T(128)} %bitcast.2.index, bf16[128,1536]{1,0:T(8,128)(2,1)S(1)} %shard_map.95.refs_0_, bf16[128,1536]{1,0:T(8,128)(2,1)S(1)} %collective-permute-done.24.refs_1_, ...), custom_call_target="tpu_custom_call" | custom-call | flops 3221225472 | bytes 10485760 | tf_op jit(solution)/shard_map/pallas_call | solution.py:253
  140.1 4.5 %all-to-all-start.4 = ((bf16[4,128,2048]{2,1,0:T(8,128)(2,1)}), bf16[4,128,2048]{2,1,0:T(8,128)(2,1)}, u32[]{:S(2)}, u32[]{:S(2)}) async-start(bf16[4,128,2048]{2,1,0:T(8,128)(2,1)} %bitcast.14), calls=%async_computation.4 | async-start | bytes 4194304 | tf_op jit(solution)/shard_map/all_to_all | solution.py:46
  144.6 8.0 %collective-permute-start.28 = (bf16[512,768]{1,0:T(8,128)(2,1)}, bf16[512,768]{1,0:T(8,128)(2,1)S(1)}, u32[]{:S(2)}, u32[]{:S(2)}) collective-permute-start(bf16[512,768]{1,0:T(8,128)(2,1)} %get-tuple-element.52), channel_id=1, source_target_pairs={{0,32},{32,0},{64,96},{96,64},{128,160},{160,128},{192,224},{224,1... | collective-permute-start | bytes 2359304 | tf_op jit(solution)/shard_map/ppermute | solution.py:41
  153.4 1.3 collective-permute-done.28
  154.7 4.5 %fusion.4 = bf16[768,1024]{1,0:T(8,128)(2,1)} fusion(bf16[512,1024]{1,0:T(8,128)(2,1)} %collective-permute-done.29, bf16[512,1024]{1,0:T(8,128)(2,1)S(1)} %get-tuple-element.64, bf16[512,768]{1,0:T(8,128)(2,1)S(1)} %collective-permute-done.28, bf16[512,768]{1,0:T(8,128)(2,1)} %get-tuple-element.52), kind=kOutput, calls=%fused_computation.5 | convolution fusion | flops 1618739200 | bytes 5242880 | tf_op jit(solution)/shard_map/dot_general | solution.py:37
  159.2 2.5 %pad_maximum_fusion.1 = bf16[1024,768]{1,0:T(8,128)(2,1)} fusion(bf16[512,768]{1,0:T(8,128)(2,1)S(1)} %collective-permute-done.27, bf16[512,768]{1,0:T(8,128)(2,1)} %get-tuple-element.49), kind=kLoop, calls=%fused_computation.8 | loop fusion | flops 3145728 | bytes 3145728 | tf_op jit(solution)/shard_map/concatenate | solution.py:446
  161.7 1.1 copy-done.2
  162.7 4.2 %convolution_convert_fusion.1 = bf16[1024,768]{1,0:T(8,128)(2,1)} fusion(bf16[512,768]{1,0:T(8,128)(2,1)S(1)} %collective-permute-done.30, bf16[512,768]{1,0:T(8,128)(2,1)} %get-tuple-element.54, bf16[512,1024]{1,0:T(8,128)(2,1)S(1)} %collective-permute-done.23, bf16[512,1024]{1,0:T(8,128)(2,1)S(1)} %get-tuple-element.63), kind=kOutput, calls=%fused_computation.7 | convolution fusion | flops 1618739200 | bytes 5242880 | tf_op jit(solution)/shard_map/dot_general | solution.py:37
  166.9 2.5 %shard_map.97 = (bf16[64,2048]{1,0:T(8,128)(2,1)S(1)}, bf16[64,2048]{1,0:T(8,128)(2,1)S(1)}) custom-call(s32[3]{0:T(128)S(1)} %pad_add_fusion.index, bf16[4,128,2048]{2,1,0:T(8,128)(2,1)} %all-to-all-done.3.terms), custom_call_target="tpu_custom_call" | custom-call | flops 2097152 | bytes 10485760 | tf_op jit(solution)/shard_map/pallas_call | solution.py:360
  169.6 2.7 %shard_map.99 = bf16[128,2048]{1,0:T(8,128)(2,1)} custom-call(s32[1]{0:T(128)} %bitcast.2.index, bf16[4,128,2048]{2,1,0:T(8,128)(2,1)} %all-to-all-done.4.terms), custom_call_target="tpu_custom_call" | custom-call | flops 2097152 | bytes 10485760 | tf_op jit(solution)/shard_map/pallas_call | solution.py:338
  172.2 7.0 %all-to-all-start.5 = ((bf16[8,16,2048]{2,1,0:T(8,128)(2,1)}), bf16[8,16,2048]{2,1,0:T(8,128)(2,1)S(1)}, u32[]{:S(2)}, u32[]{:S(2)}) async-start(bf16[8,16,2048]{2,1,0:T(8,128)(2,1)} %bitcast.16), calls=%async_computation.5 | async-start | bytes 1048576 | tf_op jit(solution)/shard_map/all_to_all | solution.py:46
  179.2 4.7 %convolution_convert_fusion = bf16[1024,768]{1,0:T(8,128)(2,1)} fusion(bf16[1024,768]{1,0:T(8,128)(2,1)} %pad_maximum_fusion.1, bf16[512,1024]{1,0:T(8,128)(2,1)} %copy-done.2, bf16[512,1024]{1,0:T(8,128)(2,1)S(1)} %get-tuple-element.63), kind=kOutput, calls=%fused_computation.6 | convolution fusion | flops 1615593472 | bytes 5242880 | tf_op jit(solution)/shard_map/dot_general | solution.py:37
  184.0 2.6 %collective-permute-done.22.far = bf16[64,2048]{1,0:T(8,128)(2,1)S(1)} collective-permute-done((bf16[64,2048]{1,0:T(8,128)(2,1)S(1)}, bf16[64,2048]{1,0:T(8,128)(2,1)S(1)}, u32[]{:S(2)}, u32[]{:S(2)}) %collective-permute-start.22) | collective-permute-done | bytes 262176 | tf_op jit(solution)/shard_map/ppermute | solution.py:456
  187.2 2.0 collective-permute-start.31
  189.3 9.6 %collective-permute-done.31 = bf16[16,2048]{1,0:T(8,128)(2,1)S(1)} collective-permute-done((bf16[16,2048]{1,0:T(8,128)(2,1)S(1)}, bf16[16,2048]{1,0:T(8,128)(2,1)S(1)}, u32[]{:S(2)}, u32[]{:S(2)}) %collective-permute-start.31) | collective-permute-done | bytes 65568 | tf_op jit(solution)/shard_map/ppermute | solution.py:460
  198.9 1.8 collective-permute-done.33
  200.7 2.3 %collective-permute-start.34 = (bf16[16,1024]{1,0:T(8,128)(2,1)S(1)}, bf16[16,1024]{1,0:T(8,128)(2,1)S(1)}, u32[]{:S(2)}, u32[]{:S(2)}) collective-permute-start(bf16[16,1024]{1,0:T(8,128)(2,1)S(1)} %slice.37), channel_id=1, source_target_pairs={{0,32},{32,0},{64,96},{96,64},{128,160},{160,128},{192,224},{224,1... | collective-permute-start | bytes 98312 | tf_op jit(solution)/shard_map/ppermute | solution.py:41
  203.1 0.9 collective-permute-done.34
  205.1 0.9 collective-permute-done.35
  (59 shorter events, 6.6 us)
Async XLA Ops:
  3.1 27.0 %all-to-all-start = ((bf16[8,16,2048]{2,1,0:T(8,128)(2,1)}), bf16[8,16,2048]{2,1,0:T(8,128)(2,1)S(1)}, u32[]{:S(2)}, u32[]{:S(2)}) async-start(bf16[8,16,2048]{2,1,0:T(8,128)(2,1)} %tile.4), calls=%async_computation | async-start | bytes 1048576 | tf_op jit(solution)/shard_map/all_to_all | solution.py:46
  12.1 1.8 collective-permute-start
  13.0 1.2 collective-permute-start.1
  14.3 6.0 %collective-permute-start.4 = (bf16[16,2048]{1,0:T(8,128)(2,1)S(1)}, bf16[16,2048]{1,0:T(8,128)(2,1)S(1)}, u32[]{:S(2)}, u32[]{:S(2)}) collective-permute-start(bf16[16,2048]{1,0:T(8,128)(2,1)S(1)} %constant_dynamic-update-slice_fusion), channel_id=1, source_target_pairs={{0,1},{1,2},{2,3},{3,0},{4,5},{5,6},{6,7},{7,4},{8,9},{9,10},{10,1... | collective-permute-start | bytes 196616 | tf_op jit(solution)/shard_map/ppermute | solution.py:61
  15.6 6.1 %collective-permute-start.3 = (bf16[16,2048]{1,0:T(8,128)(2,1)S(1)}, bf16[16,2048]{1,0:T(8,128)(2,1)S(1)}, u32[]{:S(2)}, u32[]{:S(2)}) collective-permute-start(bf16[16,2048]{1,0:T(8,128)(2,1)S(1)} %constant_dynamic-update-slice_fusion), channel_id=1, source_target_pairs={{0,2},{1,3},{2,0},{3,1},{4,6},{5,7},{6,4},{7,5},{8,10},{9,11},{10,... | collective-permute-start | bytes 196616 | tf_op jit(solution)/shard_map/ppermute | solution.py:61
  18.2 3.5 %collective-permute-start.2 = (bf16[16,2048]{1,0:T(8,128)(2,1)S(1)}, bf16[16,2048]{1,0:T(8,128)(2,1)S(1)}, u32[]{:S(2)}, u32[]{:S(2)}) collective-permute-start(bf16[16,2048]{1,0:T(8,128)(2,1)S(1)} %constant_dynamic-update-slice_fusion), channel_id=1, source_target_pairs={{0,3},{1,0},{2,1},{3,2},{4,7},{5,4},{6,5},{7,6},{8,11},{9,8},{10,9... | collective-permute-start | bytes 196616 | tf_op jit(solution)/shard_map/ppermute | solution.py:61
  19.2 45.2 %collective-permute-start.17 = (bf16[1024,768]{1,0:T(8,128)(2,1)}, bf16[1024,768]{1,0:T(8,128)(2,1)}, u32[]{:S(2)}, u32[]{:S(2)}) collective-permute-start(bf16[1024,768]{1,0:T(8,128)(2,1)} %refs_4_.3), channel_id=1, source_target_pairs={{0,32},{32,0},{64,96},{96,64},{128,160},{160,128},{192,224},{224,1... | collective-permute-start | bytes 4718600 | tf_op jit(solution)/shard_map/ppermute | solution.py:41
  20.2 44.2 %collective-permute-start.18 = (bf16[1024,768]{1,0:T(8,128)(2,1)}, bf16[1024,768]{1,0:T(8,128)(2,1)}, u32[]{:S(2)}, u32[]{:S(2)}) collective-permute-start(bf16[1024,768]{1,0:T(8,128)(2,1)} %refs_5_.1), channel_id=1, source_target_pairs={{0,32},{32,0},{64,96},{96,64},{128,160},{160,128},{192,224},{224,1... | collective-permute-start | bytes 4718600 | tf_op jit(solution)/shard_map/ppermute | solution.py:41
  31.7 32.8 %all-to-all-start.1 = ((bf16[4,128,2048]{2,1,0:T(8,128)(2,1)}), bf16[4,128,2048]{2,1,0:T(8,128)(2,1)S(1)}, u32[]{:S(2)}, u32[]{:S(2)}) async-start(bf16[4,128,2048]{2,1,0:T(8,128)(2,1)} %tile.5), calls=%async_computation.1 | async-start | bytes 4194304 | tf_op jit(solution)/shard_map/all_to_all | solution.py:46
  35.9 8.3 %collective-permute-start.8 = (bf16[64,2048]{1,0:T(8,128)(2,1)S(1)}, bf16[64,2048]{1,0:T(8,128)(2,1)S(1)}, u32[]{:S(2)}, u32[]{:S(2)}) collective-permute-start(bf16[64,2048]{1,0:T(8,128)(2,1)S(1)} %pad_maximum_fusion.4.refs_0_), channel_id=1, source_target_pairs={{0,4},{1,5},{2,6},{3,7},{4,8},{5,9},{6,10},{7,11},{8,12},{9,13},{1... | collective-permute-start | bytes 786440 | tf_op jit(solution)/shard_map/ppermute | solution.py:68
  35.9 8.3 %collective-permute-start.5 = (bf16[64,2048]{1,0:T(8,128)(2,1)S(1)}, bf16[64,2048]{1,0:T(8,128)(2,1)S(1)}, u32[]{:S(2)}, u32[]{:S(2)}) collective-permute-start(bf16[64,2048]{1,0:T(8,128)(2,1)S(1)} %pad_maximum_fusion.4.refs_0_), channel_id=1, source_target_pairs={{4,0},{5,1},{6,2},{7,3},{8,4},{9,5},{10,6},{11,7},{12,8},{13,9},{1... | collective-permute-start | bytes 786440 | tf_op jit(solution)/shard_map/ppermute | solution.py:69
  44.1 7.3 %collective-permute-start.9 = (bf16[64,2048]{1,0:T(8,128)(2,1)S(1)}, bf16[64,2048]{1,0:T(8,128)(2,1)S(1)}, u32[]{:S(2)}, u32[]{:S(2)}) collective-permute-start(bf16[64,2048]{1,0:T(8,128)(2,1)S(1)} %collective-permute-done.8.refs_8_), channel_id=1, source_target_pairs={{0,4},{1,5},{2,6},{3,7},{4,8},{5,9},{6,10},{7,11},{8,12},{9,13},{1... | collective-permute-start | bytes 786440 | tf_op jit(solution)/shard_map/ppermute | solution.py:68
  44.1 7.3 %collective-permute-start.6 = (bf16[64,2048]{1,0:T(8,128)(2,1)S(1)}, bf16[64,2048]{1,0:T(8,128)(2,1)S(1)}, u32[]{:S(2)}, u32[]{:S(2)}) collective-permute-start(bf16[64,2048]{1,0:T(8,128)(2,1)S(1)} %collective-permute-done.5.refs_1_), channel_id=1, source_target_pairs={{4,0},{5,1},{6,2},{7,3},{8,4},{9,5},{10,6},{11,7},{12,8},{13,9},{1... | collective-permute-start | bytes 786440 | tf_op jit(solution)/shard_map/ppermute | solution.py:69
  46.8 29.4 %collective-permute-start.13 = (bf16[768,1024]{1,0:T(8,128)(2,1)}, bf16[768,1024]{1,0:T(8,128)(2,1)}, u32[]{:S(2)}, u32[]{:S(2)}) collective-permute-start(bf16[768,1024]{1,0:T(8,128)(2,1)} %refs_4_.2), channel_id=1, source_target_pairs={{0,32},{32,0},{64,96},{96,64},{128,160},{160,128},{192,224},{224,1... | collective-permute-start | bytes 4718600 | tf_op jit(solution)/shard_map/ppermute | solution.py:41
  51.5 0.7 copy-start
  51.5 6.7 %collective-permute-start.10 = (bf16[64,2048]{1,0:T(8,128)(2,1)S(1)}, bf16[64,2048]{1,0:T(8,128)(2,1)S(1)}, u32[]{:S(2)}, u32[]{:S(2)}) collective-permute-start(bf16[64,2048]{1,0:T(8,128)(2,1)S(1)} %collective-permute-done.9.refs_7_), channel_id=1, source_target_pairs={{0,4},{1,5},{2,6},{3,7},{4,8},{5,9},{6,10},{7,11},{8,12},{9,13},{1... | collective-permute-start | bytes 786440 | tf_op jit(solution)/shard_map/ppermute | solution.py:68
  52.2 6.7 %copy-start.1 = (bf16[64,2048]{1,0:T(8,128)(2,1)}, bf16[64,2048]{1,0:T(8,128)(2,1)S(1)}, u32[]{:S(2)}) copy-start(bf16[64,2048]{1,0:T(8,128)(2,1)S(1)} %collective-permute-done.6.refs_2_) | copy-start | bytes 786436
  52.2 6.7 %collective-permute-start.7 = (bf16[64,2048]{1,0:T(8,128)(2,1)S(1)}, bf16[64,2048]{1,0:T(8,128)(2,1)S(1)}, u32[]{:S(2)}, u32[]{:S(2)}) collective-permute-start(bf16[64,2048]{1,0:T(8,128)(2,1)S(1)} %collective-permute-done.6.refs_2_), channel_id=1, source_target_pairs={{4,0},{5,1},{6,2},{7,3},{8,4},{9,5},{10,6},{11,7},{12,8},{13,9},{1... | collective-permute-start | bytes 786440 | tf_op jit(solution)/shard_map/ppermute | solution.py:69
  58.9 5.2 %collective-permute-start.11 = (bf16[32,2048]{1,0:T(8,128)(2,1)}, bf16[32,2048]{1,0:T(8,128)(2,1)S(1)}, u32[]{:S(2)}, u32[]{:S(2)}) collective-permute-start(bf16[32,2048]{1,0:T(8,128)(2,1)} %slice.32), channel_id=1, source_target_pairs={{0,4},{1,5},{2,6},{3,7},{4,8},{5,9},{6,10},{7,11},{8,12},{9,13},{1... | collective-permute-start | bytes 393224 | tf_op jit(solution)/shard_map/ppermute | solution.py:70
  59.5 4.9 %collective-permute-start.12 = (bf16[32,2048]{1,0:T(8,128)(2,1)}, bf16[32,2048]{1,0:T(8,128)(2,1)}, u32[]{:S(2)}, u32[]{:S(2)}) collective-permute-start(bf16[32,2048]{1,0:T(8,128)(2,1)} %slice.33), channel_id=1, source_target_pairs={{4,0},{5,1},{6,2},{7,3},{8,4},{9,5},{10,6},{11,7},{12,8},{13,9},{1... | collective-permute-start | bytes 393224 | tf_op jit(solution)/shard_map/ppermute | solution.py:71
  71.9 20.3 %all-to-all-start.2 = ((bf16[4,128,1536]{2,1,0:T(8,128)(2,1)}), bf16[4,128,1536]{2,1,0:T(8,128)(2,1)}, u32[]{:S(2)}, u32[]{:S(2)}) async-start(bf16[4,128,1536]{2,1,0:T(8,128)(2,1)} %bitcast.17), calls=%async_computation.2 | async-start | bytes 3145728 | tf_op jit(solution)/shard_map/all_to_all | solution.py:46
  81.8 14.9 %collective-permute-start.14 = (bf16[128,768]{1,0:T(8,128)(2,1)}, bf16[128,768]{1,0:T(8,128)(2,1)S(1)}, u32[]{:S(2)}, u32[]{:S(2)}) collective-permute-start(bf16[128,768]{1,0:T(8,128)(2,1)} %get-tuple-element.36), channel_id=1, source_target_pairs={{0,64},{32,96},{64,128},{96,160},{128,192},{160,224},{192,0},{224,... | collective-permute-start | bytes 589832 | tf_op jit(solution)/shard_map/ppermute | solution.py:433
  83.2 17.7 %collective-permute-start.15 = (bf16[128,768]{1,0:T(8,128)(2,1)}, bf16[128,768]{1,0:T(8,128)(2,1)S(1)}, u32[]{:S(2)}, u32[]{:S(2)}) collective-permute-start(bf16[128,768]{1,0:T(8,128)(2,1)} %get-tuple-element.37), channel_id=1, source_target_pairs={{0,128},{32,160},{64,192},{96,224},{128,0},{160,32},{192,64},{224,... | collective-permute-start | bytes 589832 | tf_op jit(solution)/shard_map/ppermute | solution.py:433
  85.6 15.3 %collective-permute-start.16 = (bf16[128,768]{1,0:T(8,128)(2,1)}, bf16[128,768]{1,0:T(8,128)(2,1)S(1)}, u32[]{:S(2)}, u32[]{:S(2)}) collective-permute-start(bf16[128,768]{1,0:T(8,128)(2,1)} %get-tuple-element.38), channel_id=1, source_target_pairs={{0,192},{32,224},{64,0},{96,32},{128,64},{160,96},{192,128},{224,1... | collective-permute-start | bytes 589832 | tf_op jit(solution)/shard_map/ppermute | solution.py:433
  94.6 11.8 %collective-permute-start.21 = (bf16[128,768]{1,0:T(8,128)(2,1)S(1)}, bf16[128,768]{1,0:T(8,128)(2,1)S(1)}, u32[]{:S(2)}, u32[]{:S(2)}) collective-permute-start(bf16[128,768]{1,0:T(8,128)(2,1)S(1)} %get-tuple-element.42.refs_0_), channel_id=1, source_target_pairs={{0,64},{32,96},{64,128},{96,160},{128,192},{160,224},{192,0},{224,... | collective-permute-start | bytes 589832 | tf_op jit(solution)/shard_map/ppermute | solution.py:61
  94.9 14.3 %collective-permute-start.20 = (bf16[128,768]{1,0:T(8,128)(2,1)S(1)}, bf16[128,768]{1,0:T(8,128)(2,1)S(1)}, u32[]{:S(2)}, u32[]{:S(2)}) collective-permute-start(bf16[128,768]{1,0:T(8,128)(2,1)S(1)} %get-tuple-element.42.refs_0_), channel_id=1, source_target_pairs={{0,128},{32,160},{64,192},{96,224},{128,0},{160,32},{192,64},{224,... | collective-permute-start | bytes 589832 | tf_op jit(solution)/shard_map/ppermute | solution.py:61
  96.7 12.5 %collective-permute-start.19 = (bf16[128,768]{1,0:T(8,128)(2,1)S(1)}, bf16[128,768]{1,0:T(8,128)(2,1)S(1)}, u32[]{:S(2)}, u32[]{:S(2)}) collective-permute-start(bf16[128,768]{1,0:T(8,128)(2,1)S(1)} %get-tuple-element.42.refs_0_), channel_id=1, source_target_pairs={{0,192},{32,224},{64,0},{96,32},{128,64},{160,96},{192,128},{224,1... | collective-permute-start | bytes 589832 | tf_op jit(solution)/shard_map/ppermute | solution.py:61
  114.4 25.7 %all-to-all-start.3 = ((bf16[4,128,2048]{2,1,0:T(8,128)(2,1)}), bf16[4,128,2048]{2,1,0:T(8,128)(2,1)}, u32[]{:S(2)}, u32[]{:S(2)}) async-start(bf16[4,128,2048]{2,1,0:T(8,128)(2,1)} %bitcast.15), calls=%async_computation.3 | async-start | bytes 4194304 | tf_op jit(solution)/shard_map/all_to_all | solution.py:46
  118.9 13.0 %collective-permute-start.26 = (bf16[128,1536]{1,0:T(8,128)(2,1)S(1)}, bf16[128,1536]{1,0:T(8,128)(2,1)S(1)}, u32[]{:S(2)}, u32[]{:S(2)}) collective-permute-start(bf16[128,1536]{1,0:T(8,128)(2,1)S(1)} %shard_map.95.refs_0_), channel_id=1, source_target_pairs={{0,64},{32,96},{64,128},{96,160},{128,192},{160,224},{192,0},{224,... | collective-permute-start | bytes 1179656 | tf_op jit(solution)/shard_map/ppermute | solution.py:61
  119.9 12.0 %collective-permute-start.25 = (bf16[128,1536]{1,0:T(8,128)(2,1)S(1)}, bf16[128,1536]{1,0:T(8,128)(2,1)S(1)}, u32[]{:S(2)}, u32[]{:S(2)}) collective-permute-start(bf16[128,1536]{1,0:T(8,128)(2,1)S(1)} %shard_map.95.refs_0_), channel_id=1, source_target_pairs={{0,128},{32,160},{64,192},{96,224},{128,0},{160,32},{192,64},{224,... | collective-permute-start | bytes 1179656 | tf_op jit(solution)/shard_map/ppermute | solution.py:61
  121.0 11.9 %collective-permute-start.24 = (bf16[128,1536]{1,0:T(8,128)(2,1)S(1)}, bf16[128,1536]{1,0:T(8,128)(2,1)S(1)}, u32[]{:S(2)}, u32[]{:S(2)}) collective-permute-start(bf16[128,1536]{1,0:T(8,128)(2,1)S(1)} %shard_map.95.refs_0_), channel_id=1, source_target_pairs={{0,192},{32,224},{64,0},{96,32},{128,64},{160,96},{192,128},{224,1... | collective-permute-start | bytes 1179656 | tf_op jit(solution)/shard_map/ppermute | solution.py:61
  122.4 31.0 %collective-permute-start.29 = (bf16[512,1024]{1,0:T(8,128)(2,1)}, bf16[512,1024]{1,0:T(8,128)(2,1)}, u32[]{:S(2)}, u32[]{:S(2)}) collective-permute-start(bf16[512,1024]{1,0:T(8,128)(2,1)} %get-tuple-element.53), channel_id=1, source_target_pairs={{0,32},{32,0},{64,96},{96,64},{128,160},{160,128},{192,224},{224,1... | collective-permute-start | bytes 3145736 | tf_op jit(solution)/shard_map/ppermute | solution.py:41
  140.1 29.4 %all-to-all-start.4 = ((bf16[4,128,2048]{2,1,0:T(8,128)(2,1)}), bf16[4,128,2048]{2,1,0:T(8,128)(2,1)}, u32[]{:S(2)}, u32[]{:S(2)}) async-start(bf16[4,128,2048]{2,1,0:T(8,128)(2,1)} %bitcast.14), calls=%async_computation.4 | async-start | bytes 4194304 | tf_op jit(solution)/shard_map/all_to_all | solution.py:46
  144.6 10.1 %collective-permute-start.28 = (bf16[512,768]{1,0:T(8,128)(2,1)}, bf16[512,768]{1,0:T(8,128)(2,1)S(1)}, u32[]{:S(2)}, u32[]{:S(2)}) collective-permute-start(bf16[512,768]{1,0:T(8,128)(2,1)} %get-tuple-element.52), channel_id=1, source_target_pairs={{0,32},{32,0},{64,96},{96,64},{128,160},{160,128},{192,224},{224,1... | collective-permute-start | bytes 2359304 | tf_op jit(solution)/shard_map/ppermute | solution.py:41
  152.6 9.1 %collective-permute-start.23 = (bf16[512,1024]{1,0:T(8,128)(2,1)}, bf16[512,1024]{1,0:T(8,128)(2,1)S(1)}, u32[]{:S(2)}, u32[]{:S(2)}) collective-permute-start(bf16[512,1024]{1,0:T(8,128)(2,1)} %get-tuple-element.46), channel_id=1, source_target_pairs={{0,32},{32,0},{64,96},{96,64},{128,160},{160,128},{192,224},{224,1... | collective-permute-start | bytes 3145736 | tf_op jit(solution)/shard_map/ppermute | solution.py:41
  152.7 6.5 %collective-permute-start.27 = (bf16[512,768]{1,0:T(8,128)(2,1)}, bf16[512,768]{1,0:T(8,128)(2,1)S(1)}, u32[]{:S(2)}, u32[]{:S(2)}) collective-permute-start(bf16[512,768]{1,0:T(8,128)(2,1)} %get-tuple-element.49), channel_id=1, source_target_pairs={{0,32},{32,0},{64,96},{96,64},{128,160},{160,128},{192,224},{224,1... | collective-permute-start | bytes 2359304 | tf_op jit(solution)/shard_map/ppermute | solution.py:41
  153.1 8.6 %collective-permute-start.30 = (bf16[512,768]{1,0:T(8,128)(2,1)}, bf16[512,768]{1,0:T(8,128)(2,1)S(1)}, u32[]{:S(2)}, u32[]{:S(2)}) collective-permute-start(bf16[512,768]{1,0:T(8,128)(2,1)} %get-tuple-element.54), channel_id=1, source_target_pairs={{0,32},{32,0},{64,96},{96,64},{128,160},{160,128},{192,224},{224,1... | collective-permute-start | bytes 2359304 | tf_op jit(solution)/shard_map/ppermute | solution.py:41
  161.7 1.1 copy-start.2
  169.4 17.2 %collective-permute-start.22 = (bf16[64,2048]{1,0:T(8,128)(2,1)S(1)}, bf16[64,2048]{1,0:T(8,128)(2,1)S(1)}, u32[]{:S(2)}, u32[]{:S(2)}) collective-permute-start(bf16[64,2048]{1,0:T(8,128)(2,1)S(1)} %get-tuple-element.45), channel_id=1, source_target_pairs={{0,16},{1,17},{2,18},{3,19},{4,20},{5,21},{6,22},{7,23},{8,24},{9,... | collective-permute-start | bytes 786440 | tf_op jit(solution)/shard_map/ppermute | solution.py:456
  172.2 32.3 %all-to-all-start.5 = ((bf16[8,16,2048]{2,1,0:T(8,128)(2,1)}), bf16[8,16,2048]{2,1,0:T(8,128)(2,1)S(1)}, u32[]{:S(2)}, u32[]{:S(2)}) async-start(bf16[8,16,2048]{2,1,0:T(8,128)(2,1)} %bitcast.16), calls=%async_computation.5 | async-start | bytes 1048576 | tf_op jit(solution)/shard_map/all_to_all | solution.py:46
  187.2 11.6 %collective-permute-start.31 = (bf16[16,2048]{1,0:T(8,128)(2,1)S(1)}, bf16[16,2048]{1,0:T(8,128)(2,1)S(1)}, u32[]{:S(2)}, u32[]{:S(2)}) collective-permute-start(bf16[16,2048]{1,0:T(8,128)(2,1)S(1)} %get-tuple-element.59), channel_id=1, source_target_pairs={{0,28},{1,29},{2,30},{3,31},{4,0},{5,1},{6,2},{7,3},{8,4},{9,5},{1... | collective-permute-start | bytes 196616 | tf_op jit(solution)/shard_map/ppermute | solution.py:460
  189.3 9.6 %collective-permute-start.32 = (bf16[16,2048]{1,0:T(8,128)(2,1)S(1)}, bf16[16,2048]{1,0:T(8,128)(2,1)S(1)}, u32[]{:S(2)}, u32[]{:S(2)}) collective-permute-start(bf16[16,2048]{1,0:T(8,128)(2,1)S(1)} %get-tuple-element.60), channel_id=1, source_target_pairs={{0,4},{1,5},{2,6},{3,7},{4,8},{5,9},{6,10},{7,11},{8,12},{9,13},{1... | collective-permute-start | bytes 196616 | tf_op jit(solution)/shard_map/ppermute | solution.py:460
  189.3 11.4 %collective-permute-start.33 = (bf16[16,2048]{1,0:T(8,128)(2,1)S(1)}, bf16[16,2048]{1,0:T(8,128)(2,1)S(1)}, u32[]{:S(2)}, u32[]{:S(2)}) collective-permute-start(bf16[16,2048]{1,0:T(8,128)(2,1)S(1)} %get-tuple-element.61), channel_id=1, source_target_pairs={{0,8},{1,9},{2,10},{3,11},{4,12},{5,13},{6,14},{7,15},{8,16},{9,17... | collective-permute-start | bytes 196616 | tf_op jit(solution)/shard_map/ppermute | solution.py:460
  200.7 3.2 %collective-permute-start.34 = (bf16[16,1024]{1,0:T(8,128)(2,1)S(1)}, bf16[16,1024]{1,0:T(8,128)(2,1)S(1)}, u32[]{:S(2)}, u32[]{:S(2)}) collective-permute-start(bf16[16,1024]{1,0:T(8,128)(2,1)S(1)} %slice.37), channel_id=1, source_target_pairs={{0,32},{32,0},{64,96},{96,64},{128,160},{160,128},{192,224},{224,1... | collective-permute-start | bytes 98312 | tf_op jit(solution)/shard_map/ppermute | solution.py:41
  204.7 1.3 collective-permute-start.35

commit v4 on v3

--- a/solution.py
+++ b/solution.py
@@ -62,15 +62,13 @@
 
 
 def ring_eight(own, axis, up, down):
-    half = own.shape[0] // 2
     before, behind = [own], [own]
+    for _ in range(4):
+        before.append(lax.ppermute(before[-1], axis, up))
     for _ in range(3):
-        before.append(lax.ppermute(before[-1], axis, up))
         behind.append(lax.ppermute(behind[-1], axis, down))
-    top = lax.ppermute(before[3][:half], axis, up)
-    bottom = lax.ppermute(behind[3][half:], axis, down)
-    behind[2:3], before[2:3] = [in_hbm(behind[2])], [in_hbm(before[2])]
-    return own, behind[1], behind[2], behind[3], top, bottom, before[3], before[2], before[1]
+    behind[2], before[2] = in_hbm(behind[2]), in_hbm(before[2])
+    return own, behind[1], behind[2], behind[3], before[4], before[3], before[2], before[1]
 
 
 def whole(shape):
@@ -109,18 +107,16 @@
 
 
 def place_eight(index, blocks, store):
-    steps = (0, 1, 2, 3, 4, 4, 5, 6, 7)
-    for block, step in zip(blocks, steps):
+    for step, block in enumerate(blocks):
         z = lax.rem(index[0] + step, NZ)
-        first = NY // 2 if block is blocks[5] else 0
         for k in range(block.shape[0] // 16):
-            y = lax.rem(index[1] + first + k, NY)
+            y = lax.rem(index[1] + k, NY)
             start = pl.multiple_of(y * NZ * 16 + z * 16, 16)
             store(start, block[k * 16 : (k + 1) * 16, :])
 
 
 def gate_up_kernel(index, tok_a, *refs):
-    blocks, (gate_a, gate_b, up_a, up_b, out, tok_b) = refs[:9], refs[9:]
+    blocks, (gate_a, gate_b, up_a, up_b, out, tok_b) = refs[:NZ], refs[NZ:]
     step = pl.program_id(0)
 
     @pl.when(step == 0)
@@ -158,8 +154,8 @@
 
 
 def hidden_term_kernel(index, grad_a, *refs):
-    blocks, (down_a, down_b) = refs[:9], refs[9:11]
-    outs, (grad_b, total) = refs[11 : 11 + NX], refs[11 + NX :]
+    blocks, (down_a, down_b) = refs[:NZ], refs[NZ : NZ + 2]
+    outs, (grad_b, total) = refs[NZ + 2 : NZ + 2 + NX], refs[NZ + 2 + NX :]
 
     @pl.when(pl.program_id(0) == 0)
     def _():
@@ -420,7 +416,7 @@
     other_y = jnp.concatenate(gather_blocks(other, "col", Y_STEP), axis=0)
     other_blocks = ring_eight(other_y, "col", Z_UP, Z_DOWN)
     own_z = share(own, "col", Z_GROUPS)
-    own_all = share(after(own_z, other_y), "col", Y_GROUPS)
+    own_all = share(after(own_z, other_blocks[7]), "col", Y_GROUPS)
 
     gate_up_term, tok_other = gate_up_product(
         zyx, own_all, other_blocks, gate_own, gate_other, up_own, up_other

time: 208 us -> 212 us (1.019)
  waiting for transfers between devices: 59.7 us -> 69.2 us
  starting transfers between devices: 86.3 us -> 81.4 us
    ppermute x9, waiting for transfers between devices: 9.98 us -> 21.6 us  [gather_blocks(): lax.ppermute(own, axis, steps[count - k])]
    ppermute x3, waiting for transfers between devices: 0.01 us -> 8.91 us  [ring_eight(): behind.append(lax.ppermute(behind[-1], axis, down))]
    ppermute x12, starting transfers between devices: 24.3 us -> 16.5 us  [swap_core(): return lax.ppermute(value, 'row', CORE_PAIRS)]
    ppermute x3, waiting for transfers between devices: 11.4 us -> 7.62 us  [body(): mixed_sum += lax.ppermute(block, 'col', Z_STEP[step]).astype(F32)]
    ppermute x2 -> x0, starting transfers between devices: 2.67 us -> none  [the longest x1 2.67 us: ring_eight(): bottom = lax.ppermute(behind[3][half:], axis, down)]
    ppermute x1, waiting for transfers between devices: 2.65 us -> 0.01 us  [body(): lax.ppermute(far, 'col', Z_STEP[4])]
    ppermute x2 -> x0, waiting for transfers between devices: 2.19 us -> none  [the longest x1 1.81 us: ring_eight(): top = lax.ppermute(before[3][:half], axis, up)]
    ppermute x3 -> x4, waiting for transfers between devices: 12 us -> 10.6 us  [ring_eight(): before.append(lax.ppermute(before[-1], axis, up))]
  transfers between devices with their start and end apart: 42 -> 41, of which waited for: 21 -> 23; matrix products, arithmetic and copies ran while one was open for 10% -> 9% of each run, Pallas kernels for 14% -> 14%
where the time goes in v4:
time: 212 us; the launch traced here: 209 us
  starting transfers between devices  81.4 us (38%)
  waiting for transfers between devices  69.2 us (33%)
  Pallas kernels  35.1 us (17%)
  matrix products  13.4 us (6%)
  local copies, waits for them, and re-layouts  5.3 us (2%)
  other arithmetic  3.98 us (2%)
    all_to_all x6, starting transfers between devices, exchange(): lax.all_to_all(value, axis, 0, 0, axis_index_groups=groups, tiled=True)  33.7 us
    ppermute x9, waiting for transfers between devices, gather_blocks(): lax.ppermute(own, axis, steps[count - k])  21.6 us
    ppermute x12, starting transfers between devices, swap_core(): return lax.ppermute(value, 'row', CORE_PAIRS)  16.5 us
    all_to_all x6, waiting for transfers between devices, exchange(): lax.all_to_all(value, axis, 0, 0, axis_index_groups=groups, tiled=True)  13.5 us
    dot_general x3, matrix products, dot(): return lax.dot_general(left, right, dims, preferred_element_type=F32)  13.4 us
    ppermute x9, starting transfers between devices, gather_blocks(): lax.ppermute(own, axis, steps[count - k])  11 us
    ppermute x4, waiting for transfers between devices, ring_eight(): before.append(lax.ppermute(before[-1], axis, up))  10.6 us
    ppermute x3, waiting for transfers between devices, ring_eight(): behind.append(lax.ppermute(behind[-1], axis, down))  8.91 us
  transfers between devices with their start and end apart: 41, of which 23 were waited for; matrix products, arithmetic and copies ran while one was open for 9% of the time, Pallas kernels for 14%

profile of v4, /device:TPU:1, one launch (start us, length us, event | category | flops | bytes accessed | tf_op | source)
XLA Modules:
  0.0 209.2 jit_solution(14666667168218728868)
XLA Ops:
  0.7 0.8 constant_dynamic-slice_fusion.1
  2.2 0.8 tile.4
  3.1 9.0 %all-to-all-start = ((bf16[8,16,2048]{2,1,0:T(8,128)(2,1)}), bf16[8,16,2048]{2,1,0:T(8,128)(2,1)S(1)}, u32[]{:S(2)}, u32[]{:S(2)}) async-start(bf16[8,16,2048]{2,1,0:T(8,128)(2,1)} %tile.4), calls=%async_computation | async-start | bytes 1048576 | tf_op jit(solution)/shard_map/all_to_all | solution.py:46
  12.1 1.0 collective-permute-start
  14.3 1.3 collective-permute-start.4
  15.6 2.6 %collective-permute-start.3 = (bf16[16,2048]{1,0:T(8,128)(2,1)S(1)}, bf16[16,2048]{1,0:T(8,128)(2,1)S(1)}, u32[]{:S(2)}, u32[]{:S(2)}) collective-permute-start(bf16[16,2048]{1,0:T(8,128)(2,1)S(1)} %constant_dynamic-update-slice_fusion), channel_id=1, source_target_pairs={{0,2},{1,3},{2,0},{3,1},{4,6},{5,7},{6,4},{7,5},{8,10},{9,11},{10,... | collective-permute-start | bytes 196616 | tf_op jit(solution)/shard_map/ppermute | solution.py:61
  18.2 1.1 collective-permute-start.2
  19.2 2.4 %collective-permute-done.3 = bf16[16,2048]{1,0:T(8,128)(2,1)S(1)} collective-permute-done((bf16[16,2048]{1,0:T(8,128)(2,1)S(1)}, bf16[16,2048]{1,0:T(8,128)(2,1)S(1)}, u32[]{:S(2)}, u32[]{:S(2)}) %collective-permute-start.3) | collective-permute-done | bytes 65568 | tf_op jit(solution)/shard_map/ppermute | solution.py:61
  21.7 1.8 collective-permute-start.5
  23.5 1.8 collective-permute-start.16
  25.3 7.5 %collective-permute-done.5.refs_7_ = bf16[64,2048]{1,0:T(8,128)(2,1)S(1)} collective-permute-done((bf16[64,2048]{1,0:T(8,128)(2,1)S(1)}, bf16[64,2048]{1,0:T(8,128)(2,1)S(1)}, u32[]{:S(2)}, u32[]{:S(2)}) %collective-permute-start.5) | collective-permute-done | bytes 262176 | tf_op jit(solution)/shard_map/ppermute | solution.py:67
  32.8 1.6 tile.5
  34.4 3.6 %all-to-all-start.1 = ((bf16[4,128,2048]{2,1,0:T(8,128)(2,1)}), bf16[4,128,2048]{2,1,0:T(8,128)(2,1)S(1)}, u32[]{:S(2)}, u32[]{:S(2)}) async-start(bf16[4,128,2048]{2,1,0:T(8,128)(2,1)} %tile.5), calls=%async_computation.1 | async-start | bytes 4194304 | tf_op jit(solution)/shard_map/all_to_all | solution.py:46
  38.0 1.3 collective-permute-start.6
  39.5 4.8 %collective-permute-done.6.refs_1_ = bf16[64,2048]{1,0:T(8,128)(2,1)S(1)} collective-permute-done((bf16[64,2048]{1,0:T(8,128)(2,1)S(1)}, bf16[64,2048]{1,0:T(8,128)(2,1)S(1)}, u32[]{:S(2)}, u32[]{:S(2)}) %collective-permute-start.6) | collective-permute-done | bytes 262176 | tf_op jit(solution)/shard_map/ppermute | solution.py:69
  44.4 2.5 %collective-permute-start.7 = (bf16[64,2048]{1,0:T(8,128)(2,1)S(1)}, bf16[64,2048]{1,0:T(8,128)(2,1)}, u32[]{:S(2)}, u32[]{:S(2)}) collective-permute-start(bf16[64,2048]{1,0:T(8,128)(2,1)S(1)} %collective-permute-done.6.refs_1_), channel_id=1, source_target_pairs={{4,0},{5,1},{6,2},{7,3},{8,4},{9,5},{10,6},{11,7},{12,8},{13,9},{1... | collective-permute-start | bytes 786440 | tf_op jit(solution)/shard_map/ppermute | solution.py:69
  46.9 2.7 %collective-permute-start.12 = (bf16[768,1024]{1,0:T(8,128)(2,1)}, bf16[768,1024]{1,0:T(8,128)(2,1)}, u32[]{:S(2)}, u32[]{:S(2)}) collective-permute-start(bf16[768,1024]{1,0:T(8,128)(2,1)} %refs_4_.2), channel_id=1, source_target_pairs={{0,32},{32,0},{64,96},{96,64},{128,160},{160,128},{192,224},{224,1... | collective-permute-start | bytes 4718600 | tf_op jit(solution)/shard_map/ppermute | solution.py:41
  50.2 3.4 %collective-permute-start.8 = (bf16[64,2048]{1,0:T(8,128)(2,1)}, bf16[64,2048]{1,0:T(8,128)(2,1)S(1)}, u32[]{:S(2)}, u32[]{:S(2)}) collective-permute-start(bf16[64,2048]{1,0:T(8,128)(2,1)} %collective-permute-done.7.refs_2_), channel_id=1, source_target_pairs={{4,0},{5,1},{6,2},{7,3},{8,4},{9,5},{10,6},{11,7},{12,8},{13,9},{1... | collective-permute-start | bytes 786440 | tf_op jit(solution)/shard_map/ppermute | solution.py:69
  53.7 3.5 %collective-permute-done.8.refs_3_ = bf16[64,2048]{1,0:T(8,128)(2,1)S(1)} collective-permute-done((bf16[64,2048]{1,0:T(8,128)(2,1)}, bf16[64,2048]{1,0:T(8,128)(2,1)S(1)}, u32[]{:S(2)}, u32[]{:S(2)}) %collective-permute-start.8) | collective-permute-done | bytes 262176 | tf_op jit(solution)/shard_map/ppermute | solution.py:69
  57.3 3.1 %collective-permute-done.11.refs_4_ = bf16[64,2048]{1,0:T(8,128)(2,1)} collective-permute-done((bf16[64,2048]{1,0:T(8,128)(2,1)S(1)}, bf16[64,2048]{1,0:T(8,128)(2,1)}, u32[]{:S(2)}, u32[]{:S(2)}) %collective-permute-start.11) | collective-permute-done | bytes 262176 | tf_op jit(solution)/shard_map/ppermute | solution.py:67
  60.4 2.3 %all-to-all-done.1 = bf16[4,128,2048]{2,1,0:T(8,128)(2,1)S(1)} async-done(((bf16[4,128,2048]{2,1,0:T(8,128)(2,1)}), bf16[4,128,2048]{2,1,0:T(8,128)(2,1)S(1)}, u32[]{:S(2)}, u32[]{:S(2)}) %all-to-all-start.1) | async-done | bytes 2097184 | tf_op jit(solution)/shard_map/all_to_all | solution.py:46
  62.7 7.4 %shard_map.93 = (bf16[512,1536]{1,0:T(8,128)(2,1)}, bf16[512,1024]{1,0:T(8,128)(2,1)}) custom-call(s32[3]{0:T(128)S(1)} %pad_add_fusion.index, bf16[512,2048]{1,0:T(8,128)(2,1)S(1)} %bitcast.10, bf16[64,2048]{1,0:T(8,128)(2,1)S(1)} %pad_maximum_fusion.4.refs_0_, bf16[64,2048]{1,0:T(8,128)(2,1)S(1)} %collective-permute-done.6.refs_1_, ...), custom_call_target="tpu_custom_call" | custom-call | flops 3221225472 | bytes 10485760 | tf_op jit(solution)/shard_map/pallas_call | solution.py:144
  70.1 4.5 %all-to-all-start.2 = ((bf16[4,128,1536]{2,1,0:T(8,128)(2,1)}), bf16[4,128,1536]{2,1,0:T(8,128)(2,1)}, u32[]{:S(2)}, u32[]{:S(2)}) async-start(bf16[4,128,1536]{2,1,0:T(8,128)(2,1)} %bitcast.17), calls=%async_computation.2 | async-start | bytes 3145728 | tf_op jit(solution)/shard_map/all_to_all | solution.py:46
  74.6 5.6 %shard_map.92 = (bf16[128,768]{1,0:T(8,128)(2,1)}, bf16[128,768]{1,0:T(8,128)(2,1)}, bf16[128,768]{1,0:T(8,128)(2,1)}, bf16[128,768]{1,0:T(8,128)(2,1)}, bf16[512,1024]{1,0:T(8,128)(2,1)}) custom-call(s32[3]{0:T(128)S(1)} %pad_add_fusion.index, bf16[512,2048]{1,0:T(8,128)(2,1)S(1)} %bitcast.11, bf16[64,2048]{1,0:T(8,128)(2,1)S(1)} %pad_maximum_fusion.4.refs_0_, ...), custom_call_target="tpu_custom_call" | custom-call | flops 1610612736 | bytes 10485760 | tf_op jit(solution)/shard_map/pallas_call | solution.py:180
  80.2 1.3 collective-permute-start.13
  81.5 2.4 %collective-permute-start.14 = (bf16[128,768]{1,0:T(8,128)(2,1)}, bf16[128,768]{1,0:T(8,128)(2,1)S(1)}, u32[]{:S(2)}, u32[]{:S(2)}) collective-permute-start(bf16[128,768]{1,0:T(8,128)(2,1)} %get-tuple-element.37), channel_id=1, source_target_pairs={{0,128},{32,160},{64,192},{96,224},{128,0},{160,32},{192,64},{224,... | collective-permute-start | bytes 589832 | tf_op jit(solution)/shard_map/ppermute | solution.py:429
  83.9 1.1 collective-permute-start.15
  85.0 7.7 %all-to-all-done.2.terms = bf16[4,128,1536]{2,1,0:T(8,128)(2,1)} async-done(((bf16[4,128,1536]{2,1,0:T(8,128)(2,1)}), bf16[4,128,1536]{2,1,0:T(8,128)(2,1)}, u32[]{:S(2)}, u32[]{:S(2)}) %all-to-all-start.2) | async-done | bytes 1572896 | tf_op jit(solution)/shard_map/all_to_all | solution.py:46
  92.8 2.5 %shard_map.94 = (f32[128,1536]{1,0:T(8,128)}, bf16[128,768]{1,0:T(8,128)(2,1)S(1)}) custom-call(s32[1]{0:T(128)} %bitcast.2.index, bf16[4,128,1536]{2,1,0:T(8,128)(2,1)} %all-to-all-done.2.terms), custom_call_target="tpu_custom_call" | custom-call | flops 3145728 | bytes 10485760 | tf_op jit(solution)/shard_map/pallas_call | solution.py:278
  95.5 1.8 collective-permute-start.19
  97.9 2.9 %collective-permute-done.14.refs_2_ = bf16[128,768]{1,0:T(8,128)(2,1)S(1)} collective-permute-done((bf16[128,768]{1,0:T(8,128)(2,1)}, bf16[128,768]{1,0:T(8,128)(2,1)S(1)}, u32[]{:S(2)}, u32[]{:S(2)}) %collective-permute-start.14) | collective-permute-done | bytes 196640 | tf_op jit(solution)/shard_map/ppermute | solution.py:429
  100.8 1.5 shard_map.95.refs_0_
  102.3 2.3 %collective-permute-done.20.refs_3_ = bf16[128,768]{1,0:T(8,128)(2,1)S(1)} collective-permute-done((bf16[128,768]{1,0:T(8,128)(2,1)S(1)}, bf16[128,768]{1,0:T(8,128)(2,1)S(1)}, u32[]{:S(2)}, u32[]{:S(2)}) %collective-permute-start.20) | collective-permute-done | bytes 196640 | tf_op jit(solution)/shard_map/ppermute | solution.py:61
  104.6 4.6 %collective-permute-done.19.refs_2_ = bf16[128,768]{1,0:T(8,128)(2,1)S(1)} collective-permute-done((bf16[128,768]{1,0:T(8,128)(2,1)S(1)}, bf16[128,768]{1,0:T(8,128)(2,1)S(1)}, u32[]{:S(2)}, u32[]{:S(2)}) %collective-permute-start.19) | collective-permute-done | bytes 196640 | tf_op jit(solution)/shard_map/ppermute | solution.py:61
  109.2 5.2 %shard_map.96 = (bf16[512,2048]{1,0:T(8,128)(2,1)}, bf16[512,768]{1,0:T(8,128)(2,1)}) custom-call(s32[1]{0:T(128)} %bitcast.2.index, bf16[128,768]{1,0:T(8,128)(2,1)S(1)} %get-tuple-element.42.refs_0_, bf16[128,768]{1,0:T(8,128)(2,1)S(1)} %collective-permute-done.18.refs_1_, bf16[128,768]{1,0:T(8,128)(2,1)S(1)} %collective-permute-done.19.refs_2_, ...), custom_call_target="tpu_custom_call" | custom-call | flops 1610612736 | bytes 10485760 | tf_op jit(solution)/shard_map/pallas_call | solution.py:213
  114.4 4.5 %all-to-all-start.3 = ((bf16[4,128,2048]{2,1,0:T(8,128)(2,1)}), bf16[4,128,2048]{2,1,0:T(8,128)(2,1)}, u32[]{:S(2)}, u32[]{:S(2)}) async-start(bf16[4,128,2048]{2,1,0:T(8,128)(2,1)} %bitcast.15), calls=%async_computation.3 | async-start | bytes 4194304 | tf_op jit(solution)/shard_map/all_to_all | solution.py:46
  119.0 1.3 collective-permute-start.24
  120.2 2.0 collective-permute-start.23
  122.2 4.3 %collective-permute-start.28 = (bf16[512,1024]{1,0:T(8,128)(2,1)}, bf16[512,1024]{1,0:T(8,128)(2,1)}, u32[]{:S(2)}, u32[]{:S(2)}) collective-permute-start(bf16[512,1024]{1,0:T(8,128)(2,1)} %get-tuple-element.53), channel_id=1, source_target_pairs={{0,32},{32,0},{64,96},{96,64},{128,160},{160,128},{192,224},{224,1... | collective-permute-start | bytes 3145736 | tf_op jit(solution)/shard_map/ppermute | solution.py:41
  126.5 5.2 %collective-permute-done.25.refs_3_ = bf16[128,1536]{1,0:T(8,128)(2,1)S(1)} collective-permute-done((bf16[128,1536]{1,0:T(8,128)(2,1)S(1)}, bf16[128,1536]{1,0:T(8,128)(2,1)S(1)}, u32[]{:S(2)}, u32[]{:S(2)}) %collective-permute-start.25) | collective-permute-done | bytes 393248 | tf_op jit(solution)/shard_map/ppermute | solution.py:61
  131.7 1.1 collective-permute-done.24.refs_2_
  132.9 5.9 %collective-permute-done.23.refs_1_ = bf16[128,1536]{1,0:T(8,128)(2,1)S(1)} collective-permute-done((bf16[128,1536]{1,0:T(8,128)(2,1)S(1)}, bf16[128,1536]{1,0:T(8,128)(2,1)S(1)}, u32[]{:S(2)}, u32[]{:S(2)}) %collective-permute-start.23) | collective-permute-done | bytes 393248 | tf_op jit(solution)/shard_map/ppermute | solution.py:61
  138.8 7.2 %shard_map.98 = (bf16[512,2048]{1,0:T(8,128)(2,1)}, bf16[512,768]{1,0:T(8,128)(2,1)}, bf16[512,768]{1,0:T(8,128)(2,1)}) custom-call(s32[1]{0:T(128)} %bitcast.2.index, bf16[128,1536]{1,0:T(8,128)(2,1)S(1)} %shard_map.95.refs_0_, bf16[128,1536]{1,0:T(8,128)(2,1)S(1)} %collective-permute-done.23.refs_1_, ...), custom_call_target="tpu_custom_call" | custom-call | flops 3221225472 | bytes 10485760 | tf_op jit(solution)/shard_map/pallas_call | solution.py:249
  146.0 4.5 %all-to-all-start.4 = ((bf16[4,128,2048]{2,1,0:T(8,128)(2,1)}), bf16[4,128,2048]{2,1,0:T(8,128)(2,1)}, u32[]{:S(2)}, u32[]{:S(2)}) async-start(bf16[4,128,2048]{2,1,0:T(8,128)(2,1)} %bitcast.14), calls=%async_computation.4 | async-start | bytes 4194304 | tf_op jit(solution)/shard_map/all_to_all | solution.py:46
  150.5 2.0 collective-permute-start.27
  153.3 1.3 collective-permute-done.27
  154.6 4.5 %fusion.4 = bf16[768,1024]{1,0:T(8,128)(2,1)} fusion(bf16[512,1024]{1,0:T(8,128)(2,1)} %collective-permute-done.28, bf16[512,1024]{1,0:T(8,128)(2,1)S(1)} %get-tuple-element.64, bf16[512,768]{1,0:T(8,128)(2,1)S(1)} %collective-permute-done.27, bf16[512,768]{1,0:T(8,128)(2,1)} %get-tuple-element.52), kind=kOutput, calls=%fused_computation.5 | convolution fusion | flops 1618739200 | bytes 5242880 | tf_op jit(solution)/shard_map/dot_general | solution.py:37
  159.1 2.5 %pad_maximum_fusion.1 = bf16[1024,768]{1,0:T(8,128)(2,1)} fusion(bf16[512,768]{1,0:T(8,128)(2,1)S(1)} %collective-permute-done.26, bf16[512,768]{1,0:T(8,128)(2,1)} %get-tuple-element.49), kind=kLoop, calls=%fused_computation.8 | loop fusion | flops 3145728 | bytes 3145728 | tf_op jit(solution)/shard_map/concatenate | solution.py:442
  161.6 1.1 copy-done.1
  162.6 4.2 %convolution_convert_fusion.1 = bf16[1024,768]{1,0:T(8,128)(2,1)} fusion(bf16[512,768]{1,0:T(8,128)(2,1)S(1)} %collective-permute-done.29, bf16[512,768]{1,0:T(8,128)(2,1)} %get-tuple-element.54, bf16[512,1024]{1,0:T(8,128)(2,1)S(1)} %collective-permute-done.22, bf16[512,1024]{1,0:T(8,128)(2,1)S(1)} %get-tuple-element.63), kind=kOutput, calls=%fused_computation.7 | convolution fusion | flops 1618739200 | bytes 5242880 | tf_op jit(solution)/shard_map/dot_general | solution.py:37
  166.8 2.5 %shard_map.97 = (bf16[64,2048]{1,0:T(8,128)(2,1)S(1)}, bf16[64,2048]{1,0:T(8,128)(2,1)S(1)}) custom-call(s32[3]{0:T(128)S(1)} %pad_add_fusion.index, bf16[4,128,2048]{2,1,0:T(8,128)(2,1)} %all-to-all-done.3.terms), custom_call_target="tpu_custom_call" | custom-call | flops 2097152 | bytes 10485760 | tf_op jit(solution)/shard_map/pallas_call | solution.py:356
  169.4 2.1 %collective-permute-start.21 = (bf16[64,2048]{1,0:T(8,128)(2,1)S(1)}, bf16[64,2048]{1,0:T(8,128)(2,1)S(1)}, u32[]{:S(2)}, u32[]{:S(2)}) collective-permute-start(bf16[64,2048]{1,0:T(8,128)(2,1)S(1)} %get-tuple-element.45), channel_id=1, source_target_pairs={{0,16},{1,17},{2,18},{3,19},{4,20},{5,21},{6,22},{7,23},{8,24},{9,... | collective-permute-start | bytes 786440 | tf_op jit(solution)/shard_map/ppermute | solution.py:452
  171.5 3.4 %all-to-all-done.4.terms = bf16[4,128,2048]{2,1,0:T(8,128)(2,1)} async-done(((bf16[4,128,2048]{2,1,0:T(8,128)(2,1)}), bf16[4,128,2048]{2,1,0:T(8,128)(2,1)}, u32[]{:S(2)}, u32[]{:S(2)}) %all-to-all-start.4) | async-done | bytes 2097184 | tf_op jit(solution)/shard_map/all_to_all | solution.py:46
  174.9 2.7 %shard_map.99 = bf16[128,2048]{1,0:T(8,128)(2,1)} custom-call(s32[1]{0:T(128)} %bitcast.2.index, bf16[4,128,2048]{2,1,0:T(8,128)(2,1)} %all-to-all-done.4.terms), custom_call_target="tpu_custom_call" | custom-call | flops 2097152 | bytes 10485760 | tf_op jit(solution)/shard_map/pallas_call | solution.py:334
  177.6 7.6 %all-to-all-start.5 = ((bf16[8,16,2048]{2,1,0:T(8,128)(2,1)}), bf16[8,16,2048]{2,1,0:T(8,128)(2,1)S(1)}, u32[]{:S(2)}, u32[]{:S(2)}) async-start(bf16[8,16,2048]{2,1,0:T(8,128)(2,1)} %bitcast.16), calls=%async_computation.5 | async-start | bytes 1048576 | tf_op jit(solution)/shard_map/all_to_all | solution.py:46
  185.2 4.7 %convolution_convert_fusion = bf16[1024,768]{1,0:T(8,128)(2,1)} fusion(bf16[1024,768]{1,0:T(8,128)(2,1)} %pad_maximum_fusion.1, bf16[512,1024]{1,0:T(8,128)(2,1)} %copy-done.1, bf16[512,1024]{1,0:T(8,128)(2,1)S(1)} %get-tuple-element.63), kind=kOutput, calls=%fused_computation.6 | convolution fusion | flops 1615593472 | bytes 5242880 | tf_op jit(solution)/shard_map/dot_general | solution.py:37
  190.6 2.8 %collective-permute-start.30 = (bf16[16,2048]{1,0:T(8,128)(2,1)S(1)}, bf16[16,2048]{1,0:T(8,128)(2,1)S(1)}, u32[]{:S(2)}, u32[]{:S(2)}) collective-permute-start(bf16[16,2048]{1,0:T(8,128)(2,1)S(1)} %get-tuple-element.59), channel_id=1, source_target_pairs={{0,28},{1,29},{2,30},{3,31},{4,0},{5,1},{6,2},{7,3},{8,4},{9,5},{1... | collective-permute-start | bytes 196616 | tf_op jit(solution)/shard_map/ppermute | solution.py:456
  193.3 1.1 collective-permute-start.32
  194.5 2.1 %collective-permute-done.30 = bf16[16,2048]{1,0:T(8,128)(2,1)S(1)} collective-permute-done((bf16[16,2048]{1,0:T(8,128)(2,1)S(1)}, bf16[16,2048]{1,0:T(8,128)(2,1)S(1)}, u32[]{:S(2)}, u32[]{:S(2)}) %collective-permute-start.30) | collective-permute-done | bytes 65568 | tf_op jit(solution)/shard_map/ppermute | solution.py:456
  196.6 3.0 %collective-permute-done.31 = bf16[16,2048]{1,0:T(8,128)(2,1)S(1)} collective-permute-done((bf16[16,2048]{1,0:T(8,128)(2,1)S(1)}, bf16[16,2048]{1,0:T(8,128)(2,1)S(1)}, u32[]{:S(2)}, u32[]{:S(2)}) %collective-permute-start.31) | collective-permute-done | bytes 65568 | tf_op jit(solution)/shard_map/ppermute | solution.py:456
  199.6 2.5 %collective-permute-done.32 = bf16[16,2048]{1,0:T(8,128)(2,1)S(1)} collective-permute-done((bf16[16,2048]{1,0:T(8,128)(2,1)S(1)}, bf16[16,2048]{1,0:T(8,128)(2,1)S(1)}, u32[]{:S(2)}, u32[]{:S(2)}) %collective-permute-start.32) | collective-permute-done | bytes 65568 | tf_op jit(solution)/shard_map/ppermute | solution.py:456
  202.1 3.5 %collective-permute-start.33 = (bf16[16,1024]{1,0:T(8,128)(2,1)S(1)}, bf16[16,1024]{1,0:T(8,128)(2,1)S(1)}, u32[]{:S(2)}, u32[]{:S(2)}) collective-permute-start(bf16[16,1024]{1,0:T(8,128)(2,1)S(1)} %slice.27), channel_id=1, source_target_pairs={{0,32},{32,0},{64,96},{96,64},{128,160},{160,128},{192,224},{224,1... | collective-permute-start | bytes 98312 | tf_op jit(solution)/shard_map/ppermute | solution.py:41
  205.7 0.9 collective-permute-done.33
  207.7 0.9 collective-permute-done.34
  (53 shorter events, 7.2 us)
Async XLA Ops:
  3.1 29.7 %all-to-all-start = ((bf16[8,16,2048]{2,1,0:T(8,128)(2,1)}), bf16[8,16,2048]{2,1,0:T(8,128)(2,1)S(1)}, u32[]{:S(2)}, u32[]{:S(2)}) async-start(bf16[8,16,2048]{2,1,0:T(8,128)(2,1)} %tile.4), calls=%async_computation | async-start | bytes 1048576 | tf_op jit(solution)/shard_map/all_to_all | solution.py:46
  12.1 1.8 collective-permute-start
  13.0 1.2 collective-permute-start.1
  14.3 5.0 %collective-permute-start.4 = (bf16[16,2048]{1,0:T(8,128)(2,1)S(1)}, bf16[16,2048]{1,0:T(8,128)(2,1)S(1)}, u32[]{:S(2)}, u32[]{:S(2)}) collective-permute-start(bf16[16,2048]{1,0:T(8,128)(2,1)S(1)} %constant_dynamic-update-slice_fusion), channel_id=1, source_target_pairs={{0,1},{1,2},{2,3},{3,0},{4,5},{5,6},{6,7},{7,4},{8,9},{9,10},{10,1... | collective-permute-start | bytes 196616 | tf_op jit(solution)/shard_map/ppermute | solution.py:61
  15.6 6.1 %collective-permute-start.3 = (bf16[16,2048]{1,0:T(8,128)(2,1)S(1)}, bf16[16,2048]{1,0:T(8,128)(2,1)S(1)}, u32[]{:S(2)}, u32[]{:S(2)}) collective-permute-start(bf16[16,2048]{1,0:T(8,128)(2,1)S(1)} %constant_dynamic-update-slice_fusion), channel_id=1, source_target_pairs={{0,2},{1,3},{2,0},{3,1},{4,6},{5,7},{6,4},{7,5},{8,10},{9,11},{10,... | collective-permute-start | bytes 196616 | tf_op jit(solution)/shard_map/ppermute | solution.py:61
  18.2 3.5 %collective-permute-start.2 = (bf16[16,2048]{1,0:T(8,128)(2,1)S(1)}, bf16[16,2048]{1,0:T(8,128)(2,1)S(1)}, u32[]{:S(2)}, u32[]{:S(2)}) collective-permute-start(bf16[16,2048]{1,0:T(8,128)(2,1)S(1)} %constant_dynamic-update-slice_fusion), channel_id=1, source_target_pairs={{0,3},{1,0},{2,1},{3,2},{4,7},{5,4},{6,5},{7,6},{8,11},{9,8},{10,9... | collective-permute-start | bytes 196616 | tf_op jit(solution)/shard_map/ppermute | solution.py:61
  21.7 11.1 %collective-permute-start.5 = (bf16[64,2048]{1,0:T(8,128)(2,1)S(1)}, bf16[64,2048]{1,0:T(8,128)(2,1)S(1)}, u32[]{:S(2)}, u32[]{:S(2)}) collective-permute-start(bf16[64,2048]{1,0:T(8,128)(2,1)S(1)} %pad_maximum_fusion.4.refs_0_), channel_id=1, source_target_pairs={{0,4},{1,5},{2,6},{3,7},{4,8},{5,9},{6,10},{7,11},{8,12},{9,13},{1... | collective-permute-start | bytes 786440 | tf_op jit(solution)/shard_map/ppermute | solution.py:67
  23.5 36.9 %collective-permute-start.16 = (bf16[1024,768]{1,0:T(8,128)(2,1)}, bf16[1024,768]{1,0:T(8,128)(2,1)}, u32[]{:S(2)}, u32[]{:S(2)}) collective-permute-start(bf16[1024,768]{1,0:T(8,128)(2,1)} %refs_4_.3), channel_id=1, source_target_pairs={{0,32},{32,0},{64,96},{96,64},{128,160},{160,128},{192,224},{224,1... | collective-permute-start | bytes 4718600 | tf_op jit(solution)/shard_map/ppermute | solution.py:41
  25.3 35.1 %collective-permute-start.17 = (bf16[1024,768]{1,0:T(8,128)(2,1)}, bf16[1024,768]{1,0:T(8,128)(2,1)}, u32[]{:S(2)}, u32[]{:S(2)}) collective-permute-start(bf16[1024,768]{1,0:T(8,128)(2,1)} %refs_5_.1), channel_id=1, source_target_pairs={{0,32},{32,0},{64,96},{96,64},{128,160},{160,128},{192,224},{224,1... | collective-permute-start | bytes 4718600 | tf_op jit(solution)/shard_map/ppermute | solution.py:41
  34.4 28.3 %all-to-all-start.1 = ((bf16[4,128,2048]{2,1,0:T(8,128)(2,1)}), bf16[4,128,2048]{2,1,0:T(8,128)(2,1)S(1)}, u32[]{:S(2)}, u32[]{:S(2)}) async-start(bf16[4,128,2048]{2,1,0:T(8,128)(2,1)} %tile.5), calls=%async_computation.1 | async-start | bytes 4194304 | tf_op jit(solution)/shard_map/all_to_all | solution.py:46
  38.0 6.4 %collective-permute-start.6 = (bf16[64,2048]{1,0:T(8,128)(2,1)S(1)}, bf16[64,2048]{1,0:T(8,128)(2,1)S(1)}, u32[]{:S(2)}, u32[]{:S(2)}) collective-permute-start(bf16[64,2048]{1,0:T(8,128)(2,1)S(1)} %pad_maximum_fusion.4.refs_0_), channel_id=1, source_target_pairs={{4,0},{5,1},{6,2},{7,3},{8,4},{9,5},{10,6},{11,7},{12,8},{13,9},{1... | collective-permute-start | bytes 786440 | tf_op jit(solution)/shard_map/ppermute | solution.py:69
  39.3 7.6 %collective-permute-start.9 = (bf16[64,2048]{1,0:T(8,128)(2,1)S(1)}, bf16[64,2048]{1,0:T(8,128)(2,1)S(1)}, u32[]{:S(2)}, u32[]{:S(2)}) collective-permute-start(bf16[64,2048]{1,0:T(8,128)(2,1)S(1)} %collective-permute-done.5.refs_7_), channel_id=1, source_target_pairs={{0,4},{1,5},{2,6},{3,7},{4,8},{5,9},{6,10},{7,11},{8,12},{9,13},{1... | collective-permute-start | bytes 786440 | tf_op jit(solution)/shard_map/ppermute | solution.py:67
  44.4 5.8 %collective-permute-start.7 = (bf16[64,2048]{1,0:T(8,128)(2,1)S(1)}, bf16[64,2048]{1,0:T(8,128)(2,1)}, u32[]{:S(2)}, u32[]{:S(2)}) collective-permute-start(bf16[64,2048]{1,0:T(8,128)(2,1)S(1)} %collective-permute-done.6.refs_1_), channel_id=1, source_target_pairs={{4,0},{5,1},{6,2},{7,3},{8,4},{9,5},{10,6},{11,7},{12,8},{13,9},{1... | collective-permute-start | bytes 786440 | tf_op jit(solution)/shard_map/ppermute | solution.py:69
  46.9 6.7 %copy-start = (bf16[64,2048]{1,0:T(8,128)(2,1)}, bf16[64,2048]{1,0:T(8,128)(2,1)S(1)}, u32[]{:S(2)}) copy-start(bf16[64,2048]{1,0:T(8,128)(2,1)S(1)} %collective-permute-done.9.refs_6_) | copy-start | bytes 786436
  46.9 6.7 %collective-permute-start.10 = (bf16[64,2048]{1,0:T(8,128)(2,1)S(1)}, bf16[64,2048]{1,0:T(8,128)(2,1)S(1)}, u32[]{:S(2)}, u32[]{:S(2)}) collective-permute-start(bf16[64,2048]{1,0:T(8,128)(2,1)S(1)} %collective-permute-done.9.refs_6_), channel_id=1, source_target_pairs={{0,4},{1,5},{2,6},{3,7},{4,8},{5,9},{6,10},{7,11},{8,12},{9,13},{1... | collective-permute-start | bytes 786440 | tf_op jit(solution)/shard_map/ppermute | solution.py:67
  46.9 27.7 %collective-permute-start.12 = (bf16[768,1024]{1,0:T(8,128)(2,1)}, bf16[768,1024]{1,0:T(8,128)(2,1)}, u32[]{:S(2)}, u32[]{:S(2)}) collective-permute-start(bf16[768,1024]{1,0:T(8,128)(2,1)} %refs_4_.2), channel_id=1, source_target_pairs={{0,32},{32,0},{64,96},{96,64},{128,160},{160,128},{192,224},{224,1... | collective-permute-start | bytes 4718600 | tf_op jit(solution)/shard_map/ppermute | solution.py:41
  50.2 7.0 %collective-permute-start.8 = (bf16[64,2048]{1,0:T(8,128)(2,1)}, bf16[64,2048]{1,0:T(8,128)(2,1)S(1)}, u32[]{:S(2)}, u32[]{:S(2)}) collective-permute-start(bf16[64,2048]{1,0:T(8,128)(2,1)} %collective-permute-done.7.refs_2_), channel_id=1, source_target_pairs={{4,0},{5,1},{6,2},{7,3},{8,4},{9,5},{10,6},{11,7},{12,8},{13,9},{1... | collective-permute-start | bytes 786440 | tf_op jit(solution)/shard_map/ppermute | solution.py:69
  53.6 6.7 %collective-permute-start.11 = (bf16[64,2048]{1,0:T(8,128)(2,1)S(1)}, bf16[64,2048]{1,0:T(8,128)(2,1)}, u32[]{:S(2)}, u32[]{:S(2)}) collective-permute-start(bf16[64,2048]{1,0:T(8,128)(2,1)S(1)} %collective-permute-done.10.refs_5_), channel_id=1, source_target_pairs={{0,4},{1,5},{2,6},{3,7},{4,8},{5,9},{6,10},{7,11},{8,12},{9,13},{1... | collective-permute-start | bytes 786440 | tf_op jit(solution)/shard_map/ppermute | solution.py:67
  70.1 22.7 %all-to-all-start.2 = ((bf16[4,128,1536]{2,1,0:T(8,128)(2,1)}), bf16[4,128,1536]{2,1,0:T(8,128)(2,1)}, u32[]{:S(2)}, u32[]{:S(2)}) async-start(bf16[4,128,1536]{2,1,0:T(8,128)(2,1)} %bitcast.17), calls=%async_computation.2 | async-start | bytes 3145728 | tf_op jit(solution)/shard_map/all_to_all | solution.py:46
  80.2 17.1 %collective-permute-start.13 = (bf16[128,768]{1,0:T(8,128)(2,1)}, bf16[128,768]{1,0:T(8,128)(2,1)S(1)}, u32[]{:S(2)}, u32[]{:S(2)}) collective-permute-start(bf16[128,768]{1,0:T(8,128)(2,1)} %get-tuple-element.36), channel_id=1, source_target_pairs={{0,64},{32,96},{64,128},{96,160},{128,192},{160,224},{192,0},{224,... | collective-permute-start | bytes 589832 | tf_op jit(solution)/shard_map/ppermute | solution.py:429
  81.5 19.3 %collective-permute-start.14 = (bf16[128,768]{1,0:T(8,128)(2,1)}, bf16[128,768]{1,0:T(8,128)(2,1)S(1)}, u32[]{:S(2)}, u32[]{:S(2)}) collective-permute-start(bf16[128,768]{1,0:T(8,128)(2,1)} %get-tuple-element.37), channel_id=1, source_target_pairs={{0,128},{32,160},{64,192},{96,224},{128,0},{160,32},{192,64},{224,... | collective-permute-start | bytes 589832 | tf_op jit(solution)/shard_map/ppermute | solution.py:429
  83.9 16.9 %collective-permute-start.15 = (bf16[128,768]{1,0:T(8,128)(2,1)}, bf16[128,768]{1,0:T(8,128)(2,1)S(1)}, u32[]{:S(2)}, u32[]{:S(2)}) collective-permute-start(bf16[128,768]{1,0:T(8,128)(2,1)} %get-tuple-element.38), channel_id=1, source_target_pairs={{0,192},{32,224},{64,0},{96,32},{128,64},{160,96},{192,128},{224,1... | collective-permute-start | bytes 589832 | tf_op jit(solution)/shard_map/ppermute | solution.py:429
  95.2 9.4 %collective-permute-start.20 = (bf16[128,768]{1,0:T(8,128)(2,1)S(1)}, bf16[128,768]{1,0:T(8,128)(2,1)S(1)}, u32[]{:S(2)}, u32[]{:S(2)}) collective-permute-start(bf16[128,768]{1,0:T(8,128)(2,1)S(1)} %get-tuple-element.42.refs_0_), channel_id=1, source_target_pairs={{0,64},{32,96},{64,128},{96,160},{128,192},{160,224},{192,0},{224,... | collective-permute-start | bytes 589832 | tf_op jit(solution)/shard_map/ppermute | solution.py:61
  95.5 13.7 %collective-permute-start.19 = (bf16[128,768]{1,0:T(8,128)(2,1)S(1)}, bf16[128,768]{1,0:T(8,128)(2,1)S(1)}, u32[]{:S(2)}, u32[]{:S(2)}) collective-permute-start(bf16[128,768]{1,0:T(8,128)(2,1)S(1)} %get-tuple-element.42.refs_0_), channel_id=1, source_target_pairs={{0,128},{32,160},{64,192},{96,224},{128,0},{160,32},{192,64},{224,... | collective-permute-start | bytes 589832 | tf_op jit(solution)/shard_map/ppermute | solution.py:61
  97.3 11.9 %collective-permute-start.18 = (bf16[128,768]{1,0:T(8,128)(2,1)S(1)}, bf16[128,768]{1,0:T(8,128)(2,1)S(1)}, u32[]{:S(2)}, u32[]{:S(2)}) collective-permute-start(bf16[128,768]{1,0:T(8,128)(2,1)S(1)} %get-tuple-element.42.refs_0_), channel_id=1, source_target_pairs={{0,192},{32,224},{64,0},{96,32},{128,64},{160,96},{192,128},{224,1... | collective-permute-start | bytes 589832 | tf_op jit(solution)/shard_map/ppermute | solution.py:61
  114.4 31.6 %all-to-all-start.3 = ((bf16[4,128,2048]{2,1,0:T(8,128)(2,1)}), bf16[4,128,2048]{2,1,0:T(8,128)(2,1)}, u32[]{:S(2)}, u32[]{:S(2)}) async-start(bf16[4,128,2048]{2,1,0:T(8,128)(2,1)} %bitcast.15), calls=%async_computation.3 | async-start | bytes 4194304 | tf_op jit(solution)/shard_map/all_to_all | solution.py:46
  118.9 12.9 %collective-permute-start.25 = (bf16[128,1536]{1,0:T(8,128)(2,1)S(1)}, bf16[128,1536]{1,0:T(8,128)(2,1)S(1)}, u32[]{:S(2)}, u32[]{:S(2)}) collective-permute-start(bf16[128,1536]{1,0:T(8,128)(2,1)S(1)} %shard_map.95.refs_0_), channel_id=1, source_target_pairs={{0,64},{32,96},{64,128},{96,160},{128,192},{160,224},{192,0},{224,... | collective-permute-start | bytes 1179656 | tf_op jit(solution)/shard_map/ppermute | solution.py:61
  119.0 13.9 %collective-permute-start.24 = (bf16[128,1536]{1,0:T(8,128)(2,1)S(1)}, bf16[128,1536]{1,0:T(8,128)(2,1)S(1)}, u32[]{:S(2)}, u32[]{:S(2)}) collective-permute-start(bf16[128,1536]{1,0:T(8,128)(2,1)S(1)} %shard_map.95.refs_0_), channel_id=1, source_target_pairs={{0,128},{32,160},{64,192},{96,224},{128,0},{160,32},{192,64},{224,... | collective-permute-start | bytes 1179656 | tf_op jit(solution)/shard_map/ppermute | solution.py:61
  120.2 18.5 %collective-permute-start.23 = (bf16[128,1536]{1,0:T(8,128)(2,1)S(1)}, bf16[128,1536]{1,0:T(8,128)(2,1)S(1)}, u32[]{:S(2)}, u32[]{:S(2)}) collective-permute-start(bf16[128,1536]{1,0:T(8,128)(2,1)S(1)} %shard_map.95.refs_0_), channel_id=1, source_target_pairs={{0,192},{32,224},{64,0},{96,32},{128,64},{160,96},{192,128},{224,1... | collective-permute-start | bytes 1179656 | tf_op jit(solution)/shard_map/ppermute | solution.py:61
  122.2 31.1 %collective-permute-start.28 = (bf16[512,1024]{1,0:T(8,128)(2,1)}, bf16[512,1024]{1,0:T(8,128)(2,1)}, u32[]{:S(2)}, u32[]{:S(2)}) collective-permute-start(bf16[512,1024]{1,0:T(8,128)(2,1)} %get-tuple-element.53), channel_id=1, source_target_pairs={{0,32},{32,0},{64,96},{96,64},{128,160},{160,128},{192,224},{224,1... | collective-permute-start | bytes 3145736 | tf_op jit(solution)/shard_map/ppermute | solution.py:41
  146.0 28.9 %all-to-all-start.4 = ((bf16[4,128,2048]{2,1,0:T(8,128)(2,1)}), bf16[4,128,2048]{2,1,0:T(8,128)(2,1)}, u32[]{:S(2)}, u32[]{:S(2)}) async-start(bf16[4,128,2048]{2,1,0:T(8,128)(2,1)} %bitcast.14), calls=%async_computation.4 | async-start | bytes 4194304 | tf_op jit(solution)/shard_map/all_to_all | solution.py:46
  150.5 4.2 %collective-permute-start.27 = (bf16[512,768]{1,0:T(8,128)(2,1)}, bf16[512,768]{1,0:T(8,128)(2,1)S(1)}, u32[]{:S(2)}, u32[]{:S(2)}) collective-permute-start(bf16[512,768]{1,0:T(8,128)(2,1)} %get-tuple-element.52), channel_id=1, source_target_pairs={{0,32},{32,0},{64,96},{96,64},{128,160},{160,128},{192,224},{224,1... | collective-permute-start | bytes 2359304 | tf_op jit(solution)/shard_map/ppermute | solution.py:41
  152.5 9.1 %collective-permute-start.22 = (bf16[512,1024]{1,0:T(8,128)(2,1)}, bf16[512,1024]{1,0:T(8,128)(2,1)S(1)}, u32[]{:S(2)}, u32[]{:S(2)}) collective-permute-start(bf16[512,1024]{1,0:T(8,128)(2,1)} %get-tuple-element.46), channel_id=1, source_target_pairs={{0,32},{32,0},{64,96},{96,64},{128,160},{160,128},{192,224},{224,1... | collective-permute-start | bytes 3145736 | tf_op jit(solution)/shard_map/ppermute | solution.py:41
  152.6 6.5 %collective-permute-start.26 = (bf16[512,768]{1,0:T(8,128)(2,1)}, bf16[512,768]{1,0:T(8,128)(2,1)S(1)}, u32[]{:S(2)}, u32[]{:S(2)}) collective-permute-start(bf16[512,768]{1,0:T(8,128)(2,1)} %get-tuple-element.49), channel_id=1, source_target_pairs={{0,32},{32,0},{64,96},{96,64},{128,160},{160,128},{192,224},{224,1... | collective-permute-start | bytes 2359304 | tf_op jit(solution)/shard_map/ppermute | solution.py:41
  153.0 8.6 %collective-permute-start.29 = (bf16[512,768]{1,0:T(8,128)(2,1)}, bf16[512,768]{1,0:T(8,128)(2,1)S(1)}, u32[]{:S(2)}, u32[]{:S(2)}) collective-permute-start(bf16[512,768]{1,0:T(8,128)(2,1)} %get-tuple-element.54), channel_id=1, source_target_pairs={{0,32},{32,0},{64,96},{96,64},{128,160},{160,128},{192,224},{224,1... | collective-permute-start | bytes 2359304 | tf_op jit(solution)/shard_map/ppermute | solution.py:41
  161.6 1.1 copy-start.1
  169.4 20.6 %collective-permute-start.21 = (bf16[64,2048]{1,0:T(8,128)(2,1)S(1)}, bf16[64,2048]{1,0:T(8,128)(2,1)S(1)}, u32[]{:S(2)}, u32[]{:S(2)}) collective-permute-start(bf16[64,2048]{1,0:T(8,128)(2,1)S(1)} %get-tuple-element.45), channel_id=1, source_target_pairs={{0,16},{1,17},{2,18},{3,19},{4,20},{5,21},{6,22},{7,23},{8,24},{9,... | collective-permute-start | bytes 786440 | tf_op jit(solution)/shard_map/ppermute | solution.py:452
  177.6 29.6 %all-to-all-start.5 = ((bf16[8,16,2048]{2,1,0:T(8,128)(2,1)}), bf16[8,16,2048]{2,1,0:T(8,128)(2,1)S(1)}, u32[]{:S(2)}, u32[]{:S(2)}) async-start(bf16[8,16,2048]{2,1,0:T(8,128)(2,1)} %bitcast.16), calls=%async_computation.5 | async-start | bytes 1048576 | tf_op jit(solution)/shard_map/all_to_all | solution.py:46
  190.6 6.0 %collective-permute-start.30 = (bf16[16,2048]{1,0:T(8,128)(2,1)S(1)}, bf16[16,2048]{1,0:T(8,128)(2,1)S(1)}, u32[]{:S(2)}, u32[]{:S(2)}) collective-permute-start(bf16[16,2048]{1,0:T(8,128)(2,1)S(1)} %get-tuple-element.59), channel_id=1, source_target_pairs={{0,28},{1,29},{2,30},{3,31},{4,0},{5,1},{6,2},{7,3},{8,4},{9,5},{1... | collective-permute-start | bytes 196616 | tf_op jit(solution)/shard_map/ppermute | solution.py:456
  193.3 6.3 %collective-permute-start.31 = (bf16[16,2048]{1,0:T(8,128)(2,1)S(1)}, bf16[16,2048]{1,0:T(8,128)(2,1)S(1)}, u32[]{:S(2)}, u32[]{:S(2)}) collective-permute-start(bf16[16,2048]{1,0:T(8,128)(2,1)S(1)} %get-tuple-element.60), channel_id=1, source_target_pairs={{0,4},{1,5},{2,6},{3,7},{4,8},{5,9},{6,10},{7,11},{8,12},{9,13},{1... | collective-permute-start | bytes 196616 | tf_op jit(solution)/shard_map/ppermute | solution.py:456
  193.3 8.8 %collective-permute-start.32 = (bf16[16,2048]{1,0:T(8,128)(2,1)S(1)}, bf16[16,2048]{1,0:T(8,128)(2,1)S(1)}, u32[]{:S(2)}, u32[]{:S(2)}) collective-permute-start(bf16[16,2048]{1,0:T(8,128)(2,1)S(1)} %get-tuple-element.61), channel_id=1, source_target_pairs={{0,8},{1,9},{2,10},{3,11},{4,12},{5,13},{6,14},{7,15},{8,16},{9,17... | collective-permute-start | bytes 196616 | tf_op jit(solution)/shard_map/ppermute | solution.py:456
  202.1 4.4 %collective-permute-start.33 = (bf16[16,1024]{1,0:T(8,128)(2,1)S(1)}, bf16[16,1024]{1,0:T(8,128)(2,1)S(1)}, u32[]{:S(2)}, u32[]{:S(2)}) collective-permute-start(bf16[16,1024]{1,0:T(8,128)(2,1)S(1)} %slice.27), channel_id=1, source_target_pairs={{0,32},{32,0},{64,96},{96,64},{128,160},{160,128},{192,224},{224,1... | collective-permute-start | bytes 98312 | tf_op jit(solution)/shard_map/ppermute | solution.py:41
  207.3 1.3 collective-permute-start.34

commit v5 on v4

--- a/solution.py
+++ b/solution.py
@@ -416,7 +416,7 @@
     other_y = jnp.concatenate(gather_blocks(other, "col", Y_STEP), axis=0)
     other_blocks = ring_eight(other_y, "col", Z_UP, Z_DOWN)
     own_z = share(own, "col", Z_GROUPS)
-    own_all = share(after(own_z, other_blocks[7]), "col", Y_GROUPS)
+    own_all = share(after(own_z, other_y), "col", Y_GROUPS)
 
     gate_up_term, tok_other = gate_up_product(
         zyx, own_all, other_blocks, gate_own, gate_other, up_own, up_other

time: 212 us -> 211 us (level)
  waiting for transfers between devices: 69.2 us -> 57 us
  starting transfers between devices: 81.4 us -> 92.2 us
    ppermute x9, waiting for transfers between devices: 21.6 us -> 9.98 us  [gather_blocks(): lax.ppermute(own, axis, steps[count - k])]
    ppermute x12, starting transfers between devices: 16.5 us -> 25.8 us  [swap_core(): return lax.ppermute(value, 'row', CORE_PAIRS)]
    all_to_all x6, starting transfers between devices: 33.7 us -> 38 us  [exchange(): lax.all_to_all(value, axis, 0, 0, axis_index_groups=groups, tiled=True)]
    ppermute x3, waiting for transfers between devices: 8.91 us -> 4.79 us  [ring_eight(): behind.append(lax.ppermute(behind[-1], axis, down))]
    ppermute x4, waiting for transfers between devices: 10.6 us -> 13.1 us  [ring_eight(): before.append(lax.ppermute(before[-1], axis, up))]
  transfers between devices with their start and end apart: 41 -> 41, of which waited for: 23 -> 21; matrix products, arithmetic and copies ran while one was open for 9% -> 9% of each run, Pallas kernels for 14% -> 14%
where the time goes in v5:
time: 211 us; the launch traced here: 208 us
  starting transfers between devices  92.2 us (44%)
  waiting for transfers between devices  57 us (27%)
  Pallas kernels  35.1 us (17%)
  matrix products  13.4 us (6%)
  local copies, waits for them, and re-layouts  5.3 us (3%)
  other arithmetic  3.97 us (2%)
    all_to_all x6, starting transfers between devices, exchange(): lax.all_to_all(value, axis, 0, 0, axis_index_groups=groups, tiled=True)  38 us
    ppermute x12, starting transfers between devices, swap_core(): return lax.ppermute(value, 'row', CORE_PAIRS)  25.8 us
    all_to_all x6, waiting for transfers between devices, exchange(): lax.all_to_all(value, axis, 0, 0, axis_index_groups=groups, tiled=True)  13.7 us
    dot_general x3, matrix products, dot(): return lax.dot_general(left, right, dims, preferred_element_type=F32)  13.4 us
    ppermute x4, waiting for transfers between devices, ring_eight(): before.append(lax.ppermute(before[-1], axis, up))  13.1 us
    ppermute x9, starting transfers between devices, gather_blocks(): lax.ppermute(own, axis, steps[count - k])  11.2 us
    ppermute x9, waiting for transfers between devices, gather_blocks(): lax.ppermute(own, axis, steps[count - k])  9.98 us
    ppermute x3, starting transfers between devices, ring_eight(): behind.append(lax.ppermute(behind[-1], axis, down))  8.3 us
  transfers between devices with their start and end apart: 41, of which 21 were waited for; matrix products, arithmetic and copies ran while one was open for 9% of the time, Pallas kernels for 14%

profile of v5, /device:TPU:1, one launch (start us, length us, event | category | flops | bytes accessed | tf_op | source)
XLA Modules:
  0.0 207.8 jit_solution(5672566917376555161)
XLA Ops:
  0.7 0.8 constant_dynamic-slice_fusion.1
  1.4 0.8 constant_dynamic-slice_fusion
  2.2 0.8 tile.4
  3.1 9.0 %all-to-all-start = ((bf16[8,16,2048]{2,1,0:T(8,128)(2,1)}), bf16[8,16,2048]{2,1,0:T(8,128)(2,1)S(1)}, u32[]{:S(2)}, u32[]{:S(2)}) async-start(bf16[8,16,2048]{2,1,0:T(8,128)(2,1)} %tile.4), calls=%async_computation | async-start | bytes 1048576 | tf_op jit(solution)/shard_map/all_to_all | solution.py:46
  12.1 1.0 collective-permute-start
  13.1 0.8 collective-permute-done
  14.3 1.3 collective-permute-start.4
  15.6 2.6 %collective-permute-start.3 = (bf16[16,2048]{1,0:T(8,128)(2,1)S(1)}, bf16[16,2048]{1,0:T(8,128)(2,1)S(1)}, u32[]{:S(2)}, u32[]{:S(2)}) collective-permute-start(bf16[16,2048]{1,0:T(8,128)(2,1)S(1)} %constant_dynamic-update-slice_fusion), channel_id=1, source_target_pairs={{0,2},{1,3},{2,0},{3,1},{4,6},{5,7},{6,4},{7,5},{8,10},{9,11},{10,... | collective-permute-start | bytes 196616 | tf_op jit(solution)/shard_map/ppermute | solution.py:61
  18.2 1.1 collective-permute-start.2
  19.2 1.0 collective-permute-start.16
  20.3 1.4 collective-permute-done.3
  21.7 8.4 %all-to-all-done = bf16[8,16,2048]{2,1,0:T(8,128)(2,1)S(1)} async-done(((bf16[8,16,2048]{2,1,0:T(8,128)(2,1)}), bf16[8,16,2048]{2,1,0:T(8,128)(2,1)S(1)}, u32[]{:S(2)}, u32[]{:S(2)}) %all-to-all-start) | async-done | bytes 524320 | tf_op jit(solution)/shard_map/all_to_all | solution.py:46
  30.0 1.6 tile.5
  31.7 4.2 %all-to-all-start.1 = ((bf16[4,128,2048]{2,1,0:T(8,128)(2,1)}), bf16[4,128,2048]{2,1,0:T(8,128)(2,1)S(1)}, u32[]{:S(2)}, u32[]{:S(2)}) async-start(bf16[4,128,2048]{2,1,0:T(8,128)(2,1)} %tile.5), calls=%async_computation.1 | async-start | bytes 4194304 | tf_op jit(solution)/shard_map/all_to_all | solution.py:46
  35.9 2.7 %collective-permute-start.5 = (bf16[64,2048]{1,0:T(8,128)(2,1)S(1)}, bf16[64,2048]{1,0:T(8,128)(2,1)S(1)}, u32[]{:S(2)}, u32[]{:S(2)}) collective-permute-start(bf16[64,2048]{1,0:T(8,128)(2,1)S(1)} %pad_maximum_fusion.4.refs_0_), channel_id=1, source_target_pairs={{4,0},{5,1},{6,2},{7,3},{8,4},{9,5},{10,6},{11,7},{12,8},{13,9},{1... | collective-permute-start | bytes 786440 | tf_op jit(solution)/shard_map/ppermute | solution.py:69
  38.5 5.6 %collective-permute-done.8.refs_7_ = bf16[64,2048]{1,0:T(8,128)(2,1)S(1)} collective-permute-done((bf16[64,2048]{1,0:T(8,128)(2,1)S(1)}, bf16[64,2048]{1,0:T(8,128)(2,1)S(1)}, u32[]{:S(2)}, u32[]{:S(2)}) %collective-permute-start.8) | collective-permute-done | bytes 262176 | tf_op jit(solution)/shard_map/ppermute | solution.py:67
  44.1 2.7 %collective-permute-start.6 = (bf16[64,2048]{1,0:T(8,128)(2,1)S(1)}, bf16[64,2048]{1,0:T(8,128)(2,1)}, u32[]{:S(2)}, u32[]{:S(2)}) collective-permute-start(bf16[64,2048]{1,0:T(8,128)(2,1)S(1)} %collective-permute-done.5.refs_1_), channel_id=1, source_target_pairs={{4,0},{5,1},{6,2},{7,3},{8,4},{9,5},{10,6},{11,7},{12,8},{13,9},{1... | collective-permute-start | bytes 786440 | tf_op jit(solution)/shard_map/ppermute | solution.py:69
  46.8 4.7 %collective-permute-done.9.refs_6_ = bf16[64,2048]{1,0:T(8,128)(2,1)S(1)} collective-permute-done((bf16[64,2048]{1,0:T(8,128)(2,1)S(1)}, bf16[64,2048]{1,0:T(8,128)(2,1)S(1)}, u32[]{:S(2)}, u32[]{:S(2)}) %collective-permute-start.9) | collective-permute-done | bytes 262176 | tf_op jit(solution)/shard_map/ppermute | solution.py:67
  51.5 2.6 %collective-permute-start.12 = (bf16[768,1024]{1,0:T(8,128)(2,1)}, bf16[768,1024]{1,0:T(8,128)(2,1)}, u32[]{:S(2)}, u32[]{:S(2)}) collective-permute-start(bf16[768,1024]{1,0:T(8,128)(2,1)} %refs_4_.2), channel_id=1, source_target_pairs={{0,32},{32,0},{64,96},{96,64},{128,160},{160,128},{192,224},{224,1... | collective-permute-start | bytes 4718600 | tf_op jit(solution)/shard_map/ppermute | solution.py:41
  54.1 3.0 %collective-permute-start.7 = (bf16[64,2048]{1,0:T(8,128)(2,1)}, bf16[64,2048]{1,0:T(8,128)(2,1)S(1)}, u32[]{:S(2)}, u32[]{:S(2)}) collective-permute-start(bf16[64,2048]{1,0:T(8,128)(2,1)} %collective-permute-done.6.refs_2_), channel_id=1, source_target_pairs={{4,0},{5,1},{6,2},{7,3},{8,4},{9,5},{10,6},{11,7},{12,8},{13,9},{1... | collective-permute-start | bytes 786440 | tf_op jit(solution)/shard_map/ppermute | solution.py:69
  57.0 1.2 collective-permute-done.10.refs_5_
  58.3 4.8 %collective-permute-done.7.refs_3_ = bf16[64,2048]{1,0:T(8,128)(2,1)S(1)} collective-permute-done((bf16[64,2048]{1,0:T(8,128)(2,1)}, bf16[64,2048]{1,0:T(8,128)(2,1)S(1)}, u32[]{:S(2)}, u32[]{:S(2)}) %collective-permute-start.7) | collective-permute-done | bytes 262176 | tf_op jit(solution)/shard_map/ppermute | solution.py:69
  63.1 1.7 collective-permute-done.11.refs_4_
  64.8 7.4 %shard_map.93 = (bf16[512,1536]{1,0:T(8,128)(2,1)}, bf16[512,1024]{1,0:T(8,128)(2,1)}) custom-call(s32[3]{0:T(128)S(1)} %pad_add_fusion.index, bf16[512,2048]{1,0:T(8,128)(2,1)S(1)} %bitcast.10, bf16[64,2048]{1,0:T(8,128)(2,1)S(1)} %pad_maximum_fusion.4.refs_0_, bf16[64,2048]{1,0:T(8,128)(2,1)S(1)} %collective-permute-done.5.refs_1_, ...), custom_call_target="tpu_custom_call" | custom-call | flops 3221225472 | bytes 10485760 | tf_op jit(solution)/shard_map/pallas_call | solution.py:144
  72.1 4.5 %all-to-all-start.2 = ((bf16[4,128,1536]{2,1,0:T(8,128)(2,1)}), bf16[4,128,1536]{2,1,0:T(8,128)(2,1)}, u32[]{:S(2)}, u32[]{:S(2)}) async-start(bf16[4,128,1536]{2,1,0:T(8,128)(2,1)} %bitcast.17), calls=%async_computation.2 | async-start | bytes 3145728 | tf_op jit(solution)/shard_map/all_to_all | solution.py:46
  76.7 5.6 %shard_map.92 = (bf16[128,768]{1,0:T(8,128)(2,1)}, bf16[128,768]{1,0:T(8,128)(2,1)}, bf16[128,768]{1,0:T(8,128)(2,1)}, bf16[128,768]{1,0:T(8,128)(2,1)}, bf16[512,1024]{1,0:T(8,128)(2,1)}) custom-call(s32[3]{0:T(128)S(1)} %pad_add_fusion.index, bf16[512,2048]{1,0:T(8,128)(2,1)S(1)} %bitcast.11, bf16[64,2048]{1,0:T(8,128)(2,1)S(1)} %pad_maximum_fusion.4.refs_0_, ...), custom_call_target="tpu_custom_call" | custom-call | flops 1610612736 | bytes 10485760 | tf_op jit(solution)/shard_map/pallas_call | solution.py:180
  82.3 1.3 collective-permute-start.13
  83.5 2.4 %collective-permute-start.14 = (bf16[128,768]{1,0:T(8,128)(2,1)}, bf16[128,768]{1,0:T(8,128)(2,1)S(1)}, u32[]{:S(2)}, u32[]{:S(2)}) collective-permute-start(bf16[128,768]{1,0:T(8,128)(2,1)} %get-tuple-element.37), channel_id=1, source_target_pairs={{0,128},{32,160},{64,192},{96,224},{128,0},{160,32},{192,64},{224,... | collective-permute-start | bytes 589832 | tf_op jit(solution)/shard_map/ppermute | solution.py:429
  86.0 1.2 collective-permute-start.15
  87.1 5.3 %all-to-all-done.2.terms = bf16[4,128,1536]{2,1,0:T(8,128)(2,1)} async-done(((bf16[4,128,1536]{2,1,0:T(8,128)(2,1)}), bf16[4,128,1536]{2,1,0:T(8,128)(2,1)}, u32[]{:S(2)}, u32[]{:S(2)}) %all-to-all-start.2) | async-done | bytes 1572896 | tf_op jit(solution)/shard_map/all_to_all | solution.py:46
  92.4 2.5 %shard_map.94 = (f32[128,1536]{1,0:T(8,128)}, bf16[128,768]{1,0:T(8,128)(2,1)S(1)}) custom-call(s32[1]{0:T(128)} %bitcast.2.index, bf16[4,128,1536]{2,1,0:T(8,128)(2,1)} %all-to-all-done.2.terms), custom_call_target="tpu_custom_call" | custom-call | flops 3145728 | bytes 10485760 | tf_op jit(solution)/shard_map/pallas_call | solution.py:278
  95.2 1.8 collective-permute-start.19
  97.6 3.6 %collective-permute-done.14.refs_2_ = bf16[128,768]{1,0:T(8,128)(2,1)S(1)} collective-permute-done((bf16[128,768]{1,0:T(8,128)(2,1)}, bf16[128,768]{1,0:T(8,128)(2,1)S(1)}, u32[]{:S(2)}, u32[]{:S(2)}) %collective-permute-start.14) | collective-permute-done | bytes 196640 | tf_op jit(solution)/shard_map/ppermute | solution.py:429
  101.2 1.5 shard_map.95.refs_0_
  102.7 4.0 %collective-permute-done.20.refs_3_ = bf16[128,768]{1,0:T(8,128)(2,1)S(1)} collective-permute-done((bf16[128,768]{1,0:T(8,128)(2,1)S(1)}, bf16[128,768]{1,0:T(8,128)(2,1)S(1)}, u32[]{:S(2)}, u32[]{:S(2)}) %collective-permute-start.20) | collective-permute-done | bytes 196640 | tf_op jit(solution)/shard_map/ppermute | solution.py:61
  106.7 2.8 %collective-permute-done.19.refs_2_ = bf16[128,768]{1,0:T(8,128)(2,1)S(1)} collective-permute-done((bf16[128,768]{1,0:T(8,128)(2,1)S(1)}, bf16[128,768]{1,0:T(8,128)(2,1)S(1)}, u32[]{:S(2)}, u32[]{:S(2)}) %collective-permute-start.19) | collective-permute-done | bytes 196640 | tf_op jit(solution)/shard_map/ppermute | solution.py:61
  109.5 5.2 %shard_map.96 = (bf16[512,2048]{1,0:T(8,128)(2,1)}, bf16[512,768]{1,0:T(8,128)(2,1)}) custom-call(s32[1]{0:T(128)} %bitcast.2.index, bf16[128,768]{1,0:T(8,128)(2,1)S(1)} %get-tuple-element.42.refs_0_, bf16[128,768]{1,0:T(8,128)(2,1)S(1)} %collective-permute-done.18.refs_1_, bf16[128,768]{1,0:T(8,128)(2,1)S(1)} %collective-permute-done.19.refs_2_, ...), custom_call_target="tpu_custom_call" | custom-call | flops 1610612736 | bytes 10485760 | tf_op jit(solution)/shard_map/pallas_call | solution.py:213
  114.7 4.5 %all-to-all-start.3 = ((bf16[4,128,2048]{2,1,0:T(8,128)(2,1)}), bf16[4,128,2048]{2,1,0:T(8,128)(2,1)}, u32[]{:S(2)}, u32[]{:S(2)}) async-start(bf16[4,128,2048]{2,1,0:T(8,128)(2,1)} %bitcast.15), calls=%async_computation.3 | async-start | bytes 4194304 | tf_op jit(solution)/shard_map/all_to_all | solution.py:46
  119.2 1.1 collective-permute-start.25
  120.2 1.2 collective-permute-start.24
  121.5 1.3 collective-permute-start.23
  122.7 8.7 %collective-permute-start.28 = (bf16[512,1024]{1,0:T(8,128)(2,1)}, bf16[512,1024]{1,0:T(8,128)(2,1)}, u32[]{:S(2)}, u32[]{:S(2)}) collective-permute-start(bf16[512,1024]{1,0:T(8,128)(2,1)} %get-tuple-element.53), channel_id=1, source_target_pairs={{0,32},{32,0},{64,96},{96,64},{128,160},{160,128},{192,224},{224,1... | collective-permute-start | bytes 3145736 | tf_op jit(solution)/shard_map/ppermute | solution.py:41
  132.0 1.2 collective-permute-done.23.refs_1_
  133.2 7.2 %shard_map.98 = (bf16[512,2048]{1,0:T(8,128)(2,1)}, bf16[512,768]{1,0:T(8,128)(2,1)}, bf16[512,768]{1,0:T(8,128)(2,1)}) custom-call(s32[1]{0:T(128)} %bitcast.2.index, bf16[128,1536]{1,0:T(8,128)(2,1)S(1)} %shard_map.95.refs_0_, bf16[128,1536]{1,0:T(8,128)(2,1)S(1)} %collective-permute-done.23.refs_1_, ...), custom_call_target="tpu_custom_call" | custom-call | flops 3221225472 | bytes 10485760 | tf_op jit(solution)/shard_map/pallas_call | solution.py:249
  140.4 4.5 %all-to-all-start.4 = ((bf16[4,128,2048]{2,1,0:T(8,128)(2,1)}), bf16[4,128,2048]{2,1,0:T(8,128)(2,1)}, u32[]{:S(2)}, u32[]{:S(2)}) async-start(bf16[4,128,2048]{2,1,0:T(8,128)(2,1)} %bitcast.14), calls=%async_computation.4 | async-start | bytes 4194304 | tf_op jit(solution)/shard_map/all_to_all | solution.py:46
  144.9 8.0 %collective-permute-start.27 = (bf16[512,768]{1,0:T(8,128)(2,1)}, bf16[512,768]{1,0:T(8,128)(2,1)S(1)}, u32[]{:S(2)}, u32[]{:S(2)}) collective-permute-start(bf16[512,768]{1,0:T(8,128)(2,1)} %get-tuple-element.52), channel_id=1, source_target_pairs={{0,32},{32,0},{64,96},{96,64},{128,160},{160,128},{192,224},{224,1... | collective-permute-start | bytes 2359304 | tf_op jit(solution)/shard_map/ppermute | solution.py:41
  153.7 1.3 collective-permute-done.27
  155.0 4.5 %fusion.4 = bf16[768,1024]{1,0:T(8,128)(2,1)} fusion(bf16[512,1024]{1,0:T(8,128)(2,1)} %collective-permute-done.28, bf16[512,1024]{1,0:T(8,128)(2,1)S(1)} %get-tuple-element.64, bf16[512,768]{1,0:T(8,128)(2,1)S(1)} %collective-permute-done.27, bf16[512,768]{1,0:T(8,128)(2,1)} %get-tuple-element.52), kind=kOutput, calls=%fused_computation.5 | convolution fusion | flops 1618739200 | bytes 5242880 | tf_op jit(solution)/shard_map/dot_general | solution.py:37
  159.4 2.5 %pad_maximum_fusion.1 = bf16[1024,768]{1,0:T(8,128)(2,1)} fusion(bf16[512,768]{1,0:T(8,128)(2,1)S(1)} %collective-permute-done.26, bf16[512,768]{1,0:T(8,128)(2,1)} %get-tuple-element.49), kind=kLoop, calls=%fused_computation.8 | loop fusion | flops 3145728 | bytes 3145728 | tf_op jit(solution)/shard_map/concatenate | solution.py:442
  161.9 1.1 copy-done.1
  163.0 4.2 %convolution_convert_fusion.1 = bf16[1024,768]{1,0:T(8,128)(2,1)} fusion(bf16[512,768]{1,0:T(8,128)(2,1)S(1)} %collective-permute-done.29, bf16[512,768]{1,0:T(8,128)(2,1)} %get-tuple-element.54, bf16[512,1024]{1,0:T(8,128)(2,1)S(1)} %collective-permute-done.22, bf16[512,1024]{1,0:T(8,128)(2,1)S(1)} %get-tuple-element.63), kind=kOutput, calls=%fused_computation.7 | convolution fusion | flops 1618739200 | bytes 5242880 | tf_op jit(solution)/shard_map/dot_general | solution.py:37
  167.2 2.5 %shard_map.97 = (bf16[64,2048]{1,0:T(8,128)(2,1)S(1)}, bf16[64,2048]{1,0:T(8,128)(2,1)S(1)}) custom-call(s32[3]{0:T(128)S(1)} %pad_add_fusion.index, bf16[4,128,2048]{2,1,0:T(8,128)(2,1)} %all-to-all-done.3.terms), custom_call_target="tpu_custom_call" | custom-call | flops 2097152 | bytes 10485760 | tf_op jit(solution)/shard_map/pallas_call | solution.py:356
  169.8 2.7 %shard_map.99 = bf16[128,2048]{1,0:T(8,128)(2,1)} custom-call(s32[1]{0:T(128)} %bitcast.2.index, bf16[4,128,2048]{2,1,0:T(8,128)(2,1)} %all-to-all-done.4.terms), custom_call_target="tpu_custom_call" | custom-call | flops 2097152 | bytes 10485760 | tf_op jit(solution)/shard_map/pallas_call | solution.py:334
  172.5 11.3 %all-to-all-start.5 = ((bf16[8,16,2048]{2,1,0:T(8,128)(2,1)}), bf16[8,16,2048]{2,1,0:T(8,128)(2,1)S(1)}, u32[]{:S(2)}, u32[]{:S(2)}) async-start(bf16[8,16,2048]{2,1,0:T(8,128)(2,1)} %bitcast.16), calls=%async_computation.5 | async-start | bytes 1048576 | tf_op jit(solution)/shard_map/all_to_all | solution.py:46
  183.8 4.7 %convolution_convert_fusion = bf16[1024,768]{1,0:T(8,128)(2,1)} fusion(bf16[1024,768]{1,0:T(8,128)(2,1)} %pad_maximum_fusion.1, bf16[512,1024]{1,0:T(8,128)(2,1)} %copy-done.1, bf16[512,1024]{1,0:T(8,128)(2,1)S(1)} %get-tuple-element.63), kind=kOutput, calls=%fused_computation.6 | convolution fusion | flops 1615593472 | bytes 5242880 | tf_op jit(solution)/shard_map/dot_general | solution.py:37
  189.2 2.8 %collective-permute-start.30 = (bf16[16,2048]{1,0:T(8,128)(2,1)S(1)}, bf16[16,2048]{1,0:T(8,128)(2,1)S(1)}, u32[]{:S(2)}, u32[]{:S(2)}) collective-permute-start(bf16[16,2048]{1,0:T(8,128)(2,1)S(1)} %get-tuple-element.59), channel_id=1, source_target_pairs={{0,28},{1,29},{2,30},{3,31},{4,0},{5,1},{6,2},{7,3},{8,4},{9,5},{1... | collective-permute-start | bytes 196616 | tf_op jit(solution)/shard_map/ppermute | solution.py:456
  191.9 1.2 collective-permute-start.32
  193.1 2.2 %collective-permute-done.30 = bf16[16,2048]{1,0:T(8,128)(2,1)S(1)} collective-permute-done((bf16[16,2048]{1,0:T(8,128)(2,1)S(1)}, bf16[16,2048]{1,0:T(8,128)(2,1)S(1)}, u32[]{:S(2)}, u32[]{:S(2)}) %collective-permute-start.30) | collective-permute-done | bytes 65568 | tf_op jit(solution)/shard_map/ppermute | solution.py:456
  195.3 2.6 %collective-permute-done.31 = bf16[16,2048]{1,0:T(8,128)(2,1)S(1)} collective-permute-done((bf16[16,2048]{1,0:T(8,128)(2,1)S(1)}, bf16[16,2048]{1,0:T(8,128)(2,1)S(1)}, u32[]{:S(2)}, u32[]{:S(2)}) %collective-permute-start.31) | collective-permute-done | bytes 65568 | tf_op jit(solution)/shard_map/ppermute | solution.py:456
  197.8 2.9 %collective-permute-done.32 = bf16[16,2048]{1,0:T(8,128)(2,1)S(1)} collective-permute-done((bf16[16,2048]{1,0:T(8,128)(2,1)S(1)}, bf16[16,2048]{1,0:T(8,128)(2,1)S(1)}, u32[]{:S(2)}, u32[]{:S(2)}) %collective-permute-start.32) | collective-permute-done | bytes 65568 | tf_op jit(solution)/shard_map/ppermute | solution.py:456
  200.8 3.4 %collective-permute-start.33 = (bf16[16,1024]{1,0:T(8,128)(2,1)S(1)}, bf16[16,1024]{1,0:T(8,128)(2,1)S(1)}, u32[]{:S(2)}, u32[]{:S(2)}) collective-permute-start(bf16[16,1024]{1,0:T(8,128)(2,1)S(1)} %slice.27), channel_id=1, source_target_pairs={{0,32},{32,0},{64,96},{96,64},{128,160},{160,128},{192,224},{224,1... | collective-permute-start | bytes 98312 | tf_op jit(solution)/shard_map/ppermute | solution.py:41
  204.2 0.9 collective-permute-done.33
  205.1 0.6 pad_maximum_fusion.6
  206.3 0.9 collective-permute-done.34
  (53 shorter events, 4.8 us)
Async XLA Ops:
  3.1 27.0 %all-to-all-start = ((bf16[8,16,2048]{2,1,0:T(8,128)(2,1)}), bf16[8,16,2048]{2,1,0:T(8,128)(2,1)S(1)}, u32[]{:S(2)}, u32[]{:S(2)}) async-start(bf16[8,16,2048]{2,1,0:T(8,128)(2,1)} %tile.4), calls=%async_computation | async-start | bytes 1048576 | tf_op jit(solution)/shard_map/all_to_all | solution.py:46
  12.1 1.8 collective-permute-start
  13.0 1.2 collective-permute-start.1
  14.3 6.0 %collective-permute-start.4 = (bf16[16,2048]{1,0:T(8,128)(2,1)S(1)}, bf16[16,2048]{1,0:T(8,128)(2,1)S(1)}, u32[]{:S(2)}, u32[]{:S(2)}) collective-permute-start(bf16[16,2048]{1,0:T(8,128)(2,1)S(1)} %constant_dynamic-update-slice_fusion), channel_id=1, source_target_pairs={{0,1},{1,2},{2,3},{3,0},{4,5},{5,6},{6,7},{7,4},{8,9},{9,10},{10,1... | collective-permute-start | bytes 196616 | tf_op jit(solution)/shard_map/ppermute | solution.py:61
  15.6 6.1 %collective-permute-start.3 = (bf16[16,2048]{1,0:T(8,128)(2,1)S(1)}, bf16[16,2048]{1,0:T(8,128)(2,1)S(1)}, u32[]{:S(2)}, u32[]{:S(2)}) collective-permute-start(bf16[16,2048]{1,0:T(8,128)(2,1)S(1)} %constant_dynamic-update-slice_fusion), channel_id=1, source_target_pairs={{0,2},{1,3},{2,0},{3,1},{4,6},{5,7},{6,4},{7,5},{8,10},{9,11},{10,... | collective-permute-start | bytes 196616 | tf_op jit(solution)/shard_map/ppermute | solution.py:61
  18.2 3.5 %collective-permute-start.2 = (bf16[16,2048]{1,0:T(8,128)(2,1)S(1)}, bf16[16,2048]{1,0:T(8,128)(2,1)S(1)}, u32[]{:S(2)}, u32[]{:S(2)}) collective-permute-start(bf16[16,2048]{1,0:T(8,128)(2,1)S(1)} %constant_dynamic-update-slice_fusion), channel_id=1, source_target_pairs={{0,3},{1,0},{2,1},{3,2},{4,7},{5,4},{6,5},{7,6},{8,11},{9,8},{10,9... | collective-permute-start | bytes 196616 | tf_op jit(solution)/shard_map/ppermute | solution.py:61
  19.2 45.5 %collective-permute-start.16 = (bf16[1024,768]{1,0:T(8,128)(2,1)}, bf16[1024,768]{1,0:T(8,128)(2,1)}, u32[]{:S(2)}, u32[]{:S(2)}) collective-permute-start(bf16[1024,768]{1,0:T(8,128)(2,1)} %refs_4_.3), channel_id=1, source_target_pairs={{0,32},{32,0},{64,96},{96,64},{128,160},{160,128},{192,224},{224,1... | collective-permute-start | bytes 4718600 | tf_op jit(solution)/shard_map/ppermute | solution.py:41
  20.2 44.5 %collective-permute-start.17 = (bf16[1024,768]{1,0:T(8,128)(2,1)}, bf16[1024,768]{1,0:T(8,128)(2,1)}, u32[]{:S(2)}, u32[]{:S(2)}) collective-permute-start(bf16[1024,768]{1,0:T(8,128)(2,1)} %refs_5_.1), channel_id=1, source_target_pairs={{0,32},{32,0},{64,96},{96,64},{128,160},{160,128},{192,224},{224,1... | collective-permute-start | bytes 4718600 | tf_op jit(solution)/shard_map/ppermute | solution.py:41
  31.7 33.1 %all-to-all-start.1 = ((bf16[4,128,2048]{2,1,0:T(8,128)(2,1)}), bf16[4,128,2048]{2,1,0:T(8,128)(2,1)S(1)}, u32[]{:S(2)}, u32[]{:S(2)}) async-start(bf16[4,128,2048]{2,1,0:T(8,128)(2,1)} %tile.5), calls=%async_computation.1 | async-start | bytes 4194304 | tf_op jit(solution)/shard_map/all_to_all | solution.py:46
  35.8 8.3 %collective-permute-start.8 = (bf16[64,2048]{1,0:T(8,128)(2,1)S(1)}, bf16[64,2048]{1,0:T(8,128)(2,1)S(1)}, u32[]{:S(2)}, u32[]{:S(2)}) collective-permute-start(bf16[64,2048]{1,0:T(8,128)(2,1)S(1)} %pad_maximum_fusion.4.refs_0_), channel_id=1, source_target_pairs={{0,4},{1,5},{2,6},{3,7},{4,8},{5,9},{6,10},{7,11},{8,12},{9,13},{1... | collective-permute-start | bytes 786440 | tf_op jit(solution)/shard_map/ppermute | solution.py:67
  35.9 8.3 %collective-permute-start.5 = (bf16[64,2048]{1,0:T(8,128)(2,1)S(1)}, bf16[64,2048]{1,0:T(8,128)(2,1)S(1)}, u32[]{:S(2)}, u32[]{:S(2)}) collective-permute-start(bf16[64,2048]{1,0:T(8,128)(2,1)S(1)} %pad_maximum_fusion.4.refs_0_), channel_id=1, source_target_pairs={{4,0},{5,1},{6,2},{7,3},{8,4},{9,5},{10,6},{11,7},{12,8},{13,9},{1... | collective-permute-start | bytes 786440 | tf_op jit(solution)/shard_map/ppermute | solution.py:69
  44.1 7.3 %collective-permute-start.9 = (bf16[64,2048]{1,0:T(8,128)(2,1)S(1)}, bf16[64,2048]{1,0:T(8,128)(2,1)S(1)}, u32[]{:S(2)}, u32[]{:S(2)}) collective-permute-start(bf16[64,2048]{1,0:T(8,128)(2,1)S(1)} %collective-permute-done.8.refs_7_), channel_id=1, source_target_pairs={{0,4},{1,5},{2,6},{3,7},{4,8},{5,9},{6,10},{7,11},{8,12},{9,13},{1... | collective-permute-start | bytes 786440 | tf_op jit(solution)/shard_map/ppermute | solution.py:67
  44.1 9.9 %collective-permute-start.6 = (bf16[64,2048]{1,0:T(8,128)(2,1)S(1)}, bf16[64,2048]{1,0:T(8,128)(2,1)}, u32[]{:S(2)}, u32[]{:S(2)}) collective-permute-start(bf16[64,2048]{1,0:T(8,128)(2,1)S(1)} %collective-permute-done.5.refs_1_), channel_id=1, source_target_pairs={{4,0},{5,1},{6,2},{7,3},{8,4},{9,5},{10,6},{11,7},{12,8},{13,9},{1... | collective-permute-start | bytes 786440 | tf_op jit(solution)/shard_map/ppermute | solution.py:69
  51.5 6.7 %copy-start = (bf16[64,2048]{1,0:T(8,128)(2,1)}, bf16[64,2048]{1,0:T(8,128)(2,1)S(1)}, u32[]{:S(2)}) copy-start(bf16[64,2048]{1,0:T(8,128)(2,1)S(1)} %collective-permute-done.9.refs_6_) | copy-start | bytes 786436
  51.5 6.7 %collective-permute-start.10 = (bf16[64,2048]{1,0:T(8,128)(2,1)S(1)}, bf16[64,2048]{1,0:T(8,128)(2,1)S(1)}, u32[]{:S(2)}, u32[]{:S(2)}) collective-permute-start(bf16[64,2048]{1,0:T(8,128)(2,1)S(1)} %collective-permute-done.9.refs_6_), channel_id=1, source_target_pairs={{0,4},{1,5},{2,6},{3,7},{4,8},{5,9},{6,10},{7,11},{8,12},{9,13},{1... | collective-permute-start | bytes 786440 | tf_op jit(solution)/shard_map/ppermute | solution.py:67
  51.5 25.2 %collective-permute-start.12 = (bf16[768,1024]{1,0:T(8,128)(2,1)}, bf16[768,1024]{1,0:T(8,128)(2,1)}, u32[]{:S(2)}, u32[]{:S(2)}) collective-permute-start(bf16[768,1024]{1,0:T(8,128)(2,1)} %refs_4_.2), channel_id=1, source_target_pairs={{0,32},{32,0},{64,96},{96,64},{128,160},{160,128},{192,224},{224,1... | collective-permute-start | bytes 4718600 | tf_op jit(solution)/shard_map/ppermute | solution.py:41
  54.1 9.0 %collective-permute-start.7 = (bf16[64,2048]{1,0:T(8,128)(2,1)}, bf16[64,2048]{1,0:T(8,128)(2,1)S(1)}, u32[]{:S(2)}, u32[]{:S(2)}) collective-permute-start(bf16[64,2048]{1,0:T(8,128)(2,1)} %collective-permute-done.6.refs_2_), channel_id=1, source_target_pairs={{4,0},{5,1},{6,2},{7,3},{8,4},{9,5},{10,6},{11,7},{12,8},{13,9},{1... | collective-permute-start | bytes 786440 | tf_op jit(solution)/shard_map/ppermute | solution.py:69
  58.2 6.5 %collective-permute-start.11 = (bf16[64,2048]{1,0:T(8,128)(2,1)S(1)}, bf16[64,2048]{1,0:T(8,128)(2,1)}, u32[]{:S(2)}, u32[]{:S(2)}) collective-permute-start(bf16[64,2048]{1,0:T(8,128)(2,1)S(1)} %collective-permute-done.10.refs_5_), channel_id=1, source_target_pairs={{0,4},{1,5},{2,6},{3,7},{4,8},{5,9},{6,10},{7,11},{8,12},{9,13},{1... | collective-permute-start | bytes 786440 | tf_op jit(solution)/shard_map/ppermute | solution.py:67
  72.1 20.3 %all-to-all-start.2 = ((bf16[4,128,1536]{2,1,0:T(8,128)(2,1)}), bf16[4,128,1536]{2,1,0:T(8,128)(2,1)}, u32[]{:S(2)}, u32[]{:S(2)}) async-start(bf16[4,128,1536]{2,1,0:T(8,128)(2,1)} %bitcast.17), calls=%async_computation.2 | async-start | bytes 3145728 | tf_op jit(solution)/shard_map/all_to_all | solution.py:46
  82.3 14.7 %collective-permute-start.13 = (bf16[128,768]{1,0:T(8,128)(2,1)}, bf16[128,768]{1,0:T(8,128)(2,1)S(1)}, u32[]{:S(2)}, u32[]{:S(2)}) collective-permute-start(bf16[128,768]{1,0:T(8,128)(2,1)} %get-tuple-element.36), channel_id=1, source_target_pairs={{0,64},{32,96},{64,128},{96,160},{128,192},{160,224},{192,0},{224,... | collective-permute-start | bytes 589832 | tf_op jit(solution)/shard_map/ppermute | solution.py:429
  83.5 17.7 %collective-permute-start.14 = (bf16[128,768]{1,0:T(8,128)(2,1)}, bf16[128,768]{1,0:T(8,128)(2,1)S(1)}, u32[]{:S(2)}, u32[]{:S(2)}) collective-permute-start(bf16[128,768]{1,0:T(8,128)(2,1)} %get-tuple-element.37), channel_id=1, source_target_pairs={{0,128},{32,160},{64,192},{96,224},{128,0},{160,32},{192,64},{224,... | collective-permute-start | bytes 589832 | tf_op jit(solution)/shard_map/ppermute | solution.py:429
  86.0 15.2 %collective-permute-start.15 = (bf16[128,768]{1,0:T(8,128)(2,1)}, bf16[128,768]{1,0:T(8,128)(2,1)S(1)}, u32[]{:S(2)}, u32[]{:S(2)}) collective-permute-start(bf16[128,768]{1,0:T(8,128)(2,1)} %get-tuple-element.38), channel_id=1, source_target_pairs={{0,192},{32,224},{64,0},{96,32},{128,64},{160,96},{192,128},{224,1... | collective-permute-start | bytes 589832 | tf_op jit(solution)/shard_map/ppermute | solution.py:429
  94.9 11.8 %collective-permute-start.20 = (bf16[128,768]{1,0:T(8,128)(2,1)S(1)}, bf16[128,768]{1,0:T(8,128)(2,1)S(1)}, u32[]{:S(2)}, u32[]{:S(2)}) collective-permute-start(bf16[128,768]{1,0:T(8,128)(2,1)S(1)} %get-tuple-element.42.refs_0_), channel_id=1, source_target_pairs={{0,64},{32,96},{64,128},{96,160},{128,192},{160,224},{192,0},{224,... | collective-permute-start | bytes 589832 | tf_op jit(solution)/shard_map/ppermute | solution.py:61
  95.2 14.3 %collective-permute-start.19 = (bf16[128,768]{1,0:T(8,128)(2,1)S(1)}, bf16[128,768]{1,0:T(8,128)(2,1)S(1)}, u32[]{:S(2)}, u32[]{:S(2)}) collective-permute-start(bf16[128,768]{1,0:T(8,128)(2,1)S(1)} %get-tuple-element.42.refs_0_), channel_id=1, source_target_pairs={{0,128},{32,160},{64,192},{96,224},{128,0},{160,32},{192,64},{224,... | collective-permute-start | bytes 589832 | tf_op jit(solution)/shard_map/ppermute | solution.py:61
  97.0 12.5 %collective-permute-start.18 = (bf16[128,768]{1,0:T(8,128)(2,1)S(1)}, bf16[128,768]{1,0:T(8,128)(2,1)S(1)}, u32[]{:S(2)}, u32[]{:S(2)}) collective-permute-start(bf16[128,768]{1,0:T(8,128)(2,1)S(1)} %get-tuple-element.42.refs_0_), channel_id=1, source_target_pairs={{0,192},{32,224},{64,0},{96,32},{128,64},{160,96},{192,128},{224,1... | collective-permute-start | bytes 589832 | tf_op jit(solution)/shard_map/ppermute | solution.py:61
  114.7 25.7 %all-to-all-start.3 = ((bf16[4,128,2048]{2,1,0:T(8,128)(2,1)}), bf16[4,128,2048]{2,1,0:T(8,128)(2,1)}, u32[]{:S(2)}, u32[]{:S(2)}) async-start(bf16[4,128,2048]{2,1,0:T(8,128)(2,1)} %bitcast.15), calls=%async_computation.3 | async-start | bytes 4194304 | tf_op jit(solution)/shard_map/all_to_all | solution.py:46
  119.2 12.8 %collective-permute-start.25 = (bf16[128,1536]{1,0:T(8,128)(2,1)S(1)}, bf16[128,1536]{1,0:T(8,128)(2,1)S(1)}, u32[]{:S(2)}, u32[]{:S(2)}) collective-permute-start(bf16[128,1536]{1,0:T(8,128)(2,1)S(1)} %shard_map.95.refs_0_), channel_id=1, source_target_pairs={{0,64},{32,96},{64,128},{96,160},{128,192},{160,224},{192,0},{224,... | collective-permute-start | bytes 1179656 | tf_op jit(solution)/shard_map/ppermute | solution.py:61
  120.2 11.8 %collective-permute-start.24 = (bf16[128,1536]{1,0:T(8,128)(2,1)S(1)}, bf16[128,1536]{1,0:T(8,128)(2,1)S(1)}, u32[]{:S(2)}, u32[]{:S(2)}) collective-permute-start(bf16[128,1536]{1,0:T(8,128)(2,1)S(1)} %shard_map.95.refs_0_), channel_id=1, source_target_pairs={{0,128},{32,160},{64,192},{96,224},{128,0},{160,32},{192,64},{224,... | collective-permute-start | bytes 1179656 | tf_op jit(solution)/shard_map/ppermute | solution.py:61
  121.5 11.7 %collective-permute-start.23 = (bf16[128,1536]{1,0:T(8,128)(2,1)S(1)}, bf16[128,1536]{1,0:T(8,128)(2,1)S(1)}, u32[]{:S(2)}, u32[]{:S(2)}) collective-permute-start(bf16[128,1536]{1,0:T(8,128)(2,1)S(1)} %shard_map.95.refs_0_), channel_id=1, source_target_pairs={{0,192},{32,224},{64,0},{96,32},{128,64},{160,96},{192,128},{224,1... | collective-permute-start | bytes 1179656 | tf_op jit(solution)/shard_map/ppermute | solution.py:61
  122.7 30.9 %collective-permute-start.28 = (bf16[512,1024]{1,0:T(8,128)(2,1)}, bf16[512,1024]{1,0:T(8,128)(2,1)}, u32[]{:S(2)}, u32[]{:S(2)}) collective-permute-start(bf16[512,1024]{1,0:T(8,128)(2,1)} %get-tuple-element.53), channel_id=1, source_target_pairs={{0,32},{32,0},{64,96},{96,64},{128,160},{160,128},{192,224},{224,1... | collective-permute-start | bytes 3145736 | tf_op jit(solution)/shard_map/ppermute | solution.py:41
  140.4 29.4 %all-to-all-start.4 = ((bf16[4,128,2048]{2,1,0:T(8,128)(2,1)}), bf16[4,128,2048]{2,1,0:T(8,128)(2,1)}, u32[]{:S(2)}, u32[]{:S(2)}) async-start(bf16[4,128,2048]{2,1,0:T(8,128)(2,1)} %bitcast.14), calls=%async_computation.4 | async-start | bytes 4194304 | tf_op jit(solution)/shard_map/all_to_all | solution.py:46
  144.9 10.1 %collective-permute-start.27 = (bf16[512,768]{1,0:T(8,128)(2,1)}, bf16[512,768]{1,0:T(8,128)(2,1)S(1)}, u32[]{:S(2)}, u32[]{:S(2)}) collective-permute-start(bf16[512,768]{1,0:T(8,128)(2,1)} %get-tuple-element.52), channel_id=1, source_target_pairs={{0,32},{32,0},{64,96},{96,64},{128,160},{160,128},{192,224},{224,1... | collective-permute-start | bytes 2359304 | tf_op jit(solution)/shard_map/ppermute | solution.py:41
  152.8 9.1 %collective-permute-start.22 = (bf16[512,1024]{1,0:T(8,128)(2,1)}, bf16[512,1024]{1,0:T(8,128)(2,1)S(1)}, u32[]{:S(2)}, u32[]{:S(2)}) collective-permute-start(bf16[512,1024]{1,0:T(8,128)(2,1)} %get-tuple-element.46), channel_id=1, source_target_pairs={{0,32},{32,0},{64,96},{96,64},{128,160},{160,128},{192,224},{224,1... | collective-permute-start | bytes 3145736 | tf_op jit(solution)/shard_map/ppermute | solution.py:41
  152.9 6.5 %collective-permute-start.26 = (bf16[512,768]{1,0:T(8,128)(2,1)}, bf16[512,768]{1,0:T(8,128)(2,1)S(1)}, u32[]{:S(2)}, u32[]{:S(2)}) collective-permute-start(bf16[512,768]{1,0:T(8,128)(2,1)} %get-tuple-element.49), channel_id=1, source_target_pairs={{0,32},{32,0},{64,96},{96,64},{128,160},{160,128},{192,224},{224,1... | collective-permute-start | bytes 2359304 | tf_op jit(solution)/shard_map/ppermute | solution.py:41
  153.3 8.6 %collective-permute-start.29 = (bf16[512,768]{1,0:T(8,128)(2,1)}, bf16[512,768]{1,0:T(8,128)(2,1)S(1)}, u32[]{:S(2)}, u32[]{:S(2)}) collective-permute-start(bf16[512,768]{1,0:T(8,128)(2,1)} %get-tuple-element.54), channel_id=1, source_target_pairs={{0,32},{32,0},{64,96},{96,64},{128,160},{160,128},{192,224},{224,1... | collective-permute-start | bytes 2359304 | tf_op jit(solution)/shard_map/ppermute | solution.py:41
  161.9 1.1 copy-start.1
  169.7 18.9 %collective-permute-start.21 = (bf16[64,2048]{1,0:T(8,128)(2,1)S(1)}, bf16[64,2048]{1,0:T(8,128)(2,1)S(1)}, u32[]{:S(2)}, u32[]{:S(2)}) collective-permute-start(bf16[64,2048]{1,0:T(8,128)(2,1)S(1)} %get-tuple-element.45), channel_id=1, source_target_pairs={{0,16},{1,17},{2,18},{3,19},{4,20},{5,21},{6,22},{7,23},{8,24},{9,... | collective-permute-start | bytes 786440 | tf_op jit(solution)/shard_map/ppermute | solution.py:452
  172.5 33.3 %all-to-all-start.5 = ((bf16[8,16,2048]{2,1,0:T(8,128)(2,1)}), bf16[8,16,2048]{2,1,0:T(8,128)(2,1)S(1)}, u32[]{:S(2)}, u32[]{:S(2)}) async-start(bf16[8,16,2048]{2,1,0:T(8,128)(2,1)} %bitcast.16), calls=%async_computation.5 | async-start | bytes 1048576 | tf_op jit(solution)/shard_map/all_to_all | solution.py:46
  189.2 6.1 %collective-permute-start.30 = (bf16[16,2048]{1,0:T(8,128)(2,1)S(1)}, bf16[16,2048]{1,0:T(8,128)(2,1)S(1)}, u32[]{:S(2)}, u32[]{:S(2)}) collective-permute-start(bf16[16,2048]{1,0:T(8,128)(2,1)S(1)} %get-tuple-element.59), channel_id=1, source_target_pairs={{0,28},{1,29},{2,30},{3,31},{4,0},{5,1},{6,2},{7,3},{8,4},{9,5},{1... | collective-permute-start | bytes 196616 | tf_op jit(solution)/shard_map/ppermute | solution.py:456
  191.9 5.9 %collective-permute-start.31 = (bf16[16,2048]{1,0:T(8,128)(2,1)S(1)}, bf16[16,2048]{1,0:T(8,128)(2,1)S(1)}, u32[]{:S(2)}, u32[]{:S(2)}) collective-permute-start(bf16[16,2048]{1,0:T(8,128)(2,1)S(1)} %get-tuple-element.60), channel_id=1, source_target_pairs={{0,4},{1,5},{2,6},{3,7},{4,8},{5,9},{6,10},{7,11},{8,12},{9,13},{1... | collective-permute-start | bytes 196616 | tf_op jit(solution)/shard_map/ppermute | solution.py:456
  191.9 8.9 %collective-permute-start.32 = (bf16[16,2048]{1,0:T(8,128)(2,1)S(1)}, bf16[16,2048]{1,0:T(8,128)(2,1)S(1)}, u32[]{:S(2)}, u32[]{:S(2)}) collective-permute-start(bf16[16,2048]{1,0:T(8,128)(2,1)S(1)} %get-tuple-element.61), channel_id=1, source_target_pairs={{0,8},{1,9},{2,10},{3,11},{4,12},{5,13},{6,14},{7,15},{8,16},{9,17... | collective-permute-start | bytes 196616 | tf_op jit(solution)/shard_map/ppermute | solution.py:456
  200.8 4.3 %collective-permute-start.33 = (bf16[16,1024]{1,0:T(8,128)(2,1)S(1)}, bf16[16,1024]{1,0:T(8,128)(2,1)S(1)}, u32[]{:S(2)}, u32[]{:S(2)}) collective-permute-start(bf16[16,1024]{1,0:T(8,128)(2,1)S(1)} %slice.27), channel_id=1, source_target_pairs={{0,32},{32,0},{64,96},{96,64},{128,160},{160,128},{192,224},{224,1... | collective-permute-start | bytes 98312 | tf_op jit(solution)/shard_map/ppermute | solution.py:41
  205.8 1.3 collective-permute-start.34
